TPU v7x, 256 devices: a whole 4x4x8 slice. The times are simulated.
256 devices in a mesh: seq: 8 (over x, y_lo), tp: 16 (over z, core), section: 2 (over y_hi).
Axes of the slice: x: 4, y: 4 (y_hi: 2, y_lo: 2; y = y_hi * 2 + y_lo), z: 8, core: 2. Of those that a mesh axis runs over, the one named last changes fastest.
Arguments:
- text_states: bfloat16 [4096, 8192], P(('seq', 'section'), 'tp')
- norm_gain: bfloat16 [8192], P('tp'), may hold values from 0.099609375 to 1.8984375
- w_query: bfloat16 [8192, 4096], P(None, 'tp'), may hold values from -0.0625 to 0.0625
- w_keyval: bfloat16 [8192, 1024], P('tp'), may hold values from -0.0625 to 0.0625
- w_output: bfloat16 [4096, 8192], P('tp'), may hold values from -0.125 to 0.125
- query_gain: float32 [128], replicated, may hold values from 1 to 2
- key_gain: float32 [128], replicated, may hold values from 1 to 2
- attn_gate: float32 [1], replicated, may hold values from 0.5 to 1.5
- image_states: bfloat16 [16, 1601, 8192], P(('seq', 'section'), None, 'tp'), may hold values from -6 to 6
- seg_ids: int32 [4096], P(('seq', 'section')), may hold values from 0 to 7, as said below
- image_owner: int32 [16], P(('seq', 'section')), may hold values from 0 to 7, as said below
- image_pos: int32 [16], P(('seq', 'section')), may hold values from 0 to 4095, as said below
Outputs:
- update: bfloat16 [4096, 8192], P(('seq', 'section'), 'tp')
Inputs may be any that keep to these rules, and one draw needn't show every extreme that they name: `seg_ids`: non-decreasing along the text; each of the 8 documents holds at least one token. `image_owner`: equal to seg_ids at the image's position image_pos. `image_pos`: some image stands at position 0 and some at the last position.
All inputs are finite; a program needn't handle non-finite values.
Results may differ from a plain program's by a relative error of at most 0.012.
Values may be sent and summed in bfloat16 or wider, within the bound.
A program may use at most 192 MiB of HBM per device.

v0:
```python
import jax
import jax.numpy as jnp
from jax import lax
from jax.sharding import PartitionSpec as P

HEADS = 32
KV_HEADS = 4
HD = 128
IMG_TOK = 1601


epsilon = 1e-05


def rms_norm(vector, gain_vec):
    return (
        vector * lax.rsqrt(jnp.mean(vector * vector, axis=-1, keepdims=True) + epsilon) * gain_vec
    )


def attend(query_rows, doc_rows, place_rows, keyval, owners, image_starts):
    visible = (doc_rows[:, None] == owners[None, :]) & (
        place_rows[:, None] >= image_starts[None, :]
    )
    key_part = keyval[:, :, :HD]
    value_part = keyval[:, :, HD:]
    scores = jnp.einsum(
        "rhd,mkd->rhmk", query_rows, key_part, preferred_element_type=jnp.float32
    ) * HD ** (-0.5)
    weights_exp = jnp.where(visible[:, None, :, None], jnp.exp(scores), 0.0)
    weight_sum = jnp.sum(weights_exp, axis=(2, 3))
    acc_sum = jnp.einsum(
        "rhmk,mkd->rhd",
        weights_exp.astype(jnp.bfloat16),
        value_part,
        preferred_element_type=jnp.float32,
    )
    return (acc_sum, weight_sum)


def on_device(
    text_states,
    norm_gain,
    w_query,
    w_keyval,
    w_output,
    query_gain,
    key_gain,
    attn_gate,
    image_states,
    seg_ids,
    image_owner,
    image_pos,
):
    tok_rows = text_states.shape[0]
    normed = (text_states.astype(jnp.float32) * norm_gain.astype(jnp.float32)[None, :]).astype(
        jnp.bfloat16
    )
    query_sum = jnp.dot(
        lax.all_gather(normed, "tp", axis=1, tiled=True),
        w_query,
        preferred_element_type=jnp.float32,
    )
    head_count = w_query.shape[1] // HD
    query_heads = rms_norm(query_sum.reshape(tok_rows, head_count, HD), query_gain).astype(
        jnp.bfloat16
    )
    group = HEADS // KV_HEADS
    kv_head = lax.axis_index("tp") * head_count // group
    img_count = image_states.shape[0]
    flat_images = image_states.reshape(img_count * IMG_TOK, image_states.shape[2])
    partial_kv = jnp.dot(flat_images, w_keyval, preferred_element_type=jnp.float32)
    summed_kv = lax.psum(partial_kv, "tp")
    own_kv = lax.dynamic_slice_in_dim(summed_kv, kv_head * 2 * HD, 2 * HD, 1)
    key_part = rms_norm(own_kv[:, :HD], key_gain).astype(jnp.bfloat16)
    value_part = own_kv[:, HD:].astype(jnp.bfloat16)
    keyval = jnp.concatenate([key_part, value_part], axis=1).reshape(img_count, IMG_TOK, 2 * HD)
    places = lax.axis_index(("seq", "section")) * tok_rows + jnp.arange(tok_rows, dtype=jnp.int32)
    piece_kv = lax.all_gather(keyval, ("seq", "section"), axis=0, tiled=True)
    piece_owner = lax.all_gather(image_owner, ("seq", "section"), axis=0, tiled=True)
    piece_start = lax.all_gather(image_pos, ("seq", "section"), axis=0, tiled=True)
    acc_sum, weight_sum = attend(query_heads, seg_ids, places, piece_kv, piece_owner, piece_start)
    attended = (acc_sum / jnp.maximum(weight_sum, 1.0)[..., None]).astype(jnp.bfloat16)
    attended = attended.reshape(tok_rows, head_count * HD)
    partial_out = jnp.dot(attended, w_output, preferred_element_type=jnp.float32)
    branch = lax.psum_scatter(partial_out, "tp", scatter_dimension=1, tiled=True)
    return (jnp.tanh(attn_gate[0]) * branch).astype(jnp.bfloat16)


def solution(mesh):
    return jax.shard_map(
        on_device,
        mesh=mesh,
        in_specs=(
            P(("seq", "section"), "tp"),
            P("tp"),
            P(None, "tp"),
            P("tp", None),
            P("tp", None),
            P(),
            P(),
            P(),
            P(("seq", "section"), None, "tp"),
            P(("seq", "section")),
            P(("seq", "section")),
            P(("seq", "section")),
        ),
        out_specs=P(("seq", "section"), "tp"),
        check_vma=False,
    )
```

profile of v0, /device:TPU:1, one launch (start us, length us, event | category | flops | bytes accessed | tf_op | source)
XLA Modules:
  0.0 604.3 jit_solution(10483128115354311412)
XLA Ops:
  6.5 0.0 copy-start
  6.5 0.0 copy-start.3
  6.5 0.0 copy-start.2
  6.5 0.0 all-reduce.5.cloned.1.call-start
  6.5 1.4 copy-done
  8.0 5.8 fusion.6
  13.8 0.0 copy-start.5
  13.8 0.0 copy-start.7
  13.8 0.0 copy-start.4
  13.8 0.0 all-reduce.5.cloned.1.call-update
  13.8 0.0 all-gather.5.cloned.1.call-start
  13.9 0.0 copy-done.3
  13.9 0.0 copy-done.2
  13.9 0.8 multiply_convert_fusion.2
  14.7 0.0 all-gather.5.cloned.1.call-update
  14.7 0.0 all-gather.7.cloned.1.call-start
  14.8 131.6 %all-reduce.5.cloned.1.call-done = f32[1601,1024]{1,0:T(8,128)} async-done(((f32[1601,1024]{1,0:T(8,128)}), f32[1601,1024]{1,0:T(8,128)}) %all-reduce.5.cloned.1.call-update) | async-done | bytes 6557712 | tf_op jit(solution)/shard_map/psum | solution.py:73
  146.4 1.5 multiply_reduce_fusion
  147.9 1.2 dynamic-slice_convert_fusion
  149.1 0.0 copy-done.5
  149.1 0.0 copy-start.6
  149.1 1.4 multiply_convert_fusion
  150.5 1.0 maximum_bitcast_fusion
  151.5 0.0 all-gather.7.cloned.1.call-update
  151.5 0.0 reduce-scatter.2.cloned.1.call-start
  152.9 0.0 copy-done.7
  152.9 0.6 dynamic-slice
  153.5 0.8 dynamic-update-slice
  154.3 0.8 dynamic-update-slice.1
  155.1 12.9 %all-reduce.2 = (s32[16]{0:T(128)S(1)}, s32[16]{0:T(128)S(1)}) all-reduce(s32[16]{0:T(128)S(1)} %dynamic-update-slice.1, s32[16]{0:T(128)S(1)} %dynamic-update-slice), channel_id=1, replica_groups=mesh['seq'=8,'tp'=16,'section'=2] {'seq','section'}, use_global_device_ids=true, to_apply=%add.1 | all-reduce | flops 32 | bytes 256
  168.0 0.0 copy-done.4
  168.0 0.1 compare_and_fusion
  168.1 23.5 %all-gather.5.cloned.1.call-done = bf16[256,8192]{1,0:T(8,128)(2,1)} async-done(((bf16[256,512]{1,0:T(8,128)(2,1)}), bf16[256,8192]{1,0:T(8,128)(2,1)}) %all-gather.5.cloned.1.call-update) | async-done | bytes 4194320 | tf_op jit(solution)/shard_map/all_gather | solution.py:60
  191.6 5.2 multiply_reduce_fusion.1
  196.8 0.1 copy.14
  196.9 274.8 %all-gather.7.cloned.1.call-done = bf16[16,1601,256]{2,1,0:T(8,128)(2,1)} async-done(((bf16[1,1601,256]{2,1,0:T(8,128)(2,1)}), bf16[16,1601,256]{2,1,0:T(8,128)(2,1)}) %all-gather.7.cloned.1.call-update) | async-done | bytes 13115408 | tf_op jit(solution)/shard_map/all_gather | solution.py:79
  471.8 0.0 copy-done.6
  471.8 29.3 %fusion = (f32[256,2]{0,1:T(2,128)S(1)}, f32[256,2,16,1601]{0,3,2,1:T(8,128)}) fusion(pred[256,16]{0,1:T(8,128)(4,1)S(1)} %compare_and_fusion, bf16[16,1601,256]{2,1,0:T(8,128)(2,1)} %all-gather.7.cloned.1.call-done, f32[256,2,128]{2,0,1:T(8,128)S(1)} %copy.14, f32[128]{0:T(128)S(1)} %copy-done.6, f32[256,2]{0,1:T(2,128)S(1)} %add_rsqrt_fusion.1), kind=kOutput, calls=%fused_computation.1 | convolution fusion | flops 3397082624 | bytes 59318784 | tf_op jit(solution)/shard_map/rhd,mkd->rhmk/dot_general | solution.py:27
  501.1 21.0 %fusion.14 = bf16[256,2,128]{0,2,1:T(8,128)(2,1)S(1)} fusion(bf16[16,1601,256]{2,1,0:T(8,128)(2,1)} %all-gather.7.cloned.1.call-done, f32[256,2,16,1601]{0,3,2,1:T(8,128)} %get-tuple-element.10, pred[256,16]{0,1:T(8,128)(4,1)S(1)} %compare_and_fusion, f32[256,2]{0,1:T(2,128)S(1)} %broadcast_maximum_fusion), kind=kOutput, calls=%fused_computation.12 | convolution fusion | flops 3397017600 | bytes 59414528 | tf_op jit(solution)/shard_map/rhmk,mkd->rhd/dot_general | solution.py:32
  522.1 0.0 copy-start.1
  522.1 6.8 %fusion.23 = f32[256,8192]{1,0:T(8,128)} fusion(bf16[256,256]{0,1:T(8,128)(2,1)S(1)} %bitcast.44, bf16[256,8192]{1,0:T(8,128)(2,1)} %param.16), kind=kOutput, calls=%fused_computation.31 | convolution fusion | flops 1073741824 | bytes 12713984 | tf_op jit(solution)/shard_map/dot_general | solution.py:85
  528.9 0.0 reduce-scatter.2.cloned.1.call-update
  529.6 66.4 %reduce-scatter.2.cloned.1.call-done = f32[256,512]{1,0:T(8,128)} async-done(((f32[256,8192]{1,0:T(8,128)}), f32[256,512]{1,0:T(8,128)}) %reduce-scatter.2.cloned.1.call-update) | async-done | bytes 524304 | tf_op jit(solution)/shard_map/reduce_scatter | solution.py:86
  596.0 1.8 multiply_convert_fusion.1
  597.8 0.0 copy-done.1
  (7 shorter events, 0.0 us)
Async XLA Ops:
  6.5 1.4 copy-start
  6.5 7.3 %copy-start.3 = (bf16[512]{0:T(512)(128)(2,1)S(1)}, bf16[512]{0:T(512)(128)(2,1)}, u32[]{:S(2)}) copy-start(bf16[512]{0:T(512)(128)(2,1)} %param.13) | copy-start | bytes 3076
  6.5 7.4 %copy-start.2 = (bf16[256,512]{1,0:T(8,128)(2,1)S(1)}, bf16[256,512]{1,0:T(8,128)(2,1)}, u32[]{:S(2)}) copy-start(bf16[256,512]{1,0:T(8,128)(2,1)} %param.12) | copy-start | bytes 786436
  6.5 139.8 %all-reduce.5.cloned.1.call-start = ((), (), s32[]{:S(2)}) async-start(), calls=%async_computation.2 | async-start | bytes 13172736 | tf_op jit(solution)/shard_map/psum | solution.py:73
  13.8 135.3 %copy-start.5 = (f32[128]{0:T(128)S(1)}, f32[128]{0:T(128)}, u32[]{:S(2)}) copy-start(f32[128]{0:T(128)} %param.18) | copy-start | bytes 1540
  13.8 139.1 %copy-start.7 = (u32[256]{0:T(256)S(1)}, u32[256]{0:T(256)}, u32[]{:S(2)}) copy-start(u32[256]{0:T(256)} %constant.58) | copy-start | bytes 3076
  13.8 154.2 %copy-start.4 = (s32[256]{0:T(256)S(1)}, s32[256]{0:T(256)}, u32[]{:S(2)}) copy-start(s32[256]{0:T(256)} %param.21) | copy-start | bytes 3076
  13.8 177.7 %all-gather.5.cloned.1.call-start = ((), (), s32[]{:S(2)}) async-start(), calls=%async_computation.1 | async-start | bytes 4456448 | tf_op jit(solution)/shard_map/all_gather | solution.py:60
  14.7 457.1 %all-gather.7.cloned.1.call-start = ((), (), s32[]{:S(2)}) async-start(), calls=%async_computation.4 | async-start | bytes 13996032 | tf_op jit(solution)/shard_map/all_gather | solution.py:79
  149.1 322.7 %copy-start.6 = (f32[128]{0:T(128)S(1)}, f32[128]{0:T(128)}, u32[]{:S(2)}) copy-start(f32[128]{0:T(128)} %param.17) | copy-start | bytes 1540
  151.5 444.5 %reduce-scatter.2.cloned.1.call-start = ((), (), s32[]{:S(2)}) async-start(), calls=%async_computation.3 | async-start | bytes 8912896 | tf_op jit(solution)/shard_map/reduce_scatter | solution.py:86
  522.1 75.7 %copy-start.1 = (bf16[1,1601,512]{2,1,0:T(8,128)(2,1)S(1)}, bf16[1,1601,512]{2,1,0:T(8,128)(2,1)}, u32[]{:S(2)}) copy-start(bf16[1,1601,512]{2,1,0:T(8,128)(2,1)} %param.20) | copy-start | bytes 4918276
Sparse Core Ops, SparseCore 0:
  14.0 132.3 all-reduce.4
  148.2 43.2 all-gather.4
  193.4 278.3 all-gather.6
  529.0 66.9 reduce-scatter.1
where the time goes:
time: 607 us; the launch traced here: 604 us
  waiting for transfers between devices  496 us (82%)
  matrix products  68.2 us (11%)
  between operations  15.2 us (3%)
  blocking collectives  12.9 us (2%)
  other arithmetic  6.52 us (1%)
    all_gather x1, waiting for transfers between devices, on_device(): piece_kv = lax.all_gather(keyval, ('seq', 'section'), axis=0, tiled=True)  275 us
    psum x1, waiting for transfers between devices, on_device(): summed_kv = lax.psum(partial_kv, 'tp')  132 us
    reduce_scatter x1, waiting for transfers between devices, on_device(): lax.psum_scatter(partial_out, 'tp', scatter_dimension=1, tiled=True)  66.4 us
    dot_general x1, matrix products, attend(): jnp.einsum('rhd,mkd->rhmk', query_rows, key_part, preferred_element_type=...  29.3 us
    all_gather x1, waiting for transfers between devices, on_device(): lax.all_gather(normed, 'tp', axis=1, tiled=True)  23.5 us
    dot_general x1, matrix products, attend(): jnp.einsum('rhmk,mkd->rhd', weights_exp.astype(jnp.bfloat16), value_part,...  21 us
    unnamed x1, blocking collectives  12.9 us
  transfers between devices with their start and end apart: 4, of which 4 were waited for; matrix products, arithmetic and copies ran while one was open for 2% of the time, Pallas kernels for 0%

commit v1 on v0

v1 whole, which is shorter than its diff:
```python
import functools

import jax
import jax.numpy as jnp
from jax import lax
from jax.experimental import pallas as pl
from jax.experimental.pallas import tpu as pltpu
from jax.sharding import PartitionSpec as P

MESH = pl.DeviceIdType.MESH
F32, BF16 = jnp.float32, jnp.bfloat16
HD = 128
IMG_TOK = 1601
IMAGES = 16
TOK = 256
QUARTER = 416
HALF = 2 * QUARTER
ROWS = 4 * QUARTER
EPS = 1e-05
META = 2.0**-20
META_ROW = ROWS - 16

SUBS = ((0, 112, 96), (208, 96, 112))
LAG = 5


def remote(src, dst, send, recv, device):
    return pltpu.make_async_remote_copy(
        src_ref=src, dst_ref=dst, send_sem=send, recv_sem=recv, device_id=device, device_id_type=MESH
    )


class Place:
    def __init__(self):
        seq, tp, sec = lax.axis_index("seq"), lax.axis_index("tp"), lax.axis_index("section")
        self.tp, self.z, self.c = tp, tp // 2, tp % 2
        self.x, self.y = seq // 2, sec * 2 + seq % 2
        self.partner = {"tp": self.z * 2 + 1 - self.c}
        self.up = {"tp": ((self.z + 1) % 8) * 2 + self.c}
        self.down = {"tp": ((self.z + 7) % 8) * 2 + self.c}

    def step(self, axis, delta):
        if axis == "x":
            return {"seq": ((self.x + delta) % 4) * 2 + self.y % 2}
        y = (self.y + delta) % 4
        return {"seq": self.x * 2 + y % 2, "section": y // 2}

    def image(self, dx, dy):
        y = (self.y + dy) % 4
        return ((self.x + dx) % 4) * 4 + (y % 2) * 2 + y // 2


def greet(devices):
    barrier = pltpu.get_barrier_semaphore()
    for device in devices:
        pl.semaphore_signal(barrier, inc=1, device_id=device, device_id_type=MESH)
    pl.semaphore_wait(barrier, len(devices))


def front_kernel(
    text, gain, wq, wkv, wout, qgain, kgain, owner, pos, img,
    q_out, kv, pwout,
    nall, wqv, qacc, imgv, pimg, wkvv, pwkv, acck, accv, rk, rv, vfirst, mine,
    load_sem, ex_send, ex_recv, bs, br, xs, xr, ps, pr, cs, cr, as_, ar, acs, acr, ws, wr,
):
    me = Place()
    z, c = me.z, me.c
    zpar = z % 2
    greet([me.partner, me.up, me.down] + [me.step(a, d) for a in "xy" for d in (1, 3)])
    sends = []

    def send(src, dst, ssem, rsem, device):
        copy = remote(src, dst, ssem, rsem, device)
        copy.start()
        sends.append(copy)

    def arrived(ref, ssem, rsem):
        remote(ref, ref, ssem, rsem, me.partner).wait_recv()

    send(img.at[pl.ds((1 - c) * HALF, HALF)], pimg, ex_send.at[0], ex_recv.at[0], me.partner)
    send(wkv, pwkv, ex_send.at[1], ex_recv.at[1], me.partner)
    loads = [
        pltpu.make_async_copy(img.at[pl.ds(c * HALF, HALF)], imgv, load_sem.at[0]),
        pltpu.make_async_copy(wkv, wkvv, load_sem.at[1]),
        pltpu.make_async_copy(wq, wqv, load_sem.at[2]),
    ]
    for load in loads:
        load.start()

    shard = lambda k: ((z + k % 8) % 8) * 2 + c
    nall[me.tp] = (text[...].astype(F32) * gain[...].astype(F32)).astype(BF16)
    qacc[...] = jnp.zeros_like(qacc)

    def text_send(k, way, hop):
        ref = nall.at[shard(k)]
        if hop == 4:
            ref = ref.at[pl.ds(way * 128, 128)]
        send(ref, ref, as_.at[way, hop - 1], ar.at[way, hop - 1], (me.up, me.down)[way])

    def text_share(k):
        ref = nall.at[shard(k)]
        send(ref, ref, acs.at[k % 8], acr.at[k % 8], me.partner)

    def text_use(index):
        w = wqv[pl.ds(pl.multiple_of(index * 512, 512), 512), :]
        qacc[...] += jnp.dot(nall[index], w, preferred_element_type=F32)

    def text_arrived(hop, way):
        k = -hop if way == 0 else hop
        ref = nall.at[shard(k)]
        if hop == 4:
            ref = ref.at[pl.ds(way * 128, 128)]
        arrived(ref, as_.at[way, hop - 1], ar.at[way, hop - 1])

    def text_round(hop):
        for way in (0, 1):
            text_arrived(hop, way)
            if hop < 4:
                k = -hop if way == 0 else hop
                text_send(k, way, hop + 1)
                text_share(k)
        if hop == 4:
            text_share(4)

    def text_compute(hop):
        for k in {0: (0,), 4: (4,)}.get(hop, (hop, -hop)):
            text_use(shard(k))

    def text_compute_shared(hop):
        for k in {0: (0,), 4: (4,)}.get(hop, (hop, -hop)):
            index = ((z + k % 8) % 8) * 2 + 1 - c
            arrived(nall.at[index], acs.at[k % 8], acr.at[k % 8])
            text_use(index)

    text_send(0, 0, 1)
    text_send(0, 1, 1)
    text_share(0)

    loads[0].wait()
    loads[1].wait()
    arrived(pimg, ex_send.at[0], ex_recv.at[0])
    arrived(pwkv, ex_send.at[1], ex_recv.at[1])

    def project(k):
        d = (z + k) % 8
        rows = pl.ds(pl.multiple_of((d % 2) * QUARTER, QUARTER), QUARTER)
        cols = pl.ds(pl.multiple_of((d // 2) * 256, 256), 256)
        part = jnp.dot(imgv[rows, :], wkvv[:, cols], preferred_element_type=F32)
        part += jnp.dot(pimg[rows, :], pwkv[:, cols], preferred_element_type=F32)
        acck[d] = part[:, :HD]
        accv[d] = part[:, HD:]

    def ring_rows(u, way):
        start, first, second = SUBS[u]
        return (start, first) if way == 0 else (start + first, second)

    def ring_send(u, step):
        for way in (0, 1):
            r0, n = ring_rows(u, way)
            device = (me.up, me.down)[way]
            rows = pl.ds(r0, n)
            if step == 0:
                d = (z + (7, 1)[way]) % 8
                vfirst[rows, :] = accv[d, rows, :].astype(BF16)
                srck, srcv = acck.at[d, rows], vfirst.at[rows]
            else:
                srck, srcv = rk.at[step - 1, rows], rv.at[step - 1, rows]
            send(srck, rk.at[step, rows], bs.at[u, way, step, 0], br.at[u, way, step, 0], device)
            send(srcv, rv.at[step, rows], bs.at[u, way, step, 1], br.at[u, way, step, 1], device)

    def ring_receive(u, step):
        for way in (0, 1):
            r0, n = ring_rows(u, way)
            rows = pl.ds(r0, n)
            arrived(rk.at[step, rows], bs.at[u, way, step, 0], br.at[u, way, step, 0])
            arrived(rv.at[step, rows], bs.at[u, way, step, 1], br.at[u, way, step, 1])
            if step < 6:
                d = (z + (6 - step if way == 0 else 2 + step)) % 8
                rk[step, rows, :] += acck[d, rows, :]
                rv[step, rows, :] = (rv[step, rows, :].astype(F32) + accv[d, rows, :]).astype(BF16)

    def finish(u):
        start, first, second = SUBS[u]
        n = first + second
        rows = pl.ds(start, n)
        key = rk[6, rows, :] + acck[z, rows, :]
        val = rv[6, rows, :].astype(F32) + accv[z, rows, :]
        key = key * lax.rsqrt(jnp.mean(key * key, axis=-1, keepdims=True) + EPS) * kgain[...]
        if u == len(SUBS) - 1:
            row = c * HALF + zpar * QUARTER + start + lax.broadcasted_iota(jnp.int32, (n, HD), 0)
            lane = lax.broadcasted_iota(jnp.int32, (n, HD), 1)
            said = jnp.where(lane == 0, owner[0], jnp.where(lane == 1, pos[0] // 64, pos[0] % 64))
            said = jnp.where(lane < 3, said, 0).astype(F32) * META
            key = jnp.where(row >= META_ROW, said, key)
        at = pl.ds(pl.multiple_of(zpar * QUARTER + start, 16), n)
        mine[at, 0:HD] = key.astype(BF16)
        mine[at, HD:] = val.astype(BF16)
        pair = {"tp": (z + 1 - 2 * zpar) * 2 + c}
        send(mine.at[at], mine.at[at], xs.at[u], xr.at[u], pair)

    here = me.image(0, 0)

    def block(u, par, i, j, part=None):
        start, first, second = SUBS[u]
        n = first + second
        if part == 0:
            n = first
        if part == 1:
            start, n = start + first, second
        m = me.image(i, j) if par == 0 else me.image(j, i)
        r0 = pl.multiple_of(c * HALF + par * QUARTER + start, 16)
        return kv.at[m, pl.ds(r0, n)]

    def own(u, par):
        start, first, second = SUBS[u]
        return mine.at[pl.ds(par * QUARTER + start, first + second)]

    axes = lambda par: ("x", "y") if par == 0 else ("y", "x")

    def spread_first(u, par, i, way, part=None):
        slot = {(0, 0): 0, (0, 1): 1, (3, 0): 2, (1, 1): 3}[(i, way)]
        src = own(u, par) if i == 0 else block(u, par, i, 0, part)
        dst = block(u, par, i, 0, part)
        send(src, dst, ps.at[u, par, slot], pr.at[u, par, slot], me.step(axes(par)[0], (1, 3)[way]))

    def first_arrived(u, par, i, part=None):
        slot = {(3, None): 0, (1, None): 1, (2, 1): 2, (2, 0): 3}[(i, part)]
        arrived(block(u, par, i, 0, part), ps.at[u, par, slot], pr.at[u, par, slot])

    def spread_second(u, par, i, j, way):
        slot = 4 + 3 * i + (way if j == 0 else 2)
        src = own(u, par) if (i, j) == (0, 0) else block(u, par, i, j)
        send(src, block(u, par, i, j), ps.at[u, par, slot], pr.at[u, par, slot], me.step(axes(par)[1], (1, 3)[way]))

    def second_arrived(u, par, i, j):
        slot = 4 + 3 * i + {3: 0, 1: 1, 2: 2}[j]
        arrived(block(u, par, i, j), ps.at[u, par, slot], pr.at[u, par, slot])

    def share(u, par, i, j):
        src = own(u, par) if (i, j) == (0, 0) else block(u, par, i, j)
        send(src, block(u, par, i, j), cs.at[u, par, 4 * i + j], cr.at[u, par, 4 * i + j], me.partner)

    def column(u, par, i):
        spread_second(u, par, i, 0, 0)
        spread_second(u, par, i, 0, 1)
        share(u, par, i, 0)

    def column_arrived(u, par, i):
        for j, way in ((3, 0), (1, 1)):
            second_arrived(u, par, i, j)
            if (j == 3) == (i < 2):
                spread_second(u, par, i, j, way)
            share(u, par, i, j)

    local = []

    def plane_round(u, r):
        if r == 0:
            start, first, second = SUBS[u]
            at = pl.ds(pl.multiple_of((1 - zpar) * QUARTER + start, 16), first + second)
            arrived(mine.at[at], xs.at[u], xr.at[u])
        for par in (0, 1):
            if r == 0:
                spread_first(u, par, 0, 0)
                spread_first(u, par, 0, 1)
                column(u, par, 0)
                keep = pltpu.make_async_copy(own(u, par), block(u, par, 0, 0), load_sem.at[3 + 2 * u + par])
                keep.start()
                local.append(keep)
            if r == 1:
                first_arrived(u, par, 3)
                spread_first(u, par, 3, 0, 1)
                column(u, par, 3)
                first_arrived(u, par, 1)
                spread_first(u, par, 1, 1, 0)
                column(u, par, 1)
            if r == 2:
                column_arrived(u, par, 0)
            if r == 3:
                first_arrived(u, par, 2, 0)
                first_arrived(u, par, 2, 1)
                column(u, par, 2)
            if r == 4:
                column_arrived(u, par, 3)
                column_arrived(u, par, 1)
            if r == 5:
                column_arrived(u, par, 2)
            if r == 6:
                for i in (0, 3, 1, 2):
                    second_arrived(u, par, i, 2)
                    share(u, par, i, 2)

    def ring_step(u, step):
        ring_receive(u, step)
        if step < 6:
            ring_send(u, step + 1)
        else:
            finish(u)

    project(7)
    project(1)
    ring_send(0, 0)
    for k in (6, 2, 5, 3, 4, 0):
        project(k)
    for k in range(8):
        src = wout.at[:, pl.ds(pl.multiple_of((2 * k + 1 - c) * 512, 512), 512)]
        send(src, pwout.at[k], ws.at[k], wr.at[k], me.partner)
    loads[2].wait()
    text_compute(0)

    for step in range(LAG):
        ring_step(0, step)
    ring_send(1, 0)
    for step in range(LAG, 7):
        ring_step(0, step)
        ring_step(1, step - LAG)
    done = 7 - LAG
    plane_round(0, 0)
    ring_step(1, done)
    plane_round(0, 1)
    ring_step(1, done + 1)
    plane_round(0, 2)
    ring_step(1, done + 2)
    plane_round(0, 3)
    for step in range(done + 3, 7):
        ring_step(1, step)
    text_round(1)
    plane_round(1, 0)
    plane_round(0, 4)
    text_compute(1)
    plane_round(0, 5)
    plane_round(1, 1)
    text_round(2)
    plane_round(0, 6)
    text_compute(2)
    text_compute_shared(0)
    plane_round(1, 2)
    plane_round(1, 3)
    text_round(3)
    text_compute(3)
    text_compute_shared(1)
    plane_round(1, 4)
    text_compute_shared(2)
    text_round(4)
    plane_round(1, 5)
    text_compute(4)
    text_compute_shared(3)
    text_compute_shared(4)

    for h in range(2):
        q = qacc[:, h * HD : (h + 1) * HD]
        q = q * lax.rsqrt(jnp.mean(q * q, axis=-1, keepdims=True) + EPS) * qgain[...]
        q_out[:, h * HD : (h + 1) * HD] = q.astype(BF16)

    plane_round(1, 6)
    for u, (start, first, second) in enumerate(SUBS):
        for par in (0, 1):
            for i in range(4):
                for j in range(4):
                    m = me.image(i, j) if par == 0 else me.image(j, i)
                    r0 = pl.multiple_of((1 - c) * HALF + par * QUARTER + start, 16)
                    ref = kv.at[m, pl.ds(r0, first + second)]
                    arrived(ref, cs.at[u, par, 4 * i + j], cr.at[u, par, 4 * i + j])
    for k in range(8):
        arrived(pwout.at[k], ws.at[k], wr.at[k])
    for keep in local:
        keep.wait()
    for copy in sends:
        copy.wait_send()


def front(text, gain, wq, wkv, wout, qgain, kgain, owner, pos, img):
    vmem, anyspace, smem = (pl.BlockSpec(memory_space=m) for m in (pltpu.VMEM, pl.ANY, pltpu.SMEM))
    dma = pltpu.SemaphoreType.DMA
    n = len(SUBS)
    return pl.pallas_call(
        front_kernel,
        out_shape=(
            jax.ShapeDtypeStruct((TOK, 256), BF16),
            jax.ShapeDtypeStruct((IMAGES, ROWS, 256), BF16),
            jax.ShapeDtypeStruct((8, 256, 512), BF16),
        ),
        in_specs=[vmem, vmem, anyspace, anyspace, anyspace, vmem, vmem, smem, smem, anyspace],
        out_specs=(vmem, anyspace, anyspace),
        scratch_shapes=[
            pltpu.VMEM((16, TOK, 512), BF16),
            pltpu.VMEM((8192, 256), BF16),
            pltpu.VMEM((TOK, 256), F32),
            pltpu.VMEM((HALF, 512), BF16),
            pltpu.VMEM((HALF, 512), BF16),
            pltpu.VMEM((512, 1024), BF16),
            pltpu.VMEM((512, 1024), BF16),
            pltpu.VMEM((8, QUARTER, HD), F32),
            pltpu.VMEM((8, QUARTER, HD), F32),
            pltpu.VMEM((7, QUARTER, HD), F32),
            pltpu.VMEM((7, QUARTER, HD), BF16),
            pltpu.VMEM((QUARTER, HD), BF16),
            pltpu.VMEM((HALF, 256), BF16),
            dma((3 + 2 * n,)),
            dma((2,)),
            dma((2,)),
            dma((n, 2, 7, 2)),
            dma((n, 2, 7, 2)),
            dma((n,)),
            dma((n,)),
            dma((n, 2, 16)),
            dma((n, 2, 16)),
            dma((n, 2, 16)),
            dma((n, 2, 16)),
            dma((2, 4)),
            dma((2, 4)),
            dma((8,)),
            dma((8,)),
            dma((8,)),
            dma((8,)),
        ],
        compiler_params=pltpu.CompilerParams(
            collective_id=0, has_side_effects=True, vmem_limit_bytes=56 * 2**20
        ),
        cost_estimate=pl.CostEstimate(flops=5 * 10**9, bytes_accessed=3 * 10**7, transcendentals=0),
    )(text, gain, wq, wkv, wout, qgain, kgain, owner, pos, img)


TILES = ((0, 256), (256, 256), (512, 256), (768, 256), (1024, 256), (1280, 256), (1536, 128))


def attend_kernel(q, seg, kv, out, meta, kbuf, vbuf, wexp, total, seen, sem, meta_sem):
    first = (lax.axis_index("seq") * 2 + lax.axis_index("section")) * TOK
    fetch = pltpu.make_async_copy(kv.at[:, pl.ds(META_ROW, 16), pl.ds(0, HD)], meta, meta_sem)
    fetch.start()
    total[...] = jnp.zeros_like(total)
    row = lax.broadcasted_iota(jnp.int32, (ROWS, HD), 0)
    ones = jnp.where(row < IMG_TOK, 1.0, 0.0).astype(BF16)
    vbuf[0, :, HD:] = ones
    vbuf[1, :, HD:] = ones
    fetch.wait()
    places = (first + lax.broadcasted_iota(jnp.int32, (TOK, 1), 0)).astype(F32)
    docs = seg[...].astype(F32)

    def sees(m):
        said = meta[m, 0:1, :].astype(F32) * (1.0 / META)
        lane = lax.broadcasted_iota(jnp.int32, (1, HD), 1)
        doc = jnp.sum(jnp.where(lane == 0, said, 0.0), axis=1, keepdims=True)
        weight = jnp.where(lane == 1, 64.0, jnp.where(lane == 2, 1.0, 0.0))
        start = jnp.sum(said * weight, axis=1, keepdims=True)
        return (docs == doc) & (places >= start)

    def look(m, count):
        flag = jnp.max(jnp.where(sees(m), 1.0, 0.0)) > 0.5

        @pl.when(flag)
        def _():
            seen[count] = m

        return count + flag.astype(jnp.int32)

    count = lax.fori_loop(0, IMAGES, look, jnp.int32(0))

    def copies(n):
        slot = n % 2
        m = seen[n]
        return (
            pltpu.make_async_copy(kv.at[m, :, pl.ds(0, HD)], kbuf.at[slot], sem.at[slot, 0]),
            pltpu.make_async_copy(kv.at[m, :, pl.ds(HD, HD)], vbuf.at[slot, :, pl.ds(0, HD)], sem.at[slot, 1]),
        )

    @pl.when(count > 0)
    def _():
        for copy in copies(0):
            copy.start()

    rows = jnp.concatenate([q[:, :HD], q[:, HD:]], axis=0)

    def image(n, carry):
        slot = n % 2

        @pl.when(n + 1 < count)
        def _():
            for copy in copies(n + 1):
                copy.start()

        for copy in copies(n):
            copy.wait()
        for k0, width in TILES:
            score = lax.dot_general(
                rows, kbuf[slot, k0 : k0 + width, :], (((1,), (1,)), ((), ())), preferred_element_type=F32
            )
            wexp[:, k0 : k0 + width] = jnp.exp2(score * (HD**-0.5 * 1.4426950408889634)).astype(BF16)
        term = jnp.dot(wexp[...], vbuf[slot], preferred_element_type=F32)
        mask = sees(seen[n])
        total[0:TOK, :] += jnp.where(mask, term[:TOK], 0.0)
        total[TOK:, :] += jnp.where(mask, term[TOK:], 0.0)
        return carry

    lax.fori_loop(0, count, image, 0)
    for h in range(2):
        part = total[h * TOK : (h + 1) * TOK, :]
        out[:, h * HD : (h + 1) * HD] = (part[:, :HD] / jnp.maximum(part[:, HD:], 1.0)).astype(BF16)


def attend(q, seg, kv):
    vmem, anyspace = (pl.BlockSpec(memory_space=m) for m in (pltpu.VMEM, pl.ANY))
    return pl.pallas_call(
        attend_kernel,
        out_shape=jax.ShapeDtypeStruct((TOK, 256), BF16),
        in_specs=[vmem, vmem, anyspace],
        out_specs=vmem,
        scratch_shapes=[
            pltpu.VMEM((IMAGES, 16, HD), BF16),
            pltpu.VMEM((2, ROWS, HD), BF16),
            pltpu.VMEM((2, ROWS, 256), BF16),
            pltpu.VMEM((2 * TOK, ROWS), BF16),
            pltpu.VMEM((2 * TOK, 256), F32),
            pltpu.SMEM((IMAGES,), jnp.int32),
            pltpu.SemaphoreType.DMA((2, 2)),
            pltpu.SemaphoreType.DMA,
        ],
        compiler_params=pltpu.CompilerParams(vmem_limit_bytes=48 * 2**20),
        cost_estimate=pl.CostEstimate(flops=5 * 10**9, bytes_accessed=10**7, transcendentals=5 * 10**6),
    )(q, seg, kv)


def back_kernel(att, gate, wout, pwout, out, patt, wo, pwo, got, sent, load_sem, e_send, e_recv, bs, br):
    me = Place()
    z, c = me.z, me.c
    loads = [pltpu.make_async_copy(pwout, pwo, load_sem.at[8])]
    for k in range(8):
        src = wout.at[:, pl.ds(pl.multiple_of((2 * k + c) * 512, 512), 512)]
        loads.append(pltpu.make_async_copy(src, wo.at[k], load_sem.at[k]))
    for load in loads:
        load.start()
    greet([me.partner, me.up, me.down])
    sends = []

    def send(src, dst, ssem, rsem, device):
        copy = remote(src, dst, ssem, rsem, device)
        copy.start()
        sends.append(copy)

    send(att, patt, e_send, e_recv, me.partner)
    for load in loads:
        load.wait()
    remote(att, patt, e_send, e_recv, me.partner).wait_recv()

    def term(way, d):
        rows = slice(way * 128, way * 128 + 128)
        part = jnp.dot(att[rows, :], wo[d], preferred_element_type=F32)
        return part + jnp.dot(patt[rows, :], pwo[d], preferred_element_type=F32)

    for step in range(8):
        for way in (0, 1):
            d = (z + (7 - step if way == 0 else 1 + step)) % 8
            part = term(way, d)
            if step > 0:
                remote(got.at[step - 1, way], got.at[step - 1, way], bs.at[way, step - 1], br.at[way, step - 1], me.partner).wait_recv()
                part += got[step - 1, way].astype(F32)
            if step < 7:
                sent[step, way] = part.astype(BF16)
                send(sent.at[step, way], got.at[step, way], bs.at[way, step], br.at[way, step], (me.up, me.down)[way])
            else:
                scale = jnp.tanh(jnp.full((1, 512), gate[0], F32))
                out[way * 128 : way * 128 + 128, :] = (scale * part).astype(BF16)
    for copy in sends:
        copy.wait_send()


def back(att, gate, wout, pwout):
    vmem, anyspace, smem = (pl.BlockSpec(memory_space=m) for m in (pltpu.VMEM, pl.ANY, pltpu.SMEM))
    dma = pltpu.SemaphoreType.DMA
    return pl.pallas_call(
        back_kernel,
        out_shape=jax.ShapeDtypeStruct((TOK, 512), BF16),
        in_specs=[vmem, smem, anyspace, anyspace],
        out_specs=vmem,
        scratch_shapes=[
            pltpu.VMEM((TOK, 256), BF16),
            pltpu.VMEM((8, 256, 512), BF16),
            pltpu.VMEM((8, 256, 512), BF16),
            pltpu.VMEM((7, 2, 128, 512), BF16),
            pltpu.VMEM((7, 2, 128, 512), BF16),
            dma((9,)),
            dma,
            dma,
            dma((2, 7)),
            dma((2, 7)),
        ],
        compiler_params=pltpu.CompilerParams(
            collective_id=1, has_side_effects=True, vmem_limit_bytes=48 * 2**20
        ),
        cost_estimate=pl.CostEstimate(flops=10**9, bytes_accessed=5 * 10**6, transcendentals=0),
    )(att, gate, wout, pwout)


def on_device(
    text, gain, wq, wkv, wout, qgain, kgain, gate, images, seg, owner, pos
):
    img = jnp.pad(images[0], ((0, ROWS - IMG_TOK), (0, 0)))
    q, kv, pwout = front(
        text, gain.reshape(1, -1), wq, wkv, wout, qgain.reshape(1, -1), kgain.reshape(1, -1), owner, pos, img
    )
    att = attend(q, seg.reshape(-1, 1), kv)
    return back(att, gate, wout, pwout)


def solution(mesh):
    rows = ("seq", "section")
    return jax.shard_map(
        on_device,
        mesh=mesh,
        in_specs=(
            P(rows, "tp"),
            P("tp"),
            P(None, "tp"),
            P("tp", None),
            P("tp", None),
            P(),
            P(),
            P(),
            P(rows, None, "tp"),
            P(rows),
            P(rows),
            P(rows),
        ),
        out_specs=P(rows, "tp"),
        check_vma=False,
    )
```

time: 607 us -> 162 us (0.27)
  the two profiles are of different devices: /device:TPU:1 before, /device:TPU:30 now
where the time goes in v1:
time: 162 us
  Pallas kernels  154 us (95%)
  local copies, waits for them, and re-layouts  5.73 us (4%)
  between operations  2.01 us (1%)
    pallas_call x1, Pallas kernels, front(): pl.pallas_call(front_kernel, out_shape=(jax.ShapeDtypeStruct((TOK, 256),...  98 us
    pallas_call x1, Pallas kernels, back(): pl.pallas_call(back_kernel, out_shape=jax.ShapeDtypeStruct((TOK, 512), BF...  37.1 us
    pallas_call x1, Pallas kernels, attend(): pl.pallas_call(attend_kernel, out_shape=jax.ShapeDtypeStruct((TOK, 256),...  19 us

profile of v1, /device:TPU:30, one launch (start us, length us, event | category | flops | bytes accessed | tf_op | source)
XLA Modules:
  0.0 161.9 jit_solution(2174898343775766882)
XLA Ops:
  0.0 2.7 %pad.4.img = bf16[1664,512]{1,0:T(8,128)(2,1)} pad(bf16[1601,512]{1,0:T(8,128)(2,1)} %bitcast.4, bf16[]{:T(256)} %constant.2.clone.1), padding=0_63x0_0 | pad | bytes 3343362 | tf_op jit(solution)/shard_map/jit(_pad)/pad | solution.py:597
  2.7 1.3 reshape.12.gain
  5.3 0.0 copy-start.2
  5.3 98.0 %shard_map.118 = (bf16[256,256]{1,0:T(8,128)(2,1)}, bf16[16,1664,256]{2,1,0:T(8,128)(2,1)}, bf16[8,256,512]{2,1,0:T(8,128)(2,1)}) custom-call(bf16[256,512]{1,0:T(8,128)(2,1)} %text.1, bf16[1,512]{1,0:T(2,128)(2,1)} %reshape.12.gain, bf16[8192,256]{1,0:T(8,128)(2,1)} %wq.1, bf16[512,1024]{1,0:T(8,128)(2,1)} %wkv.1, bf16[256,8192]{1,0:T(8,128)(2,1)} %wout.3, ...), custom_call_target="tpu_custom_call" | custom-call | flops 5000000000 | bytes 30000000 | tf_op jit(solution)/shard_map/pallas_call | solution.py:376
  103.3 0.0 copy-done.2
  103.3 0.1 copy.13.seg
  103.5 0.0 copy-start.1
  103.5 0.9 copy-done.1
  104.4 0.0 copy-start
  104.4 19.0 %shard_map.119.att = bf16[256,256]{1,0:T(8,128)(2,1)S(1)} custom-call(bf16[256,256]{1,0:T(8,128)(2,1)S(1)} %copy-done.1, s32[256,1]{1,0:T(8,128)S(1)} %copy.13.seg, bf16[16,1664,256]{2,1,0:T(8,128)(2,1)} %get-tuple-element.9.kv), custom_call_target="tpu_custom_call" | custom-call | flops 5000000000 | bytes 10000000 | tf_op jit(solution)/shard_map/pallas_call | solution.py:503
  124.0 0.0 copy-done
  124.0 37.1 %shard_map.120 = bf16[256,512]{1,0:T(8,128)(2,1)S(1)} custom-call(bf16[256,256]{1,0:T(8,128)(2,1)S(1)} %shard_map.119.att, f32[1]{0:T(128)S(6)} %copy.15.gate, bf16[256,8192]{1,0:T(8,128)(2,1)} %wout.3, bf16[8,256,512]{2,1,0:T(8,128)(2,1)S(1)} %copy-done), custom_call_target="tpu_custom_call" | custom-call | flops 1000000000 | bytes 5000000 | tf_op jit(solution)/shard_map/pallas_call | solution.py:570
  161.1 0.7 copy.18
Async XLA Ops:
  5.3 98.1 %copy-start.2 = (s32[256]{0:T(256)S(1)}, s32[256]{0:T(256)}, u32[]{:S(2)}) copy-start(s32[256]{0:T(256)} %param.21) | copy-start | bytes 3076
  103.5 0.9 copy-start.1
  104.4 19.6 %copy-start = (bf16[8,256,512]{2,1,0:T(8,128)(2,1)S(1)}, bf16[8,256,512]{2,1,0:T(8,128)(2,1)}, u32[]{:S(2)}) copy-start(bf16[8,256,512]{2,1,0:T(8,128)(2,1)} %get-tuple-element.10.pwout) | copy-start | bytes 6291460

commit v2 on v1

--- a/solution.py
+++ b/solution.py
@@ -20,8 +20,8 @@
 META = 2.0**-20
 META_ROW = ROWS - 16
 
-SUBS = ((0, 112, 96), (208, 96, 112))
-LAG = 5
+SUBS = ((0, 48, 48), (96, 80, 80), (256, 80, 80))
+BODY = 768
 
 
 def remote(src, dst, send, recv, device):
@@ -58,14 +58,42 @@
 
 
 def front_kernel(
-    text, gain, wq, wkv, wout, qgain, kgain, owner, pos, img,
+    text, gain, tail, wq, wkv, wout, qgain, kgain, owner, pos, img,
     q_out, kv, pwout,
-    nall, wqv, qacc, imgv, pimg, wkvv, pwkv, acck, accv, rk, rv, vfirst, mine,
+    nall, wqv, qacc, imgv, pimg, tailv, wkvv, pwkv, acck, accv, rk, rv, vfirst, mine,
     load_sem, ex_send, ex_recv, bs, br, xs, xr, ps, pr, cs, cr, as_, ar, acs, acr, ws, wr,
 ):
     me = Place()
     z, c = me.z, me.c
     zpar = z % 2
+    loads = [
+        pltpu.make_async_copy(img.at[0, pl.ds(c * HALF, BODY)], imgv.at[pl.ds(0, BODY)], load_sem.at[0]),
+        pltpu.make_async_copy(wkv, wkvv, load_sem.at[1]),
+    ]
+    for k in range(4):
+        part = pl.ds(k * 2048, 2048)
+        loads.append(pltpu.make_async_copy(wq.at[part], wqv.at[part], load_sem.at[2 + k]))
+    rest = pl.ds(BODY, HALF - BODY)
+    load_rest = pltpu.make_async_copy(img.at[0, rest], imgv.at[rest], load_sem.at[6])
+    loads[0].start()
+    loads[1].start()
+
+    @pl.when(c == 0)
+    def _():
+        load_rest.start()
+
+    row = lax.broadcasted_iota(jnp.int32, (16, 512), 0)
+    tailv[...] = jnp.zeros_like(tailv)
+    tailv[0:16, :] = jnp.where(row == 0, tail[...].astype(F32), 0.0).astype(BF16)
+
+    @pl.when(c == 1)
+    def _():
+        imgv[BODY:, :] = tailv[...]
+
+    nall[me.tp] = (text[...].astype(F32) * gain[...].astype(F32).reshape(1, 512)).astype(BF16)
+    for load in loads[2:]:
+        load.start()
+
     greet([me.partner, me.up, me.down] + [me.step(a, d) for a in "xy" for d in (1, 3)])
     sends = []
 
@@ -77,19 +105,22 @@
     def arrived(ref, ssem, rsem):
         remote(ref, ref, ssem, rsem, me.partner).wait_recv()
 
-    send(img.at[pl.ds((1 - c) * HALF, HALF)], pimg, ex_send.at[0], ex_recv.at[0], me.partner)
+    send(img.at[0, pl.ds((1 - c) * HALF, BODY)], pimg.at[pl.ds(0, BODY)], ex_send.at[0], ex_recv.at[0], me.partner)
     send(wkv, pwkv, ex_send.at[1], ex_recv.at[1], me.partner)
-    loads = [
-        pltpu.make_async_copy(img.at[pl.ds(c * HALF, HALF)], imgv, load_sem.at[0]),
-        pltpu.make_async_copy(wkv, wkvv, load_sem.at[1]),
-        pltpu.make_async_copy(wq, wqv, load_sem.at[2]),
-    ]
-    for load in loads:
-        load.start()
+    give_rest = remote(img.at[0, rest], pimg.at[rest], ex_send.at[2], ex_recv.at[2], me.partner)
+    give_tail = remote(tailv, pimg.at[rest], ex_send.at[2], ex_recv.at[2], me.partner)
+
+    @pl.when(c == 1)
+    def _():
+        give_rest.start()
+
+    @pl.when(c == 0)
+    def _():
+        give_tail.start()
+
+    sends.append(give_tail)
 
     shard = lambda k: ((z + k % 8) % 8) * 2 + c
-    nall[me.tp] = (text[...].astype(F32) * gain[...].astype(F32)).astype(BF16)
-    qacc[...] = jnp.zeros_like(qacc)
 
     def text_send(k, way, hop):
         ref = nall.at[shard(k)]
@@ -100,10 +131,6 @@
     def text_share(k):
         ref = nall.at[shard(k)]
         send(ref, ref, acs.at[k % 8], acr.at[k % 8], me.partner)
-
-    def text_use(index):
-        w = wqv[pl.ds(pl.multiple_of(index * 512, 512), 512), :]
-        qacc[...] += jnp.dot(nall[index], w, preferred_element_type=F32)
 
     def text_arrived(hop, way):
         k = -hop if way == 0 else hop
@@ -122,15 +149,20 @@
         if hop == 4:
             text_share(4)
 
-    def text_compute(hop):
-        for k in {0: (0,), 4: (4,)}.get(hop, (hop, -hop)):
-            text_use(shard(k))
-
-    def text_compute_shared(hop):
-        for k in {0: (0,), 4: (4,)}.get(hop, (hop, -hop)):
-            index = ((z + k % 8) % 8) * 2 + 1 - c
-            arrived(nall.at[index], acs.at[k % 8], acr.at[k % 8])
-            text_use(index)
+    def text_compute():
+        for k in range(8):
+            ref = nall.at[((z + k) % 8) * 2 + 1 - c]
+            arrived(ref, acs.at[k], acr.at[k])
+        for load in loads[2:]:
+            load.wait()
+        qacc[...] = jnp.zeros_like(qacc)
+
+        def use(index, carry):
+            w = wqv[pl.ds(pl.multiple_of(index * 512, 512), 512), :]
+            qacc[...] += jnp.dot(nall[index], w, preferred_element_type=F32)
+            return carry
+
+        lax.fori_loop(0, 16, use, 0)
 
     text_send(0, 0, 1)
     text_send(0, 1, 1)
@@ -138,8 +170,14 @@
 
     loads[0].wait()
     loads[1].wait()
-    arrived(pimg, ex_send.at[0], ex_recv.at[0])
+
+    @pl.when(c == 0)
+    def _():
+        load_rest.wait()
+
+    arrived(pimg.at[pl.ds(0, BODY)], ex_send.at[0], ex_recv.at[0])
     arrived(pwkv, ex_send.at[1], ex_recv.at[1])
+    arrived(pimg.at[rest], ex_send.at[2], ex_recv.at[2])
 
     def project(k):
         d = (z + k) % 8
@@ -150,41 +188,45 @@
         acck[d] = part[:, :HD]
         accv[d] = part[:, HD:]
 
-    def ring_rows(u, way):
+    def ring_rows(u, way, stage):
         start, first, second = SUBS[u]
-        return (start, first) if way == 0 else (start + first, second)
-
-    def ring_send(u, step):
+        if stage > 0:
+            return pl.ds(start, first + second)
+        return pl.ds(start, first) if way == 0 else pl.ds(start + first, second)
+
+    def ring_send(u, stage):
         for way in (0, 1):
-            r0, n = ring_rows(u, way)
-            device = (me.up, me.down)[way]
-            rows = pl.ds(r0, n)
-            if step == 0:
-                d = (z + (7, 1)[way]) % 8
+            rows = ring_rows(u, way, stage)
+            if stage == 0:
+                d = (z + 4) % 8
                 vfirst[rows, :] = accv[d, rows, :].astype(BF16)
                 srck, srcv = acck.at[d, rows], vfirst.at[rows]
             else:
-                srck, srcv = rk.at[step - 1, rows], rv.at[step - 1, rows]
-            send(srck, rk.at[step, rows], bs.at[u, way, step, 0], br.at[u, way, step, 0], device)
-            send(srcv, rv.at[step, rows], bs.at[u, way, step, 1], br.at[u, way, step, 1], device)
-
-    def ring_receive(u, step):
+                srck, srcv = rk.at[way, stage - 1, rows], rv.at[way, stage - 1, rows]
+            device = (me.up, me.down)[way]
+            send(srck, rk.at[way, stage, rows], bs.at[u, way, stage, 0], br.at[u, way, stage, 0], device)
+            send(srcv, rv.at[way, stage, rows], bs.at[u, way, stage, 1], br.at[u, way, stage, 1], device)
+
+    def ring_receive(u, stage):
         for way in (0, 1):
-            r0, n = ring_rows(u, way)
-            rows = pl.ds(r0, n)
-            arrived(rk.at[step, rows], bs.at[u, way, step, 0], br.at[u, way, step, 0])
-            arrived(rv.at[step, rows], bs.at[u, way, step, 1], br.at[u, way, step, 1])
-            if step < 6:
-                d = (z + (6 - step if way == 0 else 2 + step)) % 8
-                rk[step, rows, :] += acck[d, rows, :]
-                rv[step, rows, :] = (rv[step, rows, :].astype(F32) + accv[d, rows, :]).astype(BF16)
+            rows = ring_rows(u, way, stage)
+            d = (z + (3 - stage if way == 0 else 5 + stage)) % 8
+            if stage == 0:
+                other = ring_rows(u, 1 - way, 0)
+                rk[way, 0, other, :] = acck[d, other, :]
+                rv[way, 0, other, :] = accv[d, other, :].astype(BF16)
+            arrived(rk.at[way, stage, rows], bs.at[u, way, stage, 0], br.at[u, way, stage, 0])
+            arrived(rv.at[way, stage, rows], bs.at[u, way, stage, 1], br.at[u, way, stage, 1])
+            if stage < 3:
+                rk[way, stage, rows, :] += acck[d, rows, :]
+                rv[way, stage, rows, :] = (rv[way, stage, rows, :].astype(F32) + accv[d, rows, :]).astype(BF16)
 
     def finish(u):
         start, first, second = SUBS[u]
         n = first + second
         rows = pl.ds(start, n)
-        key = rk[6, rows, :] + acck[z, rows, :]
-        val = rv[6, rows, :].astype(F32) + accv[z, rows, :]
+        key = rk[0, 3, rows, :] + rk[1, 3, rows, :] + acck[z, rows, :]
+        val = rv[0, 3, rows, :].astype(F32) + rv[1, 3, rows, :].astype(F32) + accv[z, rows, :]
         key = key * lax.rsqrt(jnp.mean(key * key, axis=-1, keepdims=True) + EPS) * kgain[...]
         if u == len(SUBS) - 1:
             row = c * HALF + zpar * QUARTER + start + lax.broadcasted_iota(jnp.int32, (n, HD), 0)
@@ -264,7 +306,7 @@
                 spread_first(u, par, 0, 0)
                 spread_first(u, par, 0, 1)
                 column(u, par, 0)
-                keep = pltpu.make_async_copy(own(u, par), block(u, par, 0, 0), load_sem.at[3 + 2 * u + par])
+                keep = pltpu.make_async_copy(own(u, par), block(u, par, 0, 0), load_sem.at[7 + 2 * u + par])
                 keep.start()
                 local.append(keep)
             if r == 1:
@@ -290,69 +332,69 @@
                     second_arrived(u, par, i, 2)
                     share(u, par, i, 2)
 
-    def ring_step(u, step):
-        ring_receive(u, step)
-        if step < 6:
-            ring_send(u, step + 1)
+    def ring_step(u, stage):
+        ring_receive(u, stage)
+        if stage < 3:
+            ring_send(u, stage + 1)
         else:
             finish(u)
 
-    project(7)
-    project(1)
+    def project_next(n, carry):
+        project(4 + jnp.where(n % 2 == 1, -((n + 1) // 2), n // 2))
+        return carry
+
+    project(4)
     ring_send(0, 0)
-    for k in (6, 2, 5, 3, 4, 0):
-        project(k)
+    lax.fori_loop(1, 8, project_next, 0)
     for k in range(8):
         src = wout.at[:, pl.ds(pl.multiple_of((2 * k + 1 - c) * 512, 512), 512)]
         send(src, pwout.at[k], ws.at[k], wr.at[k], me.partner)
-    loads[2].wait()
-    text_compute(0)
-
-    for step in range(LAG):
-        ring_step(0, step)
+
+    ring_step(0, 0)
     ring_send(1, 0)
-    for step in range(LAG, 7):
-        ring_step(0, step)
-        ring_step(1, step - LAG)
-    done = 7 - LAG
+    ring_step(0, 1)
+    ring_step(1, 0)
+    ring_send(2, 0)
+    ring_step(0, 2)
+    ring_step(1, 1)
+    ring_step(2, 0)
+    ring_step(0, 3)
+    ring_step(1, 2)
+    ring_step(2, 1)
     plane_round(0, 0)
-    ring_step(1, done)
+    ring_step(1, 3)
+    ring_step(2, 2)
     plane_round(0, 1)
-    ring_step(1, done + 1)
+    plane_round(1, 0)
+    text_round(1)
+    ring_step(2, 3)
     plane_round(0, 2)
-    ring_step(1, done + 2)
     plane_round(0, 3)
-    for step in range(done + 3, 7):
-        ring_step(1, step)
-    text_round(1)
-    plane_round(1, 0)
+    plane_round(1, 1)
+    plane_round(2, 0)
     plane_round(0, 4)
-    text_compute(1)
+    plane_round(1, 2)
+    text_round(2)
     plane_round(0, 5)
-    plane_round(1, 1)
-    text_round(2)
+    plane_round(1, 3)
     plane_round(0, 6)
-    text_compute(2)
-    text_compute_shared(0)
-    plane_round(1, 2)
-    plane_round(1, 3)
+    plane_round(2, 1)
+    plane_round(1, 4)
     text_round(3)
-    text_compute(3)
-    text_compute_shared(1)
-    plane_round(1, 4)
-    text_compute_shared(2)
+    plane_round(2, 2)
+    plane_round(2, 3)
+    plane_round(1, 5)
+    plane_round(1, 6)
+    plane_round(2, 4)
     text_round(4)
-    plane_round(1, 5)
-    text_compute(4)
-    text_compute_shared(3)
-    text_compute_shared(4)
-
+    plane_round(2, 5)
+    text_compute()
     for h in range(2):
         q = qacc[:, h * HD : (h + 1) * HD]
         q = q * lax.rsqrt(jnp.mean(q * q, axis=-1, keepdims=True) + EPS) * qgain[...]
         q_out[:, h * HD : (h + 1) * HD] = q.astype(BF16)
 
-    plane_round(1, 6)
+    plane_round(2, 6)
     for u, (start, first, second) in enumerate(SUBS):
         for par in (0, 1):
             for i in range(4):
@@ -369,7 +411,7 @@
         copy.wait_send()
 
 
-def front(text, gain, wq, wkv, wout, qgain, kgain, owner, pos, img):
+def front(text, gain, tail, wq, wkv, wout, qgain, kgain, owner, pos, img):
     vmem, anyspace, smem = (pl.BlockSpec(memory_space=m) for m in (pltpu.VMEM, pl.ANY, pltpu.SMEM))
     dma = pltpu.SemaphoreType.DMA
     n = len(SUBS)
@@ -380,7 +422,7 @@
             jax.ShapeDtypeStruct((IMAGES, ROWS, 256), BF16),
             jax.ShapeDtypeStruct((8, 256, 512), BF16),
         ),
-        in_specs=[vmem, vmem, anyspace, anyspace, anyspace, vmem, vmem, smem, smem, anyspace],
+        in_specs=[vmem, vmem, vmem, anyspace, anyspace, anyspace, vmem, vmem, smem, smem, anyspace],
         out_specs=(vmem, anyspace, anyspace),
         scratch_shapes=[
             pltpu.VMEM((16, TOK, 512), BF16),
@@ -388,19 +430,20 @@
             pltpu.VMEM((TOK, 256), F32),
             pltpu.VMEM((HALF, 512), BF16),
             pltpu.VMEM((HALF, 512), BF16),
+            pltpu.VMEM((HALF - BODY, 512), BF16),
             pltpu.VMEM((512, 1024), BF16),
             pltpu.VMEM((512, 1024), BF16),
             pltpu.VMEM((8, QUARTER, HD), F32),
             pltpu.VMEM((8, QUARTER, HD), F32),
-            pltpu.VMEM((7, QUARTER, HD), F32),
-            pltpu.VMEM((7, QUARTER, HD), BF16),
+            pltpu.VMEM((2, 4, QUARTER, HD), F32),
+            pltpu.VMEM((2, 4, QUARTER, HD), BF16),
             pltpu.VMEM((QUARTER, HD), BF16),
             pltpu.VMEM((HALF, 256), BF16),
-            dma((3 + 2 * n,)),
-            dma((2,)),
-            dma((2,)),
-            dma((n, 2, 7, 2)),
-            dma((n, 2, 7, 2)),
+            dma((7 + 2 * n,)),
+            dma((3,)),
+            dma((3,)),
+            dma((n, 2, 4, 2)),
+            dma((n, 2, 4, 2)),
             dma((n,)),
             dma((n,)),
             dma((n, 2, 16)),
@@ -418,7 +461,7 @@
             collective_id=0, has_side_effects=True, vmem_limit_bytes=56 * 2**20
         ),
         cost_estimate=pl.CostEstimate(flops=5 * 10**9, bytes_accessed=3 * 10**7, transcendentals=0),
-    )(text, gain, wq, wkv, wout, qgain, kgain, owner, pos, img)
+    )(text, gain, tail, wq, wkv, wout, qgain, kgain, owner, pos, img)
 
 
 TILES = ((0, 256), (256, 256), (512, 256), (768, 256), (1024, 256), (1280, 256), (1536, 128))
@@ -435,7 +478,7 @@
     vbuf[1, :, HD:] = ones
     fetch.wait()
     places = (first + lax.broadcasted_iota(jnp.int32, (TOK, 1), 0)).astype(F32)
-    docs = seg[...].astype(F32)
+    docs = jnp.broadcast_to(seg[...].astype(F32).reshape(1, TOK), (HD, TOK)).T[:, 0:1]
 
     def sees(m):
         said = meta[m, 0:1, :].astype(F32) * (1.0 / META)
@@ -520,13 +563,15 @@
     )(q, seg, kv)
 
 
-def back_kernel(att, gate, wout, pwout, out, patt, wo, pwo, got, sent, load_sem, e_send, e_recv, bs, br):
+def back_kernel(att, gate, wout, pwout, out, patt, wo, pwo, terms, got, sent, load_sem, e_send, e_recv, bs, br):
     me = Place()
     z, c = me.z, me.c
-    loads = [pltpu.make_async_copy(pwout, pwo, load_sem.at[8])]
-    for k in range(8):
+    loads = []
+    for n in range(8):
+        k = (z + 4 + n) % 8
         src = wout.at[:, pl.ds(pl.multiple_of((2 * k + c) * 512, 512), 512)]
-        loads.append(pltpu.make_async_copy(src, wo.at[k], load_sem.at[k]))
+        loads.append(pltpu.make_async_copy(src, wo.at[k], load_sem.at[0, n]))
+        loads.append(pltpu.make_async_copy(pwout.at[k], pwo.at[k], load_sem.at[1, n]))
     for load in loads:
         load.start()
     greet([me.partner, me.up, me.down])
@@ -538,28 +583,65 @@
         sends.append(copy)
 
     send(att, patt, e_send, e_recv, me.partner)
-    for load in loads:
+
+    def term(d):
+        part = jnp.dot(att[...], wo[d], preferred_element_type=F32)
+        terms[d] = part + jnp.dot(patt[...], pwo[d], preferred_element_type=F32)
+
+    def place(e, way, stage):
+        cols = pl.ds(e * 256, 256)
+        return (pl.ds(way * 128, 128) if stage == 0 else pl.ds(0, TOK)), cols
+
+    def ring_send(e, stage):
+        for way in (0, 1):
+            rows, cols = place(e, way, stage)
+            d = (z + (4 - stage if way == 0 else 4 + stage)) % 8
+            part = terms[d, :, cols]
+            if stage == 0:
+                part = part[way * 128 : way * 128 + 128]
+            elif stage == 1:
+                half = got[way, 0, way * 128 : way * 128 + 128, cols].astype(F32)
+                parts = [part[:128], part[128:]]
+                parts[way] += half
+                part = jnp.concatenate(parts, axis=0)
+            else:
+                part += got[way, stage - 1, :, cols].astype(F32)
+            sent[way, stage, rows, cols] = part.astype(BF16)
+            send(
+                sent.at[way, stage, rows, cols], got.at[way, stage, rows, cols],
+                bs.at[e, way, stage], br.at[e, way, stage], (me.up, me.down)[way],
+            )
+
+    def ring_arrived(e, stage):
+        for way in (0, 1):
+            rows, cols = place(e, way, stage)
+            ref = got.at[way, stage, rows, cols]
+            remote(ref, ref, bs.at[e, way, stage], br.at[e, way, stage], me.partner).wait_recv()
+
+    for load in loads[:2]:
         load.wait()
     remote(att, patt, e_send, e_recv, me.partner).wait_recv()
-
-    def term(way, d):
-        rows = slice(way * 128, way * 128 + 128)
-        part = jnp.dot(att[rows, :], wo[d], preferred_element_type=F32)
-        return part + jnp.dot(patt[rows, :], pwo[d], preferred_element_type=F32)
-
-    for step in range(8):
-        for way in (0, 1):
-            d = (z + (7 - step if way == 0 else 1 + step)) % 8
-            part = term(way, d)
-            if step > 0:
-                remote(got.at[step - 1, way], got.at[step - 1, way], bs.at[way, step - 1], br.at[way, step - 1], me.partner).wait_recv()
-                part += got[step - 1, way].astype(F32)
-            if step < 7:
-                sent[step, way] = part.astype(BF16)
-                send(sent.at[step, way], got.at[step, way], bs.at[way, step], br.at[way, step], (me.up, me.down)[way])
-            else:
-                scale = jnp.tanh(jnp.full((1, 512), gate[0], F32))
-                out[way * 128 : way * 128 + 128, :] = (scale * part).astype(BF16)
+    term((z + 4) % 8)
+    ring_send(0, 0)
+    ring_send(1, 0)
+    for load in loads[2:]:
+        load.wait()
+
+    def next_term(n, carry):
+        term((z + 4 + jnp.where(n % 2 == 1, -((n + 1) // 2), n // 2)) % 8)
+        return carry
+
+    lax.fori_loop(1, 8, next_term, 0)
+    for stage in range(3):
+        for e in (0, 1):
+            ring_arrived(e, stage)
+            ring_send(e, stage + 1)
+    scale = jnp.tanh(jnp.full((1, 256), gate[0], F32))
+    for e in (0, 1):
+        ring_arrived(e, 3)
+        cols = pl.ds(e * 256, 256)
+        part = terms[z, :, cols] + got[0, 3, :, cols].astype(F32) + got[1, 3, :, cols].astype(F32)
+        out[:, e * 256 : e * 256 + 256] = (scale * part).astype(BF16)
     for copy in sends:
         copy.wait_send()
 
@@ -576,13 +658,14 @@
             pltpu.VMEM((TOK, 256), BF16),
             pltpu.VMEM((8, 256, 512), BF16),
             pltpu.VMEM((8, 256, 512), BF16),
-            pltpu.VMEM((7, 2, 128, 512), BF16),
-            pltpu.VMEM((7, 2, 128, 512), BF16),
-            dma((9,)),
+            pltpu.VMEM((8, TOK, 512), F32),
+            pltpu.VMEM((2, 4, TOK, 512), BF16),
+            pltpu.VMEM((2, 4, TOK, 512), BF16),
+            dma((2, 8)),
             dma,
             dma,
-            dma((2, 7)),
-            dma((2, 7)),
+            dma((2, 2, 4)),
+            dma((2, 2, 4)),
         ],
         compiler_params=pltpu.CompilerParams(
             collective_id=1, has_side_effects=True, vmem_limit_bytes=48 * 2**20
@@ -594,11 +677,10 @@
 def on_device(
     text, gain, wq, wkv, wout, qgain, kgain, gate, images, seg, owner, pos
 ):
-    img = jnp.pad(images[0], ((0, ROWS - IMG_TOK), (0, 0)))
     q, kv, pwout = front(
-        text, gain.reshape(1, -1), wq, wkv, wout, qgain.reshape(1, -1), kgain.reshape(1, -1), owner, pos, img
+        text, gain, images[0, IMG_TOK - 1 :], wq, wkv, wout, qgain.reshape(1, -1), kgain.reshape(1, -1), owner, pos, images
     )
-    att = attend(q, seg.reshape(-1, 1), kv)
+    att = attend(q, seg, kv)
     return back(att, gate, wout, pwout)
 
 

time: 162 us -> 139 us (0.86)
  the two profiles are of different devices: /device:TPU:30 before, /device:TPU:23 now
where the time goes in v2:
time: 139 us; the launch traced here: 138 us
  Pallas kernels  134 us (96%)
  local copies, waits for them, and re-layouts  2.89 us (2%)
  between operations  2 us (1%)
    pallas_call x1, Pallas kernels, front(): pl.pallas_call(front_kernel, out_shape=(jax.ShapeDtypeStruct((TOK, 256),...  87.8 us
    pallas_call x1, Pallas kernels, back(): pl.pallas_call(back_kernel, out_shape=jax.ShapeDtypeStruct((TOK, 512), BF...  28.2 us
    pallas_call x1, Pallas kernels, attend(): pl.pallas_call(attend_kernel, out_shape=jax.ShapeDtypeStruct((TOK, 256),...  17.5 us

profile of v2, /device:TPU:23, one launch (start us, length us, event | category | flops | bytes accessed | tf_op | source)
XLA Modules:
  0.0 138.5 jit_solution(5601917283565486302)
XLA Ops:
  0.0 1.3 slice_bitcast_fusion.tail
  2.6 0.0 copy-start.1
  2.6 87.8 %shard_map.118 = (bf16[256,256]{1,0:T(8,128)(2,1)}, bf16[16,1664,256]{2,1,0:T(8,128)(2,1)}, bf16[8,256,512]{2,1,0:T(8,128)(2,1)}) custom-call(bf16[256,512]{1,0:T(8,128)(2,1)} %text.1, bf16[512]{0:T(512)(128)(2,1)} %gain.1, bf16[1,512]{1,0:T(2,128)(2,1)} %slice_bitcast_fusion.tail, bf16[8192,256]{1,0:T(8,128)(2,1)} %wq.1, bf16[512,1024]{1,0:T(8,128)(2,1)} %wkv.1, ...), custom_call_target="tpu_custom_call" | custom-call | flops 5000000000 | bytes 30000000 | tf_op jit(solution)/shard_map/pallas_call | solution.py:418
  90.4 0.0 copy-done.1
  90.4 0.0 copy-start.2
  90.4 0.9 copy-done.2
  91.3 0.0 copy-start
  91.3 17.5 %shard_map.119.att = bf16[256,256]{1,0:T(8,128)(2,1)S(1)} custom-call(bf16[256,256]{1,0:T(8,128)(2,1)S(1)} %copy-done.2, s32[256]{0:T(256)S(1)} %copy-done.1, bf16[16,1664,256]{2,1,0:T(8,128)(2,1)} %get-tuple-element.9.kv), custom_call_target="tpu_custom_call" | custom-call | flops 5000000000 | bytes 10000000 | tf_op jit(solution)/shard_map/pallas_call | solution.py:546
  109.5 0.0 copy-done
  109.5 28.2 %shard_map.120 = bf16[256,512]{1,0:T(8,128)(2,1)S(1)} custom-call(bf16[256,256]{1,0:T(8,128)(2,1)S(1)} %shard_map.119.att, f32[1]{0:T(128)S(6)} %copy.14.gate, bf16[256,8192]{1,0:T(8,128)(2,1)} %wout.3, bf16[8,256,512]{2,1,0:T(8,128)(2,1)S(1)} %copy-done), custom_call_target="tpu_custom_call" | custom-call | flops 1000000000 | bytes 5000000 | tf_op jit(solution)/shard_map/pallas_call | solution.py:652
  137.8 0.7 copy.17
Async XLA Ops:
  2.6 87.8 %copy-start.1 = (s32[256]{0:T(256)S(1)}, s32[256]{0:T(256)}, u32[]{:S(2)}) copy-start(s32[256]{0:T(256)} %seg.1) | copy-start | bytes 3076
  90.4 0.9 copy-start.2
  91.3 18.2 %copy-start = (bf16[8,256,512]{2,1,0:T(8,128)(2,1)S(1)}, bf16[8,256,512]{2,1,0:T(8,128)(2,1)}, u32[]{:S(2)}) copy-start(bf16[8,256,512]{2,1,0:T(8,128)(2,1)} %get-tuple-element.10.pwout) | copy-start | bytes 6291460

commit v3 on v2

v3 whole, which is shorter than its diff:
```python
import jax
import jax.numpy as jnp
from jax import lax
from jax.experimental import pallas as pl
from jax.experimental.pallas import tpu as pltpu
from jax.sharding import PartitionSpec as P

MESH = pl.DeviceIdType.MESH
F32, BF16 = jnp.float32, jnp.bfloat16
HD = 128
IMG_TOK = 1601
IMAGES = 16
TOK = 256
QUARTER = 416
HALF = 2 * QUARTER
ROWS = 4 * QUARTER
EPS = 1e-05
META = 2.0**-40
META_ROW = ROWS - 16
VALID = 3 * 96 + IMG_TOK - 3 * QUARTER - 320

SUBS = ((320, 48, 48), (0, 112, 112), (224, 48, 48))
BODY = 768


def remote(src, dst, send, recv, device):
    return pltpu.make_async_remote_copy(
        src_ref=src, dst_ref=dst, send_sem=send, recv_sem=recv, device_id=device, device_id_type=MESH
    )


class Place:
    def __init__(self):
        seq, tp, sec = lax.axis_index("seq"), lax.axis_index("tp"), lax.axis_index("section")
        self.tp, self.z, self.c = tp, tp // 2, tp % 2
        self.x, self.y = seq // 2, sec * 2 + seq % 2
        self.partner = {"tp": self.z * 2 + 1 - self.c}
        self.up = {"tp": ((self.z + 1) % 8) * 2 + self.c}
        self.down = {"tp": ((self.z + 7) % 8) * 2 + self.c}

    def step(self, axis, delta):
        if axis == "x":
            return {"seq": ((self.x + delta) % 4) * 2 + self.y % 2}
        y = (self.y + delta) % 4
        return {"seq": self.x * 2 + y % 2, "section": y // 2}

    def image(self, dx, dy):
        y = (self.y + dy) % 4
        return ((self.x + dx) % 4) * 4 + (y % 2) * 2 + y // 2


NEAR = ((0, 0), (1, 0), (3, 0), (0, 1), (0, 3))
DIAGONAL = ((1, 1), (1, 3), (3, 1), (3, 3))
FAR = ((2, 0), (0, 2), (2, 1), (2, 3), (1, 2), (3, 2), (2, 2))


def greet(devices):
    barrier = pltpu.get_barrier_semaphore()
    for device in devices:
        pl.semaphore_signal(barrier, inc=1, device_id=device, device_id_type=MESH)
    pl.semaphore_wait(barrier, len(devices))


def kernel(
    text, gain, tail, wq, wkv, wout, qgain, kgain, gate, owner, pos, seg, img,
    out,
    nall, wqv, qacc, imgv, pimg, tailv, wkvv, pwkv, acck, accv, rk, rv, vfirst, mine,
    kv, qrows, wexp, total, mass, att, patt, wo, pwo, terms, got, sent,
    load_sem, ex_send, ex_recv, bs, br, xs, xr, ps, pr, cs, cr, as_, ar, acs, acr, ws, wr,
    wo_sem, es, er, ds, dr,
):
    me = Place()
    z, c = me.z, me.c
    zpar = z % 2
    loads = [
        pltpu.make_async_copy(img.at[0, pl.ds(c * HALF, BODY)], imgv.at[pl.ds(0, BODY)], load_sem.at[0]),
        pltpu.make_async_copy(wkv, wkvv, load_sem.at[1]),
    ]
    for k in range(4):
        part = pl.ds(k * 2048, 2048)
        loads.append(pltpu.make_async_copy(wq.at[part], wqv.at[part], load_sem.at[2 + k]))
    rest = pl.ds(BODY, HALF - BODY)
    load_rest = pltpu.make_async_copy(img.at[0, rest], imgv.at[rest], load_sem.at[6])
    loads[0].start()
    loads[1].start()

    @pl.when(c == 0)
    def _():
        load_rest.start()

    row = lax.broadcasted_iota(jnp.int32, (16, 512), 0)
    tailv[...] = jnp.zeros_like(tailv)
    tailv[0:16, :] = jnp.where(row == 0, tail[...].astype(F32), 0.0).astype(BF16)

    @pl.when(c == 1)
    def _():
        imgv[BODY:, :] = tailv[...]

    nall[me.tp] = (text[...].astype(F32) * gain[...].astype(F32).reshape(1, 512)).astype(BF16)
    for load in loads[2:6]:
        load.start()

    greet([me.partner, me.up, me.down] + [me.step(a, d) for a in "xy" for d in (1, 3)])
    sends = []

    def send(src, dst, ssem, rsem, device):
        copy = remote(src, dst, ssem, rsem, device)
        copy.start()
        sends.append(copy)

    def arrived(ref, ssem, rsem):
        remote(ref, ref, ssem, rsem, me.partner).wait_recv()

    send(img.at[0, pl.ds((1 - c) * HALF, BODY)], pimg.at[pl.ds(0, BODY)], ex_send.at[0], ex_recv.at[0], me.partner)
    send(wkv, pwkv, ex_send.at[1], ex_recv.at[1], me.partner)
    give_rest = remote(img.at[0, rest], pimg.at[rest], ex_send.at[2], ex_recv.at[2], me.partner)
    give_tail = remote(tailv, pimg.at[rest], ex_send.at[2], ex_recv.at[2], me.partner)

    @pl.when(c == 1)
    def _():
        give_rest.start()

    @pl.when(c == 0)
    def _():
        give_tail.start()

    sends.append(give_tail)

    shard = lambda k: ((z + k % 8) % 8) * 2 + c

    def text_send(k, way, hop):
        ref = nall.at[shard(k)]
        if hop == 4:
            ref = ref.at[pl.ds(way * 128, 128)]
        send(ref, ref, as_.at[way, hop - 1], ar.at[way, hop - 1], (me.up, me.down)[way])

    def text_share(k):
        ref = nall.at[shard(k)]
        send(ref, ref, acs.at[k % 8], acr.at[k % 8], me.partner)

    def text_arrived(hop, way):
        k = -hop if way == 0 else hop
        ref = nall.at[shard(k)]
        if hop == 4:
            ref = ref.at[pl.ds(way * 128, 128)]
        arrived(ref, as_.at[way, hop - 1], ar.at[way, hop - 1])

    def text_round(hop):
        for way in (0, 1):
            text_arrived(hop, way)
            if hop < 4:
                k = -hop if way == 0 else hop
                text_send(k, way, hop + 1)
                text_share(k)
        if hop == 4:
            text_share(4)

    def text_compute():
        for k in range(8):
            ref = nall.at[((z + k) % 8) * 2 + 1 - c]
            arrived(ref, acs.at[k], acr.at[k])
        for load in loads[2:6]:
            load.wait()
        qacc[...] = jnp.zeros_like(qacc)

        def use(index, carry):
            w = wqv[pl.ds(pl.multiple_of(index * 512, 512), 512), :]
            qacc[...] += jnp.dot(nall[index], w, preferred_element_type=F32)
            return carry

        lax.fori_loop(0, 16, use, 0)
        for h in range(2):
            q = qacc[:, h * HD : (h + 1) * HD]
            q = q * lax.rsqrt(jnp.mean(q * q, axis=-1, keepdims=True) + EPS) * qgain[...]
            qrows[h * TOK : (h + 1) * TOK, :] = q.astype(BF16)

    text_send(0, 0, 1)
    text_send(0, 1, 1)
    text_share(0)

    loads[0].wait()
    loads[1].wait()

    @pl.when(c == 0)
    def _():
        load_rest.wait()

    arrived(pimg.at[pl.ds(0, BODY)], ex_send.at[0], ex_recv.at[0])
    arrived(pwkv, ex_send.at[1], ex_recv.at[1])
    arrived(pimg.at[rest], ex_send.at[2], ex_recv.at[2])

    def project(d):
        rows = pl.ds(pl.multiple_of((d % 2) * QUARTER, QUARTER), QUARTER)
        cols = pl.ds(pl.multiple_of((d // 2) * 256, 256), 256)
        part = jnp.dot(imgv[rows, :], wkvv[:, cols], preferred_element_type=F32)
        part += jnp.dot(pimg[rows, :], pwkv[:, cols], preferred_element_type=F32)
        acck[d] = part[:, :HD]
        accv[d] = part[:, HD:]

    def ring_rows(u, way, stage):
        start, first, second = SUBS[u]
        if stage > 0:
            return pl.ds(start, first + second)
        return pl.ds(start, first) if way == 0 else pl.ds(start + first, second)

    def ring_send(u, stage):
        for way in (0, 1):
            rows = ring_rows(u, way, stage)
            if stage == 0:
                d = (z + 4) % 8
                vfirst[rows, :] = accv[d, rows, :].astype(BF16)
                srck, srcv = acck.at[d, rows], vfirst.at[rows]
            else:
                srck, srcv = rk.at[way, stage - 1, rows], rv.at[way, stage - 1, rows]
            device = (me.up, me.down)[way]
            send(srck, rk.at[way, stage, rows], bs.at[u, way, stage, 0], br.at[u, way, stage, 0], device)
            send(srcv, rv.at[way, stage, rows], bs.at[u, way, stage, 1], br.at[u, way, stage, 1], device)

    def ring_receive(u, stage):
        for way in (0, 1):
            rows = ring_rows(u, way, stage)
            d = (z + (3 - stage if way == 0 else 5 + stage)) % 8
            if stage == 0:
                other = ring_rows(u, 1 - way, 0)
                rk[way, 0, other, :] = acck[d, other, :]
                rv[way, 0, other, :] = accv[d, other, :].astype(BF16)
            arrived(rk.at[way, stage, rows], bs.at[u, way, stage, 0], br.at[u, way, stage, 0])
            arrived(rv.at[way, stage, rows], bs.at[u, way, stage, 1], br.at[u, way, stage, 1])
            if stage < 3:
                rk[way, stage, rows, :] += acck[d, rows, :]
                rv[way, stage, rows, :] = (rv[way, stage, rows, :].astype(F32) + accv[d, rows, :]).astype(BF16)

    def finish(u):
        start, first, second = SUBS[u]
        n = first + second
        rows = pl.ds(start, n)
        key = rk[0, 3, rows, :] + rk[1, 3, rows, :] + acck[z, rows, :]
        val = rv[0, 3, rows, :].astype(F32) + rv[1, 3, rows, :].astype(F32) + accv[z, rows, :]
        key = key * lax.rsqrt(jnp.mean(key * key, axis=-1, keepdims=True) + EPS) * kgain[...]
        if u == 0:
            row = c * HALF + zpar * QUARTER + start + lax.broadcasted_iota(jnp.int32, (n, HD), 0)
            lane = lax.broadcasted_iota(jnp.int32, (n, HD), 1)
            said = jnp.where(lane == 0, owner[0], jnp.where(lane == 1, pos[0] // 64, pos[0] % 64))
            said = jnp.where(lane < 3, said, 0).astype(F32) * META
            key = jnp.where(row >= META_ROW, said, key)
        at = pl.ds(pl.multiple_of(zpar * QUARTER + start, 16), n)
        mine[at, 0:HD] = key.astype(BF16)
        mine[at, HD:] = val.astype(BF16)
        pair = {"tp": (z + 1 - 2 * zpar) * 2 + c}
        send(mine.at[at], mine.at[at], xs.at[u], xr.at[u], pair)

    here = me.image(0, 0)

    def block(u, par, i, j, part=None):
        start, first, second = SUBS[u]
        n = first + second
        if part == 0:
            n = first
        if part == 1:
            start, n = start + first, second
        m = me.image(i, j) if par == 0 else me.image(j, i)
        r0 = pl.multiple_of(c * HALF + par * QUARTER + start, 16)
        return kv.at[m, pl.ds(r0, n)]

    def own(u, par):
        start, first, second = SUBS[u]
        return mine.at[pl.ds(par * QUARTER + start, first + second)]

    axes = lambda par: ("x", "y") if par == 0 else ("y", "x")

    def spread_first(u, par, i, way, part=None):
        slot = {(0, 0): 0, (0, 1): 1, (3, 0): 2, (1, 1): 3}[(i, way)]
        src = own(u, par) if i == 0 else block(u, par, i, 0, part)
        dst = block(u, par, i, 0, part)
        send(src, dst, ps.at[u, par, slot], pr.at[u, par, slot], me.step(axes(par)[0], (1, 3)[way]))

    def first_arrived(u, par, i, part=None):
        slot = {(3, None): 0, (1, None): 1, (2, 1): 2, (2, 0): 3}[(i, part)]
        arrived(block(u, par, i, 0, part), ps.at[u, par, slot], pr.at[u, par, slot])

    def spread_second(u, par, i, j, way):
        slot = 4 + 3 * i + (way if j == 0 else 2)
        src = own(u, par) if (i, j) == (0, 0) else block(u, par, i, j)
        send(src, block(u, par, i, j), ps.at[u, par, slot], pr.at[u, par, slot], me.step(axes(par)[1], (1, 3)[way]))

    def second_arrived(u, par, i, j):
        slot = 4 + 3 * i + {3: 0, 1: 1, 2: 2}[j]
        arrived(block(u, par, i, j), ps.at[u, par, slot], pr.at[u, par, slot])

    def share(u, par, i, j):
        src = own(u, par) if (i, j) == (0, 0) else block(u, par, i, j)
        send(src, block(u, par, i, j), cs.at[u, par, 4 * i + j], cr.at[u, par, 4 * i + j], me.partner)

    def column(u, par, i):
        spread_second(u, par, i, 0, 0)
        spread_second(u, par, i, 0, 1)
        share(u, par, i, 0)

    def column_arrived(u, par, i):
        for j, way in ((3, 0), (1, 1)):
            second_arrived(u, par, i, j)
            if (j == 3) == (i < 2):
                spread_second(u, par, i, j, way)
            share(u, par, i, j)


    def plane_round(u, r):
        if r == 0:
            start, first, second = SUBS[u]
            at = pl.ds(pl.multiple_of((1 - zpar) * QUARTER + start, 16), first + second)
            arrived(mine.at[at], xs.at[u], xr.at[u])
        for par in (0, 1):
            if r == 0:
                spread_first(u, par, 0, 0)
                spread_first(u, par, 0, 1)
                column(u, par, 0)
                start, first, second = SUBS[u]
                r0 = pl.multiple_of(c * HALF + par * QUARTER + start, 16)
                kv[here, pl.ds(r0, first + second), :] = mine[par * QUARTER + start : par * QUARTER + start + first + second, :]
            if r == 1:
                first_arrived(u, par, 3)
                spread_first(u, par, 3, 0, 1)
                column(u, par, 3)
                first_arrived(u, par, 1)
                spread_first(u, par, 1, 1, 0)
                column(u, par, 1)
            if r == 2:
                column_arrived(u, par, 0)
            if r == 3:
                first_arrived(u, par, 2, 0)
                first_arrived(u, par, 2, 1)
                column(u, par, 2)
            if r == 4:
                column_arrived(u, par, 3)
                column_arrived(u, par, 1)
            if r == 5:
                column_arrived(u, par, 2)
            if r == 6:
                for i in (0, 3, 1, 2):
                    second_arrived(u, par, i, 2)
                    share(u, par, i, 2)

    docs = jnp.broadcast_to(seg[...].astype(F32).reshape(1, TOK), (HD, TOK)).T[:, 0:1]
    places = ((me.x * 4 + me.y % 2 * 2 + me.y // 2) * TOK + lax.broadcasted_iota(jnp.int32, (TOK, 1), 0)).astype(F32)
    total[...] = jnp.zeros_like(total)
    mass[...] = jnp.zeros_like(mass)

    def attend_image(u, m):
        start, first, second = SUBS[u]
        n = first + second
        parts = [kv[m, q * QUARTER + start : q * QUARTER + start + n, :] for q in range(4)]
        keys = jnp.concatenate([p[:, :HD] for p in parts], axis=0)
        values = jnp.concatenate([p[:, HD:] for p in parts], axis=0)
        weight = jnp.zeros((2 * TOK, HD), F32)
        rows = qrows[...]
        for k0 in range(0, 4 * n, 256):
            width = min(256, 4 * n - k0)
            score = lax.dot_general(
                rows, keys[k0 : k0 + width, :], (((1,), (1,)), ((), ())), preferred_element_type=F32
            )
            expo = jnp.exp2(score * (HD**-0.5 * 1.4426950408889634))
            if u == 0 and k0 + width > VALID:
                lane = k0 + lax.broadcasted_iota(jnp.int32, expo.shape, 1)
                expo = jnp.where(lane < VALID, expo, 0.0)
            for lanes in range(0, width, HD):
                weight += expo[:, lanes : lanes + HD]
            wexp[:, k0 : k0 + width] = expo.astype(BF16)
        term = jnp.dot(wexp[:, 0 : 4 * n], values, preferred_element_type=F32)
        said = kv[m, META_ROW : META_ROW + 16, 0:HD].astype(F32)[0:1, :] * (1.0 / META)
        lane = lax.broadcasted_iota(jnp.int32, (1, HD), 1)
        doc = jnp.sum(jnp.where(lane == 0, said, 0.0), axis=1, keepdims=True)
        scale = jnp.where(lane == 1, 64.0, jnp.where(lane == 2, 1.0, 0.0))
        mask = (docs == doc) & (places >= jnp.sum(said * scale, axis=1, keepdims=True))
        for h in range(2):
            at = slice(h * TOK, (h + 1) * TOK)
            total[at, :] += jnp.where(mask, term[at], 0.0)
            mass[at, :] += jnp.where(mask, weight[at], 0.0)

    def attend(u, images):
        start, first, second = SUBS[u]
        for dx, dy in images:
            for par, i, j in ((0, dx, dy), (1, dy, dx)):
                r0 = pl.multiple_of((1 - c) * HALF + par * QUARTER + start, 16)
                ref = kv.at[me.image(dx, dy), pl.ds(r0, first + second)]
                arrived(ref, cs.at[u, par, 4 * i + j], cr.at[u, par, 4 * i + j])
        codes = [4 * dx + dy for dx, dy in images]

        def one(n, carry):
            code = codes[0]
            for k in range(1, len(codes)):
                code = jnp.where(n == k, codes[k], code)
            attend_image(u, me.image(code // 4, code % 4))
            return carry

        lax.fori_loop(0, len(codes), one, 0)

    def ring_step(u, stage):
        ring_receive(u, stage)
        if stage < 3:
            ring_send(u, stage + 1)
        else:
            finish(u)

    def order(n):
        return (z + 4 + jnp.where(n % 2 == 1, -((n + 1) // 2), n // 2)) % 8

    def project_next(n, carry):
        project(order(n))
        return carry

    project((z + 4) % 8)
    ring_send(0, 0)
    lax.fori_loop(1, 8, project_next, 0)
    for k in range(8):
        src = wout.at[:, pl.ds(pl.multiple_of((2 * k + 1 - c) * 512, 512), 512)]
        send(src, pwo.at[k], ws.at[k], wr.at[k], me.partner)
        src = wout.at[:, pl.ds(pl.multiple_of((2 * k + c) * 512, 512), 512)]
        load = pltpu.make_async_copy(src, wo.at[k], wo_sem.at[k])
        load.start()
        loads.append(load)

    ring_step(0, 0)
    ring_send(1, 0)
    ring_step(0, 1)
    ring_step(1, 0)
    ring_send(2, 0)
    ring_step(0, 2)
    ring_step(1, 1)
    ring_step(2, 0)
    ring_step(0, 3)
    ring_step(1, 2)
    ring_step(2, 1)
    plane_round(0, 0)
    ring_step(1, 3)
    ring_step(2, 2)
    plane_round(0, 1)
    plane_round(1, 0)
    text_round(1)
    ring_step(2, 3)
    plane_round(0, 2)
    plane_round(0, 3)
    plane_round(2, 0)
    plane_round(0, 4)
    plane_round(0, 5)
    text_round(2)
    plane_round(0, 6)
    plane_round(1, 1)
    text_round(3)
    plane_round(1, 2)
    text_round(4)
    plane_round(1, 3)
    text_compute()
    attend(0, NEAR)
    plane_round(1, 4)
    attend(0, DIAGONAL)
    plane_round(2, 1)
    attend(0, FAR)
    plane_round(1, 5)
    attend(1, NEAR)
    plane_round(2, 2)
    plane_round(1, 6)
    plane_round(2, 3)
    attend(1, DIAGONAL)
    plane_round(2, 4)
    plane_round(2, 5)
    attend(1, FAR)
    attend(2, NEAR)
    attend(2, DIAGONAL)
    plane_round(2, 6)
    attend(2, FAR)

    for h in range(2):
        rows = slice(h * TOK, (h + 1) * TOK)
        weight = jnp.maximum(jnp.sum(mass[rows, :], axis=1, keepdims=True), 1.0)
        att[:, h * HD : (h + 1) * HD] = (total[rows, :] / weight).astype(BF16)

    send(att, patt, es, er, me.partner)

    def term(d):
        part = jnp.dot(att[...], wo[d], preferred_element_type=F32)
        terms[d] = part + jnp.dot(patt[...], pwo[d], preferred_element_type=F32)

    def next_term(n, carry):
        term(order(n))
        return carry

    def term_rows(way, stage):
        return pl.ds(way * 128, 128) if stage == 0 else pl.ds(0, TOK)

    def term_send(e, stage):
        cols = pl.ds(e * 256, 256)
        for way in (0, 1):
            rows = term_rows(way, stage)
            part = terms[(z + (4 - stage if way == 0 else 4 + stage)) % 8, :, cols]
            if stage == 0:
                part = part[way * 128 : way * 128 + 128]
            elif stage == 1:
                parts = [part[:128], part[128:]]
                parts[way] += got[way, 0, way * 128 : way * 128 + 128, cols].astype(F32)
                part = jnp.concatenate(parts, axis=0)
            else:
                part += got[way, stage - 1, :, cols].astype(F32)
            sent[way, stage, rows, cols] = part.astype(BF16)
            send(
                sent.at[way, stage, rows, cols], got.at[way, stage, rows, cols],
                ds.at[e, way, stage], dr.at[e, way, stage], (me.up, me.down)[way],
            )

    def term_arrived(e, stage):
        for way in (0, 1):
            ref = got.at[way, stage, term_rows(way, stage), pl.ds(e * 256, 256)]
            arrived(ref, ds.at[e, way, stage], dr.at[e, way, stage])

    for k in range(8):
        arrived(pwo.at[k], ws.at[k], wr.at[k])
    for load in loads[6:]:
        load.wait()
    arrived(patt, es, er)
    term((z + 4) % 8)
    term_send(0, 0)
    term_send(1, 0)
    lax.fori_loop(1, 8, next_term, 0)
    for stage in range(3):
        for e in (0, 1):
            term_arrived(e, stage)
            term_send(e, stage + 1)
    scale = jnp.tanh(jnp.full((1, 256), gate[0], F32))
    for e in (0, 1):
        term_arrived(e, 3)
        cols = pl.ds(e * 256, 256)
        part = terms[z, :, cols] + got[0, 3, :, cols].astype(F32) + got[1, 3, :, cols].astype(F32)
        out[:, e * 256 : e * 256 + 256] = (scale * part).astype(BF16)

    for copy in sends:
        copy.wait_send()


def fused(*args):
    vmem, anyspace, smem = (pl.BlockSpec(memory_space=m) for m in (pltpu.VMEM, pl.ANY, pltpu.SMEM))
    dma = pltpu.SemaphoreType.DMA
    n = len(SUBS)
    return pl.pallas_call(
        kernel,
        out_shape=jax.ShapeDtypeStruct((TOK, 512), BF16),
        in_specs=[vmem, vmem, vmem, anyspace, anyspace, anyspace, vmem, vmem, smem, smem, smem, vmem, anyspace],
        out_specs=vmem,
        scratch_shapes=[
            pltpu.VMEM((16, TOK, 512), BF16),
            pltpu.VMEM((8192, 256), BF16),
            pltpu.VMEM((TOK, 256), F32),
            pltpu.VMEM((HALF, 512), BF16),
            pltpu.VMEM((HALF, 512), BF16),
            pltpu.VMEM((HALF - BODY, 512), BF16),
            pltpu.VMEM((512, 1024), BF16),
            pltpu.VMEM((512, 1024), BF16),
            pltpu.VMEM((8, QUARTER, HD), F32),
            pltpu.VMEM((8, QUARTER, HD), F32),
            pltpu.VMEM((2, 4, QUARTER, HD), F32),
            pltpu.VMEM((2, 4, QUARTER, HD), BF16),
            pltpu.VMEM((QUARTER, HD), BF16),
            pltpu.VMEM((HALF, 256), BF16),
            pltpu.VMEM((IMAGES, ROWS, 256), BF16),
            pltpu.VMEM((2 * TOK, HD), BF16),
            pltpu.VMEM((2 * TOK, 896), BF16),
            pltpu.VMEM((2 * TOK, HD), F32),
            pltpu.VMEM((2 * TOK, HD), F32),
            pltpu.VMEM((TOK, 256), BF16),
            pltpu.VMEM((TOK, 256), BF16),
            pltpu.VMEM((8, 256, 512), BF16),
            pltpu.VMEM((8, 256, 512), BF16),
            pltpu.VMEM((8, TOK, 512), F32),
            pltpu.VMEM((2, 4, TOK, 512), BF16),
            pltpu.VMEM((2, 4, TOK, 512), BF16),
            dma((7,)),
            dma((3,)),
            dma((3,)),
            dma((n, 2, 4, 2)),
            dma((n, 2, 4, 2)),
            dma((n,)),
            dma((n,)),
            dma((n, 2, 16)),
            dma((n, 2, 16)),
            dma((n, 2, 16)),
            dma((n, 2, 16)),
            dma((2, 4)),
            dma((2, 4)),
            dma((8,)),
            dma((8,)),
            dma((8,)),
            dma((8,)),
            dma((8,)),
            dma,
            dma,
            dma((2, 2, 4)),
            dma((2, 2, 4)),
        ],
        compiler_params=pltpu.CompilerParams(
            collective_id=0, has_side_effects=True, vmem_limit_bytes=60 * 2**20
        ),
        cost_estimate=pl.CostEstimate(flops=2 * 10**10, bytes_accessed=3 * 10**7, transcendentals=13 * 10**6),
    )(*args)


def on_device(
    text, gain, wq, wkv, wout, qgain, kgain, gate, images, seg, owner, pos
):
    return fused(
        text, gain, images[0, IMG_TOK - 1 :], wq, wkv, wout, qgain.reshape(1, -1), kgain.reshape(1, -1),
        gate, owner, pos, seg, images,
    )


def solution(mesh):
    rows = ("seq", "section")
    return jax.shard_map(
        on_device,
        mesh=mesh,
        in_specs=(
            P(rows, "tp"),
            P("tp"),
            P(None, "tp"),
            P("tp", None),
            P("tp", None),
            P(),
            P(),
            P(),
            P(rows, None, "tp"),
            P(rows),
            P(rows),
            P(rows),
        ),
        out_specs=P(rows, "tp"),
        check_vma=False,
    )
```

time: 139 us -> 139 us (level)
  the two profiles are of different devices: /device:TPU:23 before, /device:TPU:1 now
where the time goes in v3:
time: 139 us; the launch traced here: 138 us
  Pallas kernels  133 us (96%)
  local copies, waits for them, and re-layouts  2.95 us (2%)
  between operations  1.95 us (1%)
    pallas_call x1, Pallas kernels, fused(): pl.pallas_call(kernel, out_shape=jax.ShapeDtypeStruct((TOK, 512), BF16),...  133 us

profile of v3, /device:TPU:1, one launch (start us, length us, event | category | flops | bytes accessed | tf_op | source)
XLA Modules:
  0.0 138.3 jit_solution(10484275209992358114)
XLA Ops:
  1.9 1.3 slice_bitcast_fusion.tail
  3.2 133.4 %shard_map.118 = bf16[256,512]{1,0:T(8,128)(2,1)} custom-call(bf16[256,512]{1,0:T(8,128)(2,1)} %text.1, bf16[512]{0:T(512)(128)(2,1)} %gain.1, bf16[1,512]{1,0:T(2,128)(2,1)} %slice_bitcast_fusion.tail, bf16[8192,256]{1,0:T(8,128)(2,1)} %wq.1, bf16[512,1024]{1,0:T(8,128)(2,1)} %wkv.1, bf16[256,8192]{1,0:T(8,128)(2,1)} %wout.1, f32[1,128]{1,0:T(1,128)} %bitcast.4, ...), custom_call_target="tpu_custom_call" | custom-call | flops 20000000000 | bytes 30000000 | tf_op jit(solution)/shard_map/pallas_call | solution.py:542
  136.6 1.7 %copy.17 = bf16[256,512]{1,0:T(8,128)(2,1)} copy(bf16[256,512]{1,0:T(8,128)(2,1)} %shard_map.118) | data formatting | bytes 524288

commit v4 on v3

v4 whole, which is shorter than its diff:
```python
import jax
import jax.numpy as jnp
from jax import lax
from jax.experimental import pallas as pl
from jax.experimental.pallas import tpu as pltpu
from jax.sharding import PartitionSpec as P

MESH = pl.DeviceIdType.MESH
F32, BF16 = jnp.float32, jnp.bfloat16
HD = 128
IMG_TOK = 1601
IMAGES = 16
TOK = 256
QUARTER = 416
BODY = 400
HALF = 2 * QUARTER
EPS = 1e-05
META = 2.0**-40
META_ROW = 408

SUBS = ((224, 48, 48, 48, 48), (0, 64, 48, 64, 48))

EARLY = (('start', 0), ('start', 1))
ORDER = (
    ('text', 1),
    ('ring', 0, 0),
    ('ring', 1, 0),
    ('ring', 0, 1),
    ('ring', 1, 1),
    ('ring', 0, 2),
    ('ring', 1, 2),
    ('text', 2),
    ('ring', 0, 3),
    ('ring', 1, 3),
    ('PF', 0, 0, 3),
    ('PF', 0, 0, 1),
    ('PF', 0, 1, 3),
    ('PF', 0, 1, 1),
    ('PS', 0, 0, 0, 3),
    ('PS', 0, 0, 0, 1),
    ('PS', 0, 1, 0, 3),
    ('PS', 0, 1, 0, 1),
    ('PF', 1, 0, 3),
    ('PF', 1, 0, 1),
    ('PS', 1, 0, 0, 3),
    ('PS', 1, 0, 0, 1),
    ('text', 3),
    ('PF', 1, 1, 3),
    ('PG', 0, 0),
    ('PF', 1, 1, 1),
    ('PS', 0, 0, 3, 3),
    ('PS', 0, 0, 3, 1),
    ('PS', 0, 1, 3, 3),
    ('PS', 0, 1, 3, 1),
    ('PS', 1, 1, 0, 3),
    ('PS', 1, 1, 0, 1),
    ('PS', 0, 0, 1, 3),
    ('PS', 0, 0, 1, 1),
    ('PS', 0, 1, 1, 3),
    ('PS', 0, 1, 1, 1),
    ('PG', 0, 1),
    ('PT', 0, 1, 0),
    ('PT', 0, 0, 0),
    ('PS', 1, 0, 3, 1),
    ('PG', 1, 0),
    ('text', 4),
    ('PS', 1, 1, 3, 1),
    ('PS', 1, 0, 3, 3),
    ('PS', 1, 0, 1, 1),
    ('PS', 1, 1, 3, 3),
    ('PS', 1, 1, 1, 1),
    ('textc',),
    ('PG', 1, 1),
    ('PS', 0, 0, 2, 1),
    ('PS', 0, 1, 2, 1),
    ('PS', 0, 0, 2, 3),
    ('PS', 1, 0, 1, 3),
    ('PS', 1, 1, 1, 3),
    ('PT', 0, 0, 3),
    ('PT', 0, 1, 3),
    ('PS', 0, 1, 2, 3),
    ('PT', 0, 1, 1),
    ('PT', 0, 0, 1),
    ('PT', 1, 0, 0),
    ('PT', 1, 0, 3),
    ('PT', 1, 1, 0),
    ('PT', 1, 1, 3),
    ('PS', 1, 0, 2, 1),
    ('PS', 1, 0, 2, 3),
    ('PS', 1, 1, 2, 3),
    ('PS', 1, 1, 2, 1),
    ('PT', 0, 0, 2),
    ('PT', 1, 0, 1),
    ('q2',),
    ('att', 0, (0, 0), (1, 0), (3, 0), (0, 1), (0, 3)),
    ('PT', 0, 1, 2),
    ('PT', 1, 0, 2),
    ('PT', 1, 1, 1),
    ('PT', 1, 1, 2),
    ('att', 0, (1, 1), (1, 3), (3, 1), (3, 3)),
    ('att', 0, (2, 0), (0, 2), (2, 1), (2, 3), (1, 2), (3, 2), (2, 2)),
    ('att', 1, (0, 0), (1, 0), (3, 0), (0, 1), (0, 3)),
    ('att', 1, (1, 1), (1, 3), (3, 1), (3, 3)),
    ('att', 1, (2, 0), (0, 2), (2, 1), (2, 3), (1, 2), (3, 2), (2, 2)),
)


def remote(src, dst, send, recv, device):
    return pltpu.make_async_remote_copy(
        src_ref=src, dst_ref=dst, send_sem=send, recv_sem=recv, device_id=device, device_id_type=MESH
    )


class Place:
    def __init__(self):
        seq, tp, sec = lax.axis_index("seq"), lax.axis_index("tp"), lax.axis_index("section")
        self.tp, self.z, self.c = tp, tp // 2, tp % 2
        self.x, self.y = seq // 2, sec * 2 + seq % 2
        self.partner = {"tp": self.z * 2 + 1 - self.c}
        self.up = {"tp": ((self.z + 1) % 8) * 2 + self.c}
        self.down = {"tp": ((self.z + 7) % 8) * 2 + self.c}

    def step(self, axis, delta):
        if axis == "x":
            return {"seq": ((self.x + delta) % 4) * 2 + self.y % 2}
        y = (self.y + delta) % 4
        return {"seq": self.x * 2 + y % 2, "section": y // 2}

    def image(self, dx, dy):
        y = (self.y + dy) % 4
        return ((self.x + dx) % 4) * 4 + (y % 2) * 2 + y // 2


def greet(devices):
    barrier = pltpu.get_barrier_semaphore()
    for device in devices:
        pl.semaphore_signal(barrier, inc=1, device_id=device, device_id_type=MESH)
    pl.semaphore_wait(barrier, len(devices))


def kernel(
    text, gain, tail, wq, wkv, wout, qgain, kgain, gate, owner, pos, seg, img,
    out,
    nall, wqv, qacc, imgv, pimg, tailv, wkvv, pwkv, acck, accv, rk, rv, vfirst,
    kv, qrows, total, mass, half, theirs, mhalf, mtheirs, att, patt, wo, pwo, terms, got, sent,
    load_sem, ex_send, ex_recv, bs, br, ps, pr, cs, cr, as_, ar, acs, acr, ws, wr,
    wo_sem, es, er, ds, dr, qs, qr, ts, tr,
):
    me = Place()
    z, c = me.z, me.c
    zpar = z % 2
    loads = [pltpu.make_async_copy(wkv, wkvv, load_sem.at[0])]
    for k in range(2):
        src = img.at[0, pl.ds(pl.multiple_of(c * 2 * BODY + k * BODY, 16), BODY)]
        loads.append(pltpu.make_async_copy(src, imgv.at[pl.ds(k * QUARTER, BODY)], load_sem.at[1 + k]))
    for k in range(4):
        part = pl.ds(k * 2048, 2048)
        loads.append(pltpu.make_async_copy(wq.at[part], wqv.at[part], load_sem.at[3 + k]))
    for load in loads[:3]:
        load.start()

    row = lax.broadcasted_iota(jnp.int32, (16, 512), 0)
    last = tail[...].astype(F32)
    tailv[...] = jnp.where(row == 16 * c, last, 0.0).astype(BF16)
    imgv[BODY:QUARTER, :] = jnp.zeros((16, 512), BF16)
    pimg[BODY:QUARTER, :] = jnp.zeros((16, 512), BF16)
    imgv[QUARTER + BODY :, :] = jnp.where(row == 16 * (1 - c), last, 0.0).astype(BF16)

    nall[me.tp] = (text[...].astype(F32) * gain[...].astype(F32).reshape(1, 512)).astype(BF16)
    for load in loads[3:7]:
        load.start()

    greet([me.partner, me.up, me.down] + [me.step(a, d) for a in "xy" for d in (1, 3)])
    sends = []

    def send(src, dst, ssem, rsem, device):
        copy = remote(src, dst, ssem, rsem, device)
        copy.start()
        sends.append(copy)

    def arrived(ref, ssem, rsem):
        remote(ref, ref, ssem, rsem, me.partner).wait_recv()

    send(wkv, pwkv, ex_send.at[0], ex_recv.at[0], me.partner)
    for k in range(2):
        src = img.at[0, pl.ds(pl.multiple_of((1 - c) * 2 * BODY + k * BODY, 16), BODY)]
        send(src, pimg.at[pl.ds(k * QUARTER, BODY)], ex_send.at[1 + k], ex_recv.at[1 + k], me.partner)
    end = pimg.at[pl.ds(QUARTER + BODY, 16)]
    send(tailv, end, ex_send.at[3], ex_recv.at[3], me.partner)

    shard = lambda k: ((z + k % 8) % 8) * 2 + c

    def text_send(k, way, hop):
        ref = nall.at[shard(k)]
        if hop == 4:
            ref = ref.at[pl.ds(way * 128, 128)]
        send(ref, ref, as_.at[way, hop - 1], ar.at[way, hop - 1], (me.up, me.down)[way])

    def text_share(k):
        ref = nall.at[shard(k)]
        send(ref, ref, acs.at[k % 8], acr.at[k % 8], me.partner)

    def text_arrived(hop, way):
        k = -hop if way == 0 else hop
        ref = nall.at[shard(k)]
        if hop == 4:
            ref = ref.at[pl.ds(way * 128, 128)]
        arrived(ref, as_.at[way, hop - 1], ar.at[way, hop - 1])

    def text_round(hop):
        for way in (0, 1):
            text_arrived(hop, way)
            if hop < 4:
                k = -hop if way == 0 else hop
                text_send(k, way, hop + 1)
                text_share(k)
        if hop == 4:
            text_share(4)

    def text_compute():
        for k in range(8):
            ref = nall.at[((z + k) % 8) * 2 + 1 - c]
            arrived(ref, acs.at[k], acr.at[k])
        for load in loads[3:7]:
            load.wait()
        qacc[...] = jnp.zeros_like(qacc)

        def use(index, carry):
            w = wqv[pl.ds(pl.multiple_of(index * 512, 512), 512), :]
            qacc[...] += jnp.dot(nall[index], w, preferred_element_type=F32)
            return carry

        lax.fori_loop(0, 16, use, 0)
        for h in range(2):
            q = qacc[:, h * HD : (h + 1) * HD]
            q = q * lax.rsqrt(jnp.mean(q * q, axis=-1, keepdims=True) + EPS) * qgain[...]
            qrows[h * TOK : (h + 1) * TOK, :] = q.astype(BF16)

    text_send(0, 0, 1)
    text_send(0, 1, 1)
    text_share(0)

    def order(n):
        return (z + 4 + jnp.where(n % 2 == 1, -((n + 1) // 2), n // 2)) % 8

    def project(d):
        rows = pl.ds(pl.multiple_of((d % 2) * QUARTER, QUARTER), QUARTER)
        cols = pl.ds(pl.multiple_of((d // 2) * 256, 256), 256)
        part = jnp.dot(imgv[rows, :], wkvv[:, cols], preferred_element_type=F32)
        part += jnp.dot(pimg[rows, :], pwkv[:, cols], preferred_element_type=F32)
        acck[d] = part[:, :HD]
        accv[d] = part[:, HD:]

    def project_next(n, carry):
        project(order(n))
        return carry

    def piece(u, par, part=None):
        start, *sizes = SUBS[u]
        start += par * (sizes[0] + sizes[1])
        pair = sizes[2 * par : 2 * par + 2]
        if part is None:
            return start, pair[0] + pair[1]
        return start + part * pair[0], pair[part]

    def ring_rows(u, way, stage):
        if stage == 0:
            return pl.ds(*piece(u, way))
        return pl.ds(SUBS[u][0], sum(SUBS[u][1:]))

    def ring_send(u, stage):
        for way in (0, 1):
            rows = ring_rows(u, way, stage)
            if stage == 0:
                d = (z + 4) % 8
                vfirst[rows, :] = accv[d, rows, :].astype(BF16)
                srck, srcv = acck.at[d, rows], vfirst.at[rows]
            else:
                srck, srcv = rk.at[way, stage - 1, rows], rv.at[way, stage - 1, rows]
            device = (me.up, me.down)[way]
            send(srck, rk.at[way, stage, rows], bs.at[u, way, stage, 0], br.at[u, way, stage, 0], device)
            send(srcv, rv.at[way, stage, rows], bs.at[u, way, stage, 1], br.at[u, way, stage, 1], device)

    def ring_receive(u, stage):
        for way in (0, 1):
            rows = ring_rows(u, way, stage)
            d = (z + (3 - stage if way == 0 else 5 + stage)) % 8
            if stage == 0:
                other = ring_rows(u, 1 - way, 0)
                rk[way, 0, other, :] = acck[d, other, :]
                rv[way, 0, other, :] = accv[d, other, :].astype(BF16)
            arrived(rk.at[way, stage, rows], bs.at[u, way, stage, 0], br.at[u, way, stage, 0])
            arrived(rv.at[way, stage, rows], bs.at[u, way, stage, 1], br.at[u, way, stage, 1])
            if stage < 3:
                rk[way, stage, rows, :] += acck[d, rows, :]
                rv[way, stage, rows, :] = (rv[way, stage, rows, :].astype(F32) + accv[d, rows, :]).astype(BF16)

    here = me.image(0, 0)
    here_rows = lambda start, n: pl.ds(pl.multiple_of(c * QUARTER + start, 16), n)

    def finish(u):
        start, n = SUBS[u][0], sum(SUBS[u][1:])
        rows = pl.ds(start, n)
        key = rk[0, 3, rows, :] + rk[1, 3, rows, :] + acck[z, rows, :]
        val = rv[0, 3, rows, :].astype(F32) + rv[1, 3, rows, :].astype(F32) + accv[z, rows, :]
        key = key * lax.rsqrt(jnp.mean(key * key, axis=-1, keepdims=True) + EPS) * kgain[...]
        if start + n == QUARTER:
            row = start + lax.broadcasted_iota(jnp.int32, (n, HD), 0)
            lane = lax.broadcasted_iota(jnp.int32, (n, HD), 1)
            said = jnp.where(lane == 0, owner[0], jnp.where(lane == 1, pos[0] // 64, pos[0] % 64))
            said = jnp.where(lane < 3, said, 0).astype(F32) * META
            key = jnp.where(row >= META_ROW, said, key)
        kv[here, here_rows(start, n), 0:HD] = key.astype(BF16)
        kv[here, here_rows(start, n), HD:] = val.astype(BF16)


    def block(u, par, i, j, part=None):
        m = me.image(i, j) if par == 0 else me.image(j, i)
        return kv.at[m, here_rows(*piece(u, par, part))]

    axes = lambda par: ("x", "y") if par == 0 else ("y", "x")

    def spread_first(u, par, i, way, part=None):
        slot = {(0, 0): 0, (0, 1): 1, (3, 0): 2, (1, 1): 3}[(i, way)]
        ref = block(u, par, i, 0, part)
        send(ref, ref, ps.at[u, par, slot], pr.at[u, par, slot], me.step(axes(par)[0], (1, 3)[way]))

    def first_arrived(u, par, i, part=None):
        slot = {(3, None): 0, (1, None): 1, (2, 1): 2, (2, 0): 3}[(i, part)]
        arrived(block(u, par, i, 0, part), ps.at[u, par, slot], pr.at[u, par, slot])

    def spread_second(u, par, i, j, way):
        slot = 4 + 3 * i + (way if j == 0 else 2)
        ref = block(u, par, i, j)
        send(ref, ref, ps.at[u, par, slot], pr.at[u, par, slot], me.step(axes(par)[1], (1, 3)[way]))

    def second_arrived(u, par, i, j):
        slot = 4 + 3 * i + {3: 0, 1: 1, 2: 2}[j]
        arrived(block(u, par, i, j), ps.at[u, par, slot], pr.at[u, par, slot])

    def share(u, par, i, j):
        ref = block(u, par, i, j)
        send(ref, ref, cs.at[u, par, 4 * i + j], cr.at[u, par, 4 * i + j], me.partner)

    def column(u, par, i):
        spread_second(u, par, i, 0, 0)
        spread_second(u, par, i, 0, 1)
        share(u, par, i, 0)

    def spread_start(u):
        for par in (0, 1):
            spread_first(u, par, 0, 0)
            spread_first(u, par, 0, 1)
            column(u, par, 0)

    def spread_first_on(u, par, i):
        first_arrived(u, par, i)
        spread_first(u, par, i, 0 if i == 3 else 1, 1 if i == 3 else 0)
        column(u, par, i)

    def spread_opposite(u, par):
        first_arrived(u, par, 2, 0)
        first_arrived(u, par, 2, 1)
        column(u, par, 2)

    def spread_second_on(u, par, i, j):
        second_arrived(u, par, i, j)
        if (j == 3) == (i < 2):
            spread_second(u, par, i, j, 0 if j == 3 else 1)
        share(u, par, i, j)

    def spread_end(u, par, i):
        second_arrived(u, par, i, 2)
        share(u, par, i, 2)

    docs = jnp.broadcast_to(seg[...].astype(F32).reshape(1, TOK), (HD, TOK)).T[:, 0:1]
    places = ((me.x * 4 + me.y % 2 * 2 + me.y // 2) * TOK + lax.broadcasted_iota(jnp.int32, (TOK, 1), 0)).astype(F32)
    total[...] = jnp.zeros_like(total)
    mass[...] = jnp.zeros_like(mass)

    def attend_image(u, m):
        start, n = SUBS[u][0], sum(SUBS[u][1:])
        parts = [kv[m, q * QUARTER + start : q * QUARTER + start + n, :] for q in range(2)]
        both = jnp.concatenate(parts, axis=0)
        keys, values = both[:, :HD], both[:, HD:]
        said = kv[m, QUARTER - 16 : QUARTER, 0:HD].astype(F32)[15:16, :] * (1.0 / META)
        lane = lax.broadcasted_iota(jnp.int32, (1, HD), 1)
        doc = jnp.sum(jnp.where(lane == 0, said, 0.0), axis=1, keepdims=True)
        scale = jnp.where(lane == 1, 64.0, jnp.where(lane == 2, 1.0, 0.0))
        mask = (docs == doc) & (places >= jnp.sum(said * scale, axis=1, keepdims=True))
        for h in range(4):
            at = slice(h * TOK, (h + 1) * TOK)
            rows = qrows[at, :]
            weight = jnp.zeros((TOK, HD), F32)
            term = jnp.zeros((TOK, HD), F32)
            for k0 in range(0, 2 * n, 256):
                width = min(256, 2 * n - k0)
                score = lax.dot_general(
                    rows, keys[k0 : k0 + width, :], (((1,), (1,)), ((), ())), preferred_element_type=F32
                )
                expo = jnp.exp2(score * (HD**-0.5 * 1.4426950408889634))
                if start + n == QUARTER:
                    lane = k0 + lax.broadcasted_iota(jnp.int32, expo.shape, 1)
                    good = (lane < BODY - start) | ((lane >= n) & (lane < n + BODY - start + zpar))
                    expo = jnp.where(good, expo, 0.0)
                for lanes in range(0, width, HD):
                    some = expo[:, lanes : min(lanes + HD, width)]
                    if some.shape[1] < HD:
                        some = jnp.concatenate([some, jnp.zeros((TOK, HD - some.shape[1]), F32)], axis=1)
                    weight += some
                term += jnp.dot(expo.astype(BF16), values[k0 : k0 + width, :], preferred_element_type=F32)
            total[at, :] += jnp.where(mask, term, 0.0)
            mass[at, :] += jnp.where(mask, weight, 0.0)

    def attend(u, images):
        for dx, dy in images:
            for par, i, j in ((0, dx, dy), (1, dy, dx)):
                start, n = piece(u, par)
                ref = kv.at[me.image(dx, dy), pl.ds(pl.multiple_of((1 - c) * QUARTER + start, 16), n)]
                arrived(ref, cs.at[u, par, 4 * i + j], cr.at[u, par, 4 * i + j])
        codes = [4 * dx + dy for dx, dy in images]

        def one(n, carry):
            code = codes[0]
            for k in range(1, len(codes)):
                code = jnp.where(n == k, codes[k], code)
            attend_image(u, me.image(code // 4, code % 4))
            return carry

        lax.fori_loop(0, len(codes), one, 0)

    def ring_step(u, stage):
        ring_receive(u, stage)
        if stage < 3:
            ring_send(u, stage + 1)
        else:
            finish(u)
            spread_start(u)

    pair = {"tp": (z + 1 - 2 * zpar) * 2 + c}
    own_rows, pair_rows = pl.ds(0, 2 * TOK), pl.ds(2 * TOK, 2 * TOK)

    def queries_swap():
        text_compute()
        send(qrows.at[own_rows], qrows.at[pair_rows], qs, qr, pair)

    def queries_arrived():
        arrived(qrows.at[pair_rows], qs, qr)

    handlers = {
        "start": lambda u: ring_send(u, 0),
        "ring": ring_step,
        "PF": spread_first_on,
        "PG": spread_opposite,
        "PS": spread_second_on,
        "PT": spread_end,
        "text": text_round,
        "textc": queries_swap,
        "q2": queries_arrived,
        "att": lambda u, *images: attend(u, images),
    }

    for load in loads[:3]:
        load.wait()
    arrived(pwkv, ex_send.at[0], ex_recv.at[0])
    for k in range(2):
        arrived(pimg.at[pl.ds(k * QUARTER, BODY)], ex_send.at[1 + k], ex_recv.at[1 + k])
    arrived(end, ex_send.at[3], ex_recv.at[3])
    project((z + 4) % 8)
    for name, *args in EARLY:
        handlers[name](*args)
    lax.fori_loop(1, 8, project_next, 0)
    for k in range(8):
        src = wout.at[:, pl.ds(pl.multiple_of((2 * k + 1 - c) * 512, 512), 512)]
        send(src, pwo.at[k], ws.at[k], wr.at[k], me.partner)
        src = wout.at[:, pl.ds(pl.multiple_of((2 * k + c) * 512, 512), 512)]
        load = pltpu.make_async_copy(src, wo.at[k], wo_sem.at[k])
        load.start()
        loads.append(load)
    for name, *args in ORDER:
        handlers[name](*args)

    half[...] = total[pair_rows, :].astype(BF16)
    send(half, theirs, ts.at[0], tr.at[0], pair)
    weight = jnp.sum(mass[pair_rows, :], axis=1, keepdims=True)
    mhalf[...] = jnp.broadcast_to(weight, (2 * TOK, HD)).T[0:8, :]
    send(mhalf, mtheirs, ts.at[1], tr.at[1], pair)
    arrived(mtheirs, ts.at[1], tr.at[1])
    arrived(theirs, ts.at[0], tr.at[0])
    others = jnp.broadcast_to(mtheirs[0:1, :], (HD, 2 * TOK)).T

    for h in range(2):
        rows = slice(h * TOK, (h + 1) * TOK)
        weight = jnp.maximum(jnp.sum(mass[rows, :], axis=1, keepdims=True) + others[rows], 1.0)
        att[:, h * HD : (h + 1) * HD] = ((total[rows, :] + theirs[rows, :].astype(F32)) / weight).astype(BF16)

    send(att, patt, es, er, me.partner)

    def term(d):
        part = jnp.dot(att[...], wo[d], preferred_element_type=F32)
        terms[d] = part + jnp.dot(patt[...], pwo[d], preferred_element_type=F32)

    def next_term(n, carry):
        term(order(n))
        return carry

    def term_rows(way, stage):
        return pl.ds(way * 128, 128) if stage == 0 else pl.ds(0, TOK)

    def term_send(e, stage):
        cols = pl.ds(e * 256, 256)
        for way in (0, 1):
            rows = term_rows(way, stage)
            part = terms[(z + (4 - stage if way == 0 else 4 + stage)) % 8, :, cols]
            if stage == 0:
                part = part[way * 128 : way * 128 + 128]
            elif stage == 1:
                parts = [part[:128], part[128:]]
                parts[way] += got[way, 0, way * 128 : way * 128 + 128, cols].astype(F32)
                part = jnp.concatenate(parts, axis=0)
            else:
                part += got[way, stage - 1, :, cols].astype(F32)
            sent[way, stage, rows, cols] = part.astype(BF16)
            send(
                sent.at[way, stage, rows, cols], got.at[way, stage, rows, cols],
                ds.at[e, way, stage], dr.at[e, way, stage], (me.up, me.down)[way],
            )

    def term_arrived(e, stage):
        for way in (0, 1):
            ref = got.at[way, stage, term_rows(way, stage), pl.ds(e * 256, 256)]
            arrived(ref, ds.at[e, way, stage], dr.at[e, way, stage])

    for k in range(8):
        arrived(pwo.at[k], ws.at[k], wr.at[k])
    for load in loads[7:]:
        load.wait()
    arrived(patt, es, er)
    term((z + 4) % 8)
    term_send(0, 0)
    term_send(1, 0)
    lax.fori_loop(1, 8, next_term, 0)
    for stage in range(3):
        for e in (0, 1):
            term_arrived(e, stage)
            term_send(e, stage + 1)
    scale = jnp.tanh(jnp.full((1, 256), gate[0], F32))
    for e in (0, 1):
        term_arrived(e, 3)
        cols = pl.ds(e * 256, 256)
        part = terms[z, :, cols] + got[0, 3, :, cols].astype(F32) + got[1, 3, :, cols].astype(F32)
        out[:, e * 256 : e * 256 + 256] = (scale * part).astype(BF16)

    for copy in sends:
        copy.wait_send()


def fused(*args):
    vmem, anyspace, smem = (pl.BlockSpec(memory_space=m) for m in (pltpu.VMEM, pl.ANY, pltpu.SMEM))
    dma = pltpu.SemaphoreType.DMA
    n = len(SUBS)
    return pl.pallas_call(
        kernel,
        out_shape=jax.ShapeDtypeStruct((TOK, 512), BF16),
        in_specs=[vmem, vmem, vmem, anyspace, anyspace, anyspace, vmem, vmem, smem, smem, smem, vmem, anyspace],
        out_specs=vmem,
        scratch_shapes=[
            pltpu.VMEM((16, TOK, 512), BF16),
            pltpu.VMEM((8192, 256), BF16),
            pltpu.VMEM((TOK, 256), F32),
            pltpu.VMEM((HALF, 512), BF16),
            pltpu.VMEM((HALF, 512), BF16),
            pltpu.VMEM((16, 512), BF16),
            pltpu.VMEM((512, 1024), BF16),
            pltpu.VMEM((512, 1024), BF16),
            pltpu.VMEM((8, QUARTER, HD), F32),
            pltpu.VMEM((8, QUARTER, HD), F32),
            pltpu.VMEM((2, 4, QUARTER, HD), F32),
            pltpu.VMEM((2, 4, QUARTER, HD), BF16),
            pltpu.VMEM((QUARTER, HD), BF16),
            pltpu.VMEM((IMAGES, HALF, 256), BF16),
            pltpu.VMEM((4 * TOK, HD), BF16),
            pltpu.VMEM((4 * TOK, HD), F32),
            pltpu.VMEM((4 * TOK, HD), F32),
            pltpu.VMEM((2 * TOK, HD), BF16),
            pltpu.VMEM((2 * TOK, HD), BF16),
            pltpu.VMEM((8, 2 * TOK), F32),
            pltpu.VMEM((8, 2 * TOK), F32),
            pltpu.VMEM((TOK, 256), BF16),
            pltpu.VMEM((TOK, 256), BF16),
            pltpu.VMEM((8, 256, 512), BF16),
            pltpu.VMEM((8, 256, 512), BF16),
            pltpu.VMEM((8, TOK, 512), F32),
            pltpu.VMEM((2, 4, TOK, 512), BF16),
            pltpu.VMEM((2, 4, TOK, 512), BF16),
            dma((7,)),
            dma((4,)),
            dma((4,)),
            dma((n, 2, 4, 2)),
            dma((n, 2, 4, 2)),
            dma((n, 2, 16)),
            dma((n, 2, 16)),
            dma((n, 2, 16)),
            dma((n, 2, 16)),
            dma((2, 4)),
            dma((2, 4)),
            dma((8,)),
            dma((8,)),
            dma((8,)),
            dma((8,)),
            dma((8,)),
            dma,
            dma,
            dma((2, 2, 4)),
            dma((2, 2, 4)),
            dma,
            dma,
            dma((2,)),
            dma((2,)),
        ],
        compiler_params=pltpu.CompilerParams(
            collective_id=0, has_side_effects=True, vmem_limit_bytes=60 * 2**20
        ),
        cost_estimate=pl.CostEstimate(flops=2 * 10**10, bytes_accessed=3 * 10**7, transcendentals=13 * 10**6),
    )(*args)


def on_device(
    text, gain, wq, wkv, wout, qgain, kgain, gate, images, seg, owner, pos
):
    return fused(
        text, gain, images[0, IMG_TOK - 1 :], wq, wkv, wout, qgain.reshape(1, -1), kgain.reshape(1, -1),
        gate, owner, pos, seg, images,
    )


def solution(mesh):
    rows = ("seq", "section")
    return jax.shard_map(
        on_device,
        mesh=mesh,
        in_specs=(
            P(rows, "tp"),
            P("tp"),
            P(None, "tp"),
            P("tp", None),
            P("tp", None),
            P(),
            P(),
            P(),
            P(rows, None, "tp"),
            P(rows),
            P(rows),
            P(rows),
        ),
        out_specs=P(rows, "tp"),
        check_vma=False,
    )
```

time: 139 us -> 141 us (1.014)
  Pallas kernels: 133 us -> 136 us
    pallas_call x1, Pallas kernels: 133 us -> 136 us  [fused(): pl.pallas_call(kernel, out_shape=jax.ShapeDtypeStruct((TOK, 512), BF16),...]
where the time goes in v4:
time: 141 us
  Pallas kernels  136 us (96%)
  local copies, waits for them, and re-layouts  2.95 us (2%)
  between operations  1.95 us (1%)
    pallas_call x1, Pallas kernels, fused(): pl.pallas_call(kernel, out_shape=jax.ShapeDtypeStruct((TOK, 512), BF16),...  136 us

profile of v4, /device:TPU:1, one launch (start us, length us, event | category | flops | bytes accessed | tf_op | source)
XLA Modules:
  0.0 140.6 jit_solution(10318112056874274960)
XLA Ops:
  1.9 1.3 slice_bitcast_fusion.tail
  3.2 135.7 %shard_map.118 = bf16[256,512]{1,0:T(8,128)(2,1)} custom-call(bf16[256,512]{1,0:T(8,128)(2,1)} %text.1, bf16[512]{0:T(512)(128)(2,1)} %gain.1, bf16[1,512]{1,0:T(2,128)(2,1)} %slice_bitcast_fusion.tail, bf16[8192,256]{1,0:T(8,128)(2,1)} %wq.1, bf16[512,1024]{1,0:T(8,128)(2,1)} %wkv.1, bf16[256,8192]{1,0:T(8,128)(2,1)} %wout.1, f32[1,128]{1,0:T(1,128)} %bitcast.4, ...), custom_call_target="tpu_custom_call" | custom-call | flops 20000000000 | bytes 30000000 | tf_op jit(solution)/shard_map/pallas_call | solution.py:562
  138.9 1.7 %copy.17 = bf16[256,512]{1,0:T(8,128)(2,1)} copy(bf16[256,512]{1,0:T(8,128)(2,1)} %shard_map.118) | data formatting | bytes 524288

commit v5 on v4

--- a/solution.py
+++ b/solution.py
@@ -15,8 +15,7 @@
 BODY = 400
 HALF = 2 * QUARTER
 EPS = 1e-05
-META = 2.0**-40
-META_ROW = 408
+HIDDEN = -30000.0
 
 SUBS = ((224, 48, 48, 48, 48), (0, 64, 48, 64, 48))
 
@@ -24,84 +23,86 @@
 ORDER = (
     ('text', 1),
     ('ring', 0, 0),
+    ('text', 2),
     ('ring', 1, 0),
     ('ring', 0, 1),
+    ('text', 3),
     ('ring', 1, 1),
     ('ring', 0, 2),
+    ('text', 4),
+    ('textc',),
     ('ring', 1, 2),
-    ('text', 2),
     ('ring', 0, 3),
-    ('ring', 1, 3),
+    ('q2',),
     ('PF', 0, 0, 3),
     ('PF', 0, 0, 1),
-    ('PF', 0, 1, 3),
-    ('PF', 0, 1, 1),
     ('PS', 0, 0, 0, 3),
     ('PS', 0, 0, 0, 1),
     ('PS', 0, 1, 0, 3),
+    ('PF', 0, 1, 3),
+    ('PF', 0, 1, 1),
     ('PS', 0, 1, 0, 1),
-    ('PF', 1, 0, 3),
+    ('ring', 1, 3),
+    ('PG', 0, 0),
+    ('PS', 0, 0, 3, 3),
+    ('PS', 0, 0, 3, 1),
+    ('att', 0, (0, 0), (1, 0), (3, 0), (0, 1)),
+    ('PS', 0, 0, 1, 3),
+    ('PS', 0, 0, 1, 1),
+    ('PS', 0, 1, 3, 3),
+    ('PG', 0, 1),
+    ('PS', 0, 1, 3, 1),
+    ('PS', 0, 1, 1, 3),
+    ('PS', 0, 1, 1, 1),
+    ('PS', 1, 0, 0, 1),
+    ('PT', 0, 0, 0),
     ('PF', 1, 0, 1),
     ('PS', 1, 0, 0, 3),
-    ('PS', 1, 0, 0, 1),
-    ('text', 3),
+    ('PF', 1, 1, 1),
+    ('PF', 1, 0, 3),
+    ('PS', 1, 1, 0, 1),
     ('PF', 1, 1, 3),
-    ('PG', 0, 0),
-    ('PF', 1, 1, 1),
-    ('PS', 0, 0, 3, 3),
-    ('PS', 0, 0, 3, 1),
-    ('PS', 0, 1, 3, 3),
-    ('PS', 0, 1, 3, 1),
+    ('PS', 0, 0, 2, 1),
     ('PS', 1, 1, 0, 3),
-    ('PS', 1, 1, 0, 1),
-    ('PS', 0, 0, 1, 3),
-    ('PS', 0, 0, 1, 1),
-    ('PS', 0, 1, 1, 3),
-    ('PS', 0, 1, 1, 1),
-    ('PG', 0, 1),
     ('PT', 0, 1, 0),
-    ('PT', 0, 0, 0),
-    ('PS', 1, 0, 3, 1),
-    ('PG', 1, 0),
-    ('text', 4),
-    ('PS', 1, 1, 3, 1),
-    ('PS', 1, 0, 3, 3),
+    ('att', 0, (0, 3), (1, 1), (1, 3), (3, 1)),
+    ('PS', 0, 0, 2, 3),
+    ('PS', 0, 1, 2, 3),
+    ('PS', 0, 1, 2, 1),
     ('PS', 1, 0, 1, 1),
-    ('PS', 1, 1, 3, 3),
-    ('PS', 1, 1, 1, 1),
-    ('textc',),
-    ('PG', 1, 1),
-    ('PS', 0, 0, 2, 1),
-    ('PS', 0, 1, 2, 1),
-    ('PS', 0, 0, 2, 3),
+    ('PT', 0, 0, 3),
+    ('PT', 0, 0, 1),
+    ('PT', 0, 1, 3),
+    ('PT', 0, 1, 1),
     ('PS', 1, 0, 1, 3),
     ('PS', 1, 1, 1, 3),
-    ('PT', 0, 0, 3),
-    ('PT', 0, 1, 3),
-    ('PS', 0, 1, 2, 3),
-    ('PT', 0, 1, 1),
-    ('PT', 0, 0, 1),
+    ('PS', 1, 1, 1, 1),
+    ('PG', 1, 0),
+    ('PS', 1, 0, 3, 1),
     ('PT', 1, 0, 0),
-    ('PT', 1, 0, 3),
+    ('att', 0, (3, 3), (2, 0), (0, 2), (2, 1)),
+    ('PG', 1, 1),
+    ('PS', 1, 0, 3, 3),
+    ('PS', 1, 1, 3, 3),
+    ('PS', 1, 1, 3, 1),
+    ('PT', 0, 0, 2),
+    ('PT', 0, 1, 2),
     ('PT', 1, 1, 0),
-    ('PT', 1, 1, 3),
+    ('PT', 1, 0, 1),
     ('PS', 1, 0, 2, 1),
+    ('PT', 1, 1, 1),
+    ('att', 0, (2, 3), (1, 2), (3, 2), (2, 2)),
     ('PS', 1, 0, 2, 3),
     ('PS', 1, 1, 2, 3),
     ('PS', 1, 1, 2, 1),
-    ('PT', 0, 0, 2),
-    ('PT', 1, 0, 1),
-    ('q2',),
-    ('att', 0, (0, 0), (1, 0), (3, 0), (0, 1), (0, 3)),
-    ('PT', 0, 1, 2),
+    ('PT', 1, 0, 3),
+    ('att', 1, (0, 0), (1, 0), (3, 0), (0, 1)),
     ('PT', 1, 0, 2),
-    ('PT', 1, 1, 1),
+    ('PT', 1, 1, 3),
+    ('att', 1, (0, 3), (1, 1), (1, 3), (3, 1)),
     ('PT', 1, 1, 2),
-    ('att', 0, (1, 1), (1, 3), (3, 1), (3, 3)),
-    ('att', 0, (2, 0), (0, 2), (2, 1), (2, 3), (1, 2), (3, 2), (2, 2)),
-    ('att', 1, (0, 0), (1, 0), (3, 0), (0, 1), (0, 3)),
-    ('att', 1, (1, 1), (1, 3), (3, 1), (3, 3)),
-    ('att', 1, (2, 0), (0, 2), (2, 1), (2, 3), (1, 2), (3, 2), (2, 2)),
+    ('att', 1, (3, 3), (2, 0), (0, 2), (2, 1)),
+    ('att', 1, (2, 3), (1, 2), (3, 2), (2, 2)),
 )
 
 
@@ -126,6 +127,10 @@
         y = (self.y + delta) % 4
         return {"seq": self.x * 2 + y % 2, "section": y // 2}
 
+    def plane(self, dx, dy):
+        y = (self.y + dy) % 4
+        return {"seq": ((self.x + dx) % 4) * 2 + y % 2, "section": y // 2}
+
     def image(self, dx, dy):
         y = (self.y + dy) % 4
         return ((self.x + dx) % 4) * 4 + (y % 2) * 2 + y // 2
@@ -142,9 +147,9 @@
     text, gain, tail, wq, wkv, wout, qgain, kgain, gate, owner, pos, seg, img,
     out,
     nall, wqv, qacc, imgv, pimg, tailv, wkvv, pwkv, acck, accv, rk, rv, vfirst,
-    kv, qrows, total, mass, half, theirs, mhalf, mtheirs, att, patt, wo, pwo, terms, got, sent,
+    kv, qrows, wexp, total, metas, half, theirs, mhalf, mtheirs, att, patt, wo, pwo, terms, got, sent,
     load_sem, ex_send, ex_recv, bs, br, ps, pr, cs, cr, as_, ar, acs, acr, ws, wr,
-    wo_sem, es, er, ds, dr, qs, qr, ts, tr,
+    wo_sem, es, er, ds, dr, qs, qr, ts, tr, ms, mr,
 ):
     me = Place()
     z, c = me.z, me.c
@@ -170,7 +175,25 @@
     for load in loads[3:7]:
         load.start()
 
-    greet([me.partner, me.up, me.down] + [me.step(a, d) for a in "xy" for d in (1, 3)])
+    here = me.image(0, 0)
+    row = lax.broadcasted_iota(jnp.int32, (8, HD), 0)
+    lane = lax.broadcasted_iota(jnp.int32, (8, HD), 1)
+    said = jnp.where(row == 0, owner[0], jnp.where(row == 1, pos[0], 0))
+    metas[here] = jnp.where(lane == here, said, 0).astype(F32)
+    row = lax.broadcasted_iota(jnp.int32, (QUARTER, HD), 0)
+    lane = lax.broadcasted_iota(jnp.int32, (QUARTER, HD), 1)
+    for q in range(2):
+        padding = (lane == IMAGES) & (row >= BODY + zpar * q)
+
+        def name_rows(m, carry):
+            kv[m, q * QUARTER : (q + 1) * QUARTER, 0:HD] = jnp.where((lane == m) | padding, 1.0, 0.0).astype(BF16)
+            kv[m, q * QUARTER : (q + 1) * QUARTER, 3 * HD :] = jnp.ones((QUARTER, HD), BF16)
+            return carry
+
+        lax.fori_loop(0, IMAGES, name_rows, 0)
+
+    across = [(dx, dy) for dx in range(4) for dy in range(4) if (dx, dy) != (0, 0)]
+    greet([me.partner, me.up, me.down] + [me.plane(*step) for step in across])
     sends = []
 
     def send(src, dst, ssem, rsem, device):
@@ -234,11 +257,14 @@
         for h in range(2):
             q = qacc[:, h * HD : (h + 1) * HD]
             q = q * lax.rsqrt(jnp.mean(q * q, axis=-1, keepdims=True) + EPS) * qgain[...]
-            qrows[h * TOK : (h + 1) * TOK, :] = q.astype(BF16)
+            qrows[h * TOK : (h + 1) * TOK, HD:] = q.astype(BF16)
 
     text_send(0, 0, 1)
     text_send(0, 1, 1)
     text_share(0)
+    for dx, dy in across:
+        k = dx * 4 + dy
+        send(metas.at[here], metas.at[here], ms.at[k], mr.at[k], me.plane(dx, dy))
 
     def order(n):
         return (z + 4 + jnp.where(n % 2 == 1, -((n + 1) // 2), n // 2)) % 8
@@ -295,7 +321,6 @@
                 rk[way, stage, rows, :] += acck[d, rows, :]
                 rv[way, stage, rows, :] = (rv[way, stage, rows, :].astype(F32) + accv[d, rows, :]).astype(BF16)
 
-    here = me.image(0, 0)
     here_rows = lambda start, n: pl.ds(pl.multiple_of(c * QUARTER + start, 16), n)
 
     def finish(u):
@@ -304,19 +329,13 @@
         key = rk[0, 3, rows, :] + rk[1, 3, rows, :] + acck[z, rows, :]
         val = rv[0, 3, rows, :].astype(F32) + rv[1, 3, rows, :].astype(F32) + accv[z, rows, :]
         key = key * lax.rsqrt(jnp.mean(key * key, axis=-1, keepdims=True) + EPS) * kgain[...]
-        if start + n == QUARTER:
-            row = start + lax.broadcasted_iota(jnp.int32, (n, HD), 0)
-            lane = lax.broadcasted_iota(jnp.int32, (n, HD), 1)
-            said = jnp.where(lane == 0, owner[0], jnp.where(lane == 1, pos[0] // 64, pos[0] % 64))
-            said = jnp.where(lane < 3, said, 0).astype(F32) * META
-            key = jnp.where(row >= META_ROW, said, key)
-        kv[here, here_rows(start, n), 0:HD] = key.astype(BF16)
-        kv[here, here_rows(start, n), HD:] = val.astype(BF16)
+        kv[here, here_rows(start, n), HD : 2 * HD] = key.astype(BF16)
+        kv[here, here_rows(start, n), 2 * HD : 3 * HD] = val.astype(BF16)
 
 
     def block(u, par, i, j, part=None):
         m = me.image(i, j) if par == 0 else me.image(j, i)
-        return kv.at[m, here_rows(*piece(u, par, part))]
+        return kv.at[m, here_rows(*piece(u, par, part)), pl.ds(HD, 2 * HD)]
 
     axes = lambda par: ("x", "y") if par == 0 else ("y", "x")
 
@@ -373,61 +392,65 @@
         second_arrived(u, par, i, 2)
         share(u, par, i, 2)
 
-    docs = jnp.broadcast_to(seg[...].astype(F32).reshape(1, TOK), (HD, TOK)).T[:, 0:1]
-    places = ((me.x * 4 + me.y % 2 * 2 + me.y // 2) * TOK + lax.broadcasted_iota(jnp.int32, (TOK, 1), 0)).astype(F32)
     total[...] = jnp.zeros_like(total)
-    mass[...] = jnp.zeros_like(mass)
-
-    def attend_image(u, m):
+
+    def hide():
+        for dx, dy in across:
+            ref = metas.at[me.image(dx, dy)]
+            k = (4 - dx) % 4 * 4 + (4 - dy) % 4
+            arrived(ref, ms.at[k], mr.at[k])
+        said = metas[0]
+        for m in range(1, IMAGES):
+            said += metas[m]
+        docs = jnp.broadcast_to(seg[...].astype(F32).reshape(1, TOK), (HD, TOK)).T
+        lane = lax.broadcasted_iota(jnp.int32, (TOK, HD), 1)
+        place = here * TOK + lax.broadcasted_iota(jnp.int32, (TOK, HD), 0)
+        sees = (docs == said[0:1, :]) & (place.astype(F32) >= said[1:2, :])
+        unseen = jnp.where(lane < IMAGES, jnp.where(sees, 0.0, HIDDEN), jnp.where(lane == IMAGES, HIDDEN, 0.0))
+        for h in range(4):
+            qrows[h * TOK : (h + 1) * TOK, 0:HD] = unseen.astype(BF16)
+
+    def attend_images(u, pair):
         start, n = SUBS[u][0], sum(SUBS[u][1:])
-        parts = [kv[m, q * QUARTER + start : q * QUARTER + start + n, :] for q in range(2)]
-        both = jnp.concatenate(parts, axis=0)
-        keys, values = both[:, :HD], both[:, HD:]
-        said = kv[m, QUARTER - 16 : QUARTER, 0:HD].astype(F32)[15:16, :] * (1.0 / META)
-        lane = lax.broadcasted_iota(jnp.int32, (1, HD), 1)
-        doc = jnp.sum(jnp.where(lane == 0, said, 0.0), axis=1, keepdims=True)
-        scale = jnp.where(lane == 1, 64.0, jnp.where(lane == 2, 1.0, 0.0))
-        mask = (docs == doc) & (places >= jnp.sum(said * scale, axis=1, keepdims=True))
-        for h in range(4):
-            at = slice(h * TOK, (h + 1) * TOK)
+        both = lambda lanes: jnp.concatenate(
+            [kv[m, q * QUARTER + start : q * QUARTER + start + n, lanes] for m in pair for q in range(2)], axis=0
+        )
+        keys, values = both(slice(0, 2 * HD)), both(slice(2 * HD, 4 * HD))
+
+        def heads(r, carry):
+            at = pl.ds(pl.multiple_of(r * 2 * TOK, 2 * TOK), 2 * TOK)
             rows = qrows[at, :]
-            weight = jnp.zeros((TOK, HD), F32)
-            term = jnp.zeros((TOK, HD), F32)
-            for k0 in range(0, 2 * n, 256):
-                width = min(256, 2 * n - k0)
+            for k0 in range(0, 4 * n, 256):
+                width = min(256, 4 * n - k0)
                 score = lax.dot_general(
                     rows, keys[k0 : k0 + width, :], (((1,), (1,)), ((), ())), preferred_element_type=F32
                 )
-                expo = jnp.exp2(score * (HD**-0.5 * 1.4426950408889634))
-                if start + n == QUARTER:
-                    lane = k0 + lax.broadcasted_iota(jnp.int32, expo.shape, 1)
-                    good = (lane < BODY - start) | ((lane >= n) & (lane < n + BODY - start + zpar))
-                    expo = jnp.where(good, expo, 0.0)
-                for lanes in range(0, width, HD):
-                    some = expo[:, lanes : min(lanes + HD, width)]
-                    if some.shape[1] < HD:
-                        some = jnp.concatenate([some, jnp.zeros((TOK, HD - some.shape[1]), F32)], axis=1)
-                    weight += some
-                term += jnp.dot(expo.astype(BF16), values[k0 : k0 + width, :], preferred_element_type=F32)
-            total[at, :] += jnp.where(mask, term, 0.0)
-            mass[at, :] += jnp.where(mask, weight, 0.0)
+                wexp[:, k0 : k0 + width] = jnp.exp2(score * (HD**-0.5 * 1.4426950408889634)).astype(BF16)
+            total[at, :] += jnp.dot(wexp[:, 0 : 4 * n], values, preferred_element_type=F32)
+            return carry
+
+        lax.fori_loop(0, 2, heads, 0)
 
     def attend(u, images):
         for dx, dy in images:
             for par, i, j in ((0, dx, dy), (1, dy, dx)):
                 start, n = piece(u, par)
-                ref = kv.at[me.image(dx, dy), pl.ds(pl.multiple_of((1 - c) * QUARTER + start, 16), n)]
+                rows = pl.ds(pl.multiple_of((1 - c) * QUARTER + start, 16), n)
+                ref = kv.at[me.image(dx, dy), rows, pl.ds(HD, 2 * HD)]
                 arrived(ref, cs.at[u, par, 4 * i + j], cr.at[u, par, 4 * i + j])
         codes = [4 * dx + dy for dx, dy in images]
 
         def one(n, carry):
-            code = codes[0]
-            for k in range(1, len(codes)):
-                code = jnp.where(n == k, codes[k], code)
-            attend_image(u, me.image(code // 4, code % 4))
+            chosen = []
+            for k in range(2):
+                code = codes[k]
+                for i in range(2, len(codes), 2):
+                    code = jnp.where(n == i // 2, codes[i + k], code)
+                chosen.append(me.image(code // 4, code % 4))
+            attend_images(u, chosen)
             return carry
 
-        lax.fori_loop(0, len(codes), one, 0)
+        lax.fori_loop(0, len(codes) // 2, one, 0)
 
     def ring_step(u, stage):
         ring_receive(u, stage)
@@ -442,10 +465,12 @@
 
     def queries_swap():
         text_compute()
-        send(qrows.at[own_rows], qrows.at[pair_rows], qs, qr, pair)
+        lanes = pl.ds(HD, HD)
+        send(qrows.at[own_rows, lanes], qrows.at[pair_rows, lanes], qs, qr, pair)
+        hide()
 
     def queries_arrived():
-        arrived(qrows.at[pair_rows], qs, qr)
+        arrived(qrows.at[pair_rows, pl.ds(HD, HD)], qs, qr)
 
     handlers = {
         "start": lambda u: ring_send(u, 0),
@@ -480,10 +505,9 @@
     for name, *args in ORDER:
         handlers[name](*args)
 
-    half[...] = total[pair_rows, :].astype(BF16)
+    half[...] = total[pair_rows, 0:HD].astype(BF16)
     send(half, theirs, ts.at[0], tr.at[0], pair)
-    weight = jnp.sum(mass[pair_rows, :], axis=1, keepdims=True)
-    mhalf[...] = jnp.broadcast_to(weight, (2 * TOK, HD)).T[0:8, :]
+    mhalf[...] = total[pair_rows, HD:].T[0:8, :]
     send(mhalf, mtheirs, ts.at[1], tr.at[1], pair)
     arrived(mtheirs, ts.at[1], tr.at[1])
     arrived(theirs, ts.at[0], tr.at[0])
@@ -491,8 +515,8 @@
 
     for h in range(2):
         rows = slice(h * TOK, (h + 1) * TOK)
-        weight = jnp.maximum(jnp.sum(mass[rows, :], axis=1, keepdims=True) + others[rows], 1.0)
-        att[:, h * HD : (h + 1) * HD] = ((total[rows, :] + theirs[rows, :].astype(F32)) / weight).astype(BF16)
+        weight = jnp.maximum(total[rows, HD:] + others[rows], 1.0)
+        att[:, h * HD : (h + 1) * HD] = ((total[rows, 0:HD] + theirs[rows, :].astype(F32)) / weight).astype(BF16)
 
     send(att, patt, es, er, me.partner)
 
@@ -578,10 +602,11 @@
             pltpu.VMEM((2, 4, QUARTER, HD), F32),
             pltpu.VMEM((2, 4, QUARTER, HD), BF16),
             pltpu.VMEM((QUARTER, HD), BF16),
-            pltpu.VMEM((IMAGES, HALF, 256), BF16),
-            pltpu.VMEM((4 * TOK, HD), BF16),
-            pltpu.VMEM((4 * TOK, HD), F32),
-            pltpu.VMEM((4 * TOK, HD), F32),
+            pltpu.VMEM((IMAGES, HALF, 4 * HD), BF16),
+            pltpu.VMEM((4 * TOK, 2 * HD), BF16),
+            pltpu.VMEM((2 * TOK, 1024), BF16),
+            pltpu.VMEM((4 * TOK, 2 * HD), F32),
+            pltpu.VMEM((IMAGES, 8, HD), F32),
             pltpu.VMEM((2 * TOK, HD), BF16),
             pltpu.VMEM((2 * TOK, HD), BF16),
             pltpu.VMEM((8, 2 * TOK), F32),
@@ -617,9 +642,11 @@
             dma,
             dma((2,)),
             dma((2,)),
+            dma((16,)),
+            dma((16,)),
         ],
         compiler_params=pltpu.CompilerParams(
-            collective_id=0, has_side_effects=True, vmem_limit_bytes=60 * 2**20
+            collective_id=0, has_side_effects=True, vmem_limit_bytes=56 * 2**20
         ),
         cost_estimate=pl.CostEstimate(flops=2 * 10**10, bytes_accessed=3 * 10**7, transcendentals=13 * 10**6),
     )(*args)

time: 141 us -> 134 us (0.950)
  Pallas kernels: 136 us -> 129 us
    pallas_call x1, Pallas kernels: 136 us -> 129 us  [fused(): pl.pallas_call(kernel, out_shape=jax.ShapeDtypeStruct((TOK, 512), BF16),...]
where the time goes in v5:
time: 134 us
  Pallas kernels  129 us (96%)
  local copies, waits for them, and re-layouts  2.95 us (2%)
  between operations  1.95 us (1%)
    pallas_call x1, Pallas kernels, fused(): pl.pallas_call(kernel, out_shape=jax.ShapeDtypeStruct((TOK, 512), BF16),...  129 us

profile of v5, /device:TPU:1, one launch (start us, length us, event | category | flops | bytes accessed | tf_op | source)
XLA Modules:
  0.0 134.1 jit_solution(7309867248755213566)
XLA Ops:
  1.9 1.3 slice_bitcast_fusion.tail
  3.2 129.2 %shard_map.118 = bf16[256,512]{1,0:T(8,128)(2,1)} custom-call(bf16[256,512]{1,0:T(8,128)(2,1)} %text.1, bf16[512]{0:T(512)(128)(2,1)} %gain.1, bf16[1,512]{1,0:T(2,128)(2,1)} %slice_bitcast_fusion.tail, bf16[8192,256]{1,0:T(8,128)(2,1)} %wq.1, bf16[512,1024]{1,0:T(8,128)(2,1)} %wkv.1, bf16[256,8192]{1,0:T(8,128)(2,1)} %wout.1, f32[1,128]{1,0:T(1,128)} %bitcast.4, ...), custom_call_target="tpu_custom_call" | custom-call | flops 20000000000 | bytes 30000000 | tf_op jit(solution)/shard_map/pallas_call | solution.py:586
  132.4 1.7 %copy.17 = bf16[256,512]{1,0:T(8,128)(2,1)} copy(bf16[256,512]{1,0:T(8,128)(2,1)} %shard_map.118) | data formatting | bytes 524288

commit v6 on v5

--- a/solution.py
+++ b/solution.py
@@ -17,89 +17,90 @@
 EPS = 1e-05
 HIDDEN = -30000.0
 
-SUBS = ((224, 48, 48, 48, 48), (0, 64, 48, 64, 48))
+SUBS = ((256, 48, 32, 48, 32), (0, 64, 64, 64, 64))
 
 EARLY = (('start', 0), ('start', 1))
 ORDER = (
     ('text', 1),
     ('ring', 0, 0),
-    ('text', 2),
     ('ring', 1, 0),
     ('ring', 0, 1),
-    ('text', 3),
+    ('text', 2),
     ('ring', 1, 1),
     ('ring', 0, 2),
-    ('text', 4),
-    ('textc',),
+    ('text', 3),
+    ('textp',),
     ('ring', 1, 2),
     ('ring', 0, 3),
-    ('q2',),
+    ('text', 4),
     ('PF', 0, 0, 3),
     ('PF', 0, 0, 1),
+    ('textc',),
+    ('PF', 0, 1, 3),
+    ('PF', 0, 1, 1),
     ('PS', 0, 0, 0, 3),
     ('PS', 0, 0, 0, 1),
     ('PS', 0, 1, 0, 3),
-    ('PF', 0, 1, 3),
-    ('PF', 0, 1, 1),
     ('PS', 0, 1, 0, 1),
-    ('ring', 1, 3),
     ('PG', 0, 0),
     ('PS', 0, 0, 3, 3),
     ('PS', 0, 0, 3, 1),
-    ('att', 0, (0, 0), (1, 0), (3, 0), (0, 1)),
+    ('ring', 1, 3),
     ('PS', 0, 0, 1, 3),
     ('PS', 0, 0, 1, 1),
     ('PS', 0, 1, 3, 3),
+    ('PS', 0, 1, 3, 1),
     ('PG', 0, 1),
-    ('PS', 0, 1, 3, 1),
+    ('PT', 0, 0, 0),
     ('PS', 0, 1, 1, 3),
     ('PS', 0, 1, 1, 1),
+    ('PS', 0, 0, 2, 1),
+    ('PS', 0, 0, 2, 3),
+    ('q2',),
+    ('att', 0, (0, 0), (1, 0), (3, 0), (0, 1)),
+    ('PF', 1, 0, 3),
+    ('PF', 1, 0, 1),
+    ('PT', 0, 0, 3),
+    ('PT', 0, 1, 0),
+    ('PF', 1, 1, 3),
+    ('PS', 1, 0, 0, 3),
     ('PS', 1, 0, 0, 1),
-    ('PT', 0, 0, 0),
-    ('PF', 1, 0, 1),
-    ('PS', 1, 0, 0, 3),
+    ('PT', 0, 1, 3),
     ('PF', 1, 1, 1),
-    ('PF', 1, 0, 3),
+    ('PT', 0, 0, 1),
+    ('PS', 0, 1, 2, 3),
+    ('PS', 1, 1, 0, 3),
+    ('PS', 0, 1, 2, 1),
+    ('PT', 0, 0, 2),
     ('PS', 1, 1, 0, 1),
-    ('PF', 1, 1, 3),
-    ('PS', 0, 0, 2, 1),
-    ('PS', 1, 1, 0, 3),
-    ('PT', 0, 1, 0),
     ('att', 0, (0, 3), (1, 1), (1, 3), (3, 1)),
-    ('PS', 0, 0, 2, 3),
-    ('PS', 0, 1, 2, 3),
-    ('PS', 0, 1, 2, 1),
+    ('PT', 0, 1, 1),
+    ('PS', 1, 0, 3, 3),
+    ('PS', 1, 0, 3, 1),
+    ('PS', 1, 1, 3, 3),
+    ('PS', 1, 0, 1, 3),
+    ('PS', 1, 1, 3, 1),
     ('PS', 1, 0, 1, 1),
-    ('PT', 0, 0, 3),
-    ('PT', 0, 0, 1),
-    ('PT', 0, 1, 3),
-    ('PT', 0, 1, 1),
-    ('PS', 1, 0, 1, 3),
+    ('PG', 1, 0),
+    ('att', 0, (3, 3), (2, 0), (0, 2), (2, 1)),
+    ('PT', 0, 1, 2),
+    ('PT', 1, 0, 0),
+    ('PT', 1, 1, 0),
     ('PS', 1, 1, 1, 3),
     ('PS', 1, 1, 1, 1),
-    ('PG', 1, 0),
-    ('PS', 1, 0, 3, 1),
-    ('PT', 1, 0, 0),
-    ('att', 0, (3, 3), (2, 0), (0, 2), (2, 1)),
     ('PG', 1, 1),
-    ('PS', 1, 0, 3, 3),
-    ('PS', 1, 1, 3, 3),
-    ('PS', 1, 1, 3, 1),
-    ('PT', 0, 0, 2),
-    ('PT', 0, 1, 2),
-    ('PT', 1, 1, 0),
-    ('PT', 1, 0, 1),
-    ('PS', 1, 0, 2, 1),
-    ('PT', 1, 1, 1),
-    ('att', 0, (2, 3), (1, 2), (3, 2), (2, 2)),
-    ('PS', 1, 0, 2, 3),
-    ('PS', 1, 1, 2, 3),
-    ('PS', 1, 1, 2, 1),
     ('PT', 1, 0, 3),
     ('att', 1, (0, 0), (1, 0), (3, 0), (0, 1)),
+    ('PT', 1, 0, 1),
+    ('PT', 1, 1, 3),
+    ('PT', 1, 1, 1),
+    ('PS', 1, 0, 2, 3),
+    ('PS', 1, 0, 2, 1),
+    ('PS', 1, 1, 2, 1),
+    ('att', 0, (2, 3), (1, 2), (3, 2), (2, 2)),
+    ('PS', 1, 1, 2, 3),
+    ('att', 1, (0, 3), (1, 1), (1, 3), (3, 1)),
     ('PT', 1, 0, 2),
-    ('PT', 1, 1, 3),
-    ('att', 1, (0, 3), (1, 1), (1, 3), (3, 1)),
     ('PT', 1, 1, 2),
     ('att', 1, (3, 3), (2, 0), (0, 2), (2, 1)),
     ('att', 1, (2, 3), (1, 2), (3, 2), (2, 2)),
@@ -180,18 +181,6 @@
     lane = lax.broadcasted_iota(jnp.int32, (8, HD), 1)
     said = jnp.where(row == 0, owner[0], jnp.where(row == 1, pos[0], 0))
     metas[here] = jnp.where(lane == here, said, 0).astype(F32)
-    row = lax.broadcasted_iota(jnp.int32, (QUARTER, HD), 0)
-    lane = lax.broadcasted_iota(jnp.int32, (QUARTER, HD), 1)
-    for q in range(2):
-        padding = (lane == IMAGES) & (row >= BODY + zpar * q)
-
-        def name_rows(m, carry):
-            kv[m, q * QUARTER : (q + 1) * QUARTER, 0:HD] = jnp.where((lane == m) | padding, 1.0, 0.0).astype(BF16)
-            kv[m, q * QUARTER : (q + 1) * QUARTER, 3 * HD :] = jnp.ones((QUARTER, HD), BF16)
-            return carry
-
-        lax.fori_loop(0, IMAGES, name_rows, 0)
-
     across = [(dx, dy) for dx in range(4) for dy in range(4) if (dx, dy) != (0, 0)]
     greet([me.partner, me.up, me.down] + [me.plane(*step) for step in across])
     sends = []
@@ -240,20 +229,31 @@
         if hop == 4:
             text_share(4)
 
-    def text_compute():
-        for k in range(8):
-            ref = nall.at[((z + k) % 8) * 2 + 1 - c]
-            arrived(ref, acs.at[k], acr.at[k])
+    def text_use(index):
+        w = wqv[pl.ds(pl.multiple_of(index * 512, 512), 512), :]
+        qacc[...] += jnp.dot(nall[index], w, preferred_element_type=F32)
+
+    def text_shared(k):
+        ref = nall.at[((z + k) % 8) * 2 + 1 - c]
+        arrived(ref, acs.at[k], acr.at[k])
+
+    def text_most():
+        for k in (0, 1, 7, 2, 6, 3, 5):
+            text_shared(k)
         for load in loads[3:7]:
             load.wait()
         qacc[...] = jnp.zeros_like(qacc)
 
-        def use(index, carry):
-            w = wqv[pl.ds(pl.multiple_of(index * 512, 512), 512), :]
-            qacc[...] += jnp.dot(nall[index], w, preferred_element_type=F32)
+        def use(n, carry):
+            text_use(((z + 5 + n // 2) % 8) * 2 + n % 2)
             return carry
 
-        lax.fori_loop(0, 16, use, 0)
+        lax.fori_loop(0, 14, use, 0)
+
+    def text_compute():
+        text_shared(4)
+        for k in range(2):
+            text_use(((z + 4) % 8) * 2 + k)
         for h in range(2):
             q = qacc[:, h * HD : (h + 1) * HD]
             q = q * lax.rsqrt(jnp.mean(q * q, axis=-1, keepdims=True) + EPS) * qgain[...]
@@ -265,6 +265,18 @@
     for dx, dy in across:
         k = dx * 4 + dy
         send(metas.at[here], metas.at[here], ms.at[k], mr.at[k], me.plane(dx, dy))
+
+    row = lax.broadcasted_iota(jnp.int32, (QUARTER, HD), 0)
+    lane = lax.broadcasted_iota(jnp.int32, (QUARTER, HD), 1)
+    for q in range(2):
+        padding = (lane == IMAGES) & (row >= BODY + zpar * q)
+
+        def name_rows(m, carry):
+            kv[m, q * QUARTER : (q + 1) * QUARTER, 0:HD] = jnp.where((lane == m) | padding, 1.0, 0.0).astype(BF16)
+            kv[m, q * QUARTER : (q + 1) * QUARTER, 3 * HD :] = jnp.ones((QUARTER, HD), BF16)
+            return carry
+
+        lax.fori_loop(0, IMAGES, name_rows, 0)
 
     def order(n):
         return (z + 4 + jnp.where(n % 2 == 1, -((n + 1) // 2), n // 2)) % 8
@@ -417,19 +429,14 @@
         )
         keys, values = both(slice(0, 2 * HD)), both(slice(2 * HD, 4 * HD))
 
-        def heads(r, carry):
-            at = pl.ds(pl.multiple_of(r * 2 * TOK, 2 * TOK), 2 * TOK)
-            rows = qrows[at, :]
-            for k0 in range(0, 4 * n, 256):
-                width = min(256, 4 * n - k0)
-                score = lax.dot_general(
-                    rows, keys[k0 : k0 + width, :], (((1,), (1,)), ((), ())), preferred_element_type=F32
-                )
-                wexp[:, k0 : k0 + width] = jnp.exp2(score * (HD**-0.5 * 1.4426950408889634)).astype(BF16)
-            total[at, :] += jnp.dot(wexp[:, 0 : 4 * n], values, preferred_element_type=F32)
-            return carry
-
-        lax.fori_loop(0, 2, heads, 0)
+        rows = qrows[...]
+        for k0 in range(0, 4 * n, 256):
+            width = min(256, 4 * n - k0)
+            score = lax.dot_general(
+                rows, keys[k0 : k0 + width, :], (((1,), (1,)), ((), ())), preferred_element_type=F32
+            )
+            wexp[:, k0 : k0 + width] = jnp.exp2(score * (HD**-0.5 * 1.4426950408889634)).astype(BF16)
+        total[...] += jnp.dot(wexp[:, 0 : 4 * n], values, preferred_element_type=F32)
 
     def attend(u, images):
         for dx, dy in images:
@@ -480,6 +487,7 @@
         "PS": spread_second_on,
         "PT": spread_end,
         "text": text_round,
+        "textp": text_most,
         "textc": queries_swap,
         "q2": queries_arrived,
         "att": lambda u, *images: attend(u, images),
@@ -604,7 +612,7 @@
             pltpu.VMEM((QUARTER, HD), BF16),
             pltpu.VMEM((IMAGES, HALF, 4 * HD), BF16),
             pltpu.VMEM((4 * TOK, 2 * HD), BF16),
-            pltpu.VMEM((2 * TOK, 1024), BF16),
+            pltpu.VMEM((4 * TOK, 4 * max(sum(sub[1:]) for sub in SUBS)), BF16),
             pltpu.VMEM((4 * TOK, 2 * HD), F32),
             pltpu.VMEM((IMAGES, 8, HD), F32),
             pltpu.VMEM((2 * TOK, HD), BF16),
@@ -646,7 +654,7 @@
             dma((16,)),
         ],
         compiler_params=pltpu.CompilerParams(
-            collective_id=0, has_side_effects=True, vmem_limit_bytes=56 * 2**20
+            collective_id=0, has_side_effects=True, vmem_limit_bytes=54 * 2**20
         ),
         cost_estimate=pl.CostEstimate(flops=2 * 10**10, bytes_accessed=3 * 10**7, transcendentals=13 * 10**6),
     )(*args)

time: 134 us -> 125 us (0.933)
  Pallas kernels: 129 us -> 120 us
    pallas_call x1, Pallas kernels: 129 us -> 120 us  [fused(): pl.pallas_call(kernel, out_shape=jax.ShapeDtypeStruct((TOK, 512), BF16),...]
where the time goes in v6:
time: 125 us
  Pallas kernels  120 us (96%)
  local copies, waits for them, and re-layouts  2.95 us (2%)
  between operations  1.95 us (2%)
    pallas_call x1, Pallas kernels, fused(): pl.pallas_call(kernel, out_shape=jax.ShapeDtypeStruct((TOK, 512), BF16),...  120 us

profile of v6, /device:TPU:1, one launch (start us, length us, event | category | flops | bytes accessed | tf_op | source)
XLA Modules:
  0.0 125.1 jit_solution(15849465478013177434)
XLA Ops:
  1.9 1.3 %slice_bitcast_fusion.tail = bf16[1,512]{1,0:T(2,128)(2,1)} fusion(bf16[1,1601,512]{2,1,0:T(8,128)(2,1)} %img.1), kind=kLoop, calls=%fused_computation | loop fusion | bytes 2048 | tf_op jit(solution)/shard_map/squeeze | solution.py:667
  3.2 120.2 %shard_map.118 = bf16[256,512]{1,0:T(8,128)(2,1)} custom-call(bf16[256,512]{1,0:T(8,128)(2,1)} %text.1, bf16[512]{0:T(512)(128)(2,1)} %gain.1, bf16[1,512]{1,0:T(2,128)(2,1)} %slice_bitcast_fusion.tail, bf16[8192,256]{1,0:T(8,128)(2,1)} %wq.1, bf16[512,1024]{1,0:T(8,128)(2,1)} %wkv.1, bf16[256,8192]{1,0:T(8,128)(2,1)} %wout.1, f32[1,128]{1,0:T(1,128)} %bitcast.4, ...), custom_call_target="tpu_custom_call" | custom-call | flops 20000000000 | bytes 30000000 | tf_op jit(solution)/shard_map/pallas_call | solution.py:594
  123.5 1.7 %copy.17 = bf16[256,512]{1,0:T(8,128)(2,1)} copy(bf16[256,512]{1,0:T(8,128)(2,1)} %shard_map.118) | data formatting | bytes 524288

commit v7 on v6

--- a/solution.py
+++ b/solution.py
@@ -24,8 +24,8 @@
     ('text', 1),
     ('ring', 0, 0),
     ('ring', 1, 0),
+    ('text', 2),
     ('ring', 0, 1),
-    ('text', 2),
     ('ring', 1, 1),
     ('ring', 0, 2),
     ('text', 3),
@@ -147,7 +147,7 @@
 def kernel(
     text, gain, tail, wq, wkv, wout, qgain, kgain, gate, owner, pos, seg, img,
     out,
-    nall, wqv, qacc, imgv, pimg, tailv, wkvv, pwkv, acck, accv, rk, rv, vfirst,
+    nall, wqv, qacc, imgv, pimg, tailv, wkvv, pwkv, acc, rkv, rk, rv, kv0, k3,
     kv, qrows, wexp, total, metas, half, theirs, mhalf, mtheirs, att, patt, wo, pwo, terms, got, sent,
     load_sem, ex_send, ex_recv, bs, br, ps, pr, cs, cr, as_, ar, acs, acr, ws, wr,
     wo_sem, es, er, ds, dr, qs, qr, ts, tr, ms, mr,
@@ -286,8 +286,7 @@
         cols = pl.ds(pl.multiple_of((d // 2) * 256, 256), 256)
         part = jnp.dot(imgv[rows, :], wkvv[:, cols], preferred_element_type=F32)
         part += jnp.dot(pimg[rows, :], pwkv[:, cols], preferred_element_type=F32)
-        acck[d] = part[:, :HD]
-        accv[d] = part[:, HD:]
+        acc[d] = part
 
     def project_next(n, carry):
         project(order(n))
@@ -309,37 +308,42 @@
     def ring_send(u, stage):
         for way in (0, 1):
             rows = ring_rows(u, way, stage)
+            device = (me.up, me.down)[way]
             if stage == 0:
-                d = (z + 4) % 8
-                vfirst[rows, :] = accv[d, rows, :].astype(BF16)
-                srck, srcv = acck.at[d, rows], vfirst.at[rows]
+                kv0[rows, :] = acc[(z + 4) % 8, rows, :].astype(BF16)
+            if stage < 3:
+                src = kv0.at[rows] if stage == 0 else rkv.at[way, stage - 1, rows]
+                send(src, rkv.at[way, stage, rows], bs.at[u, way, stage], br.at[u, way, stage], device)
             else:
-                srck, srcv = rk.at[way, stage - 1, rows], rv.at[way, stage - 1, rows]
-            device = (me.up, me.down)[way]
-            send(srck, rk.at[way, stage, rows], bs.at[u, way, stage, 0], br.at[u, way, stage, 0], device)
-            send(srcv, rv.at[way, stage, rows], bs.at[u, way, stage, 1], br.at[u, way, stage, 1], device)
+                send(k3.at[way, rows], rk.at[way, rows], bs.at[u, way, 3], br.at[u, way, 3], device)
+                send(rkv.at[way, 2, rows, pl.ds(HD, HD)], rv.at[way, rows], bs.at[u, way, 4], br.at[u, way, 4], device)
 
     def ring_receive(u, stage):
         for way in (0, 1):
             rows = ring_rows(u, way, stage)
+            if stage == 3:
+                arrived(rk.at[way, rows], bs.at[u, way, 3], br.at[u, way, 3])
+                arrived(rv.at[way, rows], bs.at[u, way, 4], br.at[u, way, 4])
+                continue
             d = (z + (3 - stage if way == 0 else 5 + stage)) % 8
             if stage == 0:
                 other = ring_rows(u, 1 - way, 0)
-                rk[way, 0, other, :] = acck[d, other, :]
-                rv[way, 0, other, :] = accv[d, other, :].astype(BF16)
-            arrived(rk.at[way, stage, rows], bs.at[u, way, stage, 0], br.at[u, way, stage, 0])
-            arrived(rv.at[way, stage, rows], bs.at[u, way, stage, 1], br.at[u, way, stage, 1])
-            if stage < 3:
-                rk[way, stage, rows, :] += acck[d, rows, :]
-                rv[way, stage, rows, :] = (rv[way, stage, rows, :].astype(F32) + accv[d, rows, :]).astype(BF16)
+                rkv[way, 0, other, :] = acc[d, other, :].astype(BF16)
+            arrived(rkv.at[way, stage, rows], bs.at[u, way, stage], br.at[u, way, stage])
+            part = rkv[way, stage, rows, :].astype(F32) + acc[d, rows, :]
+            if stage < 2:
+                rkv[way, stage, rows, :] = part.astype(BF16)
+            else:
+                k3[way, rows, :] = part[:, :HD]
+                rkv[way, 2, rows, HD:] = part[:, HD:].astype(BF16)
 
     here_rows = lambda start, n: pl.ds(pl.multiple_of(c * QUARTER + start, 16), n)
 
     def finish(u):
         start, n = SUBS[u][0], sum(SUBS[u][1:])
         rows = pl.ds(start, n)
-        key = rk[0, 3, rows, :] + rk[1, 3, rows, :] + acck[z, rows, :]
-        val = rv[0, 3, rows, :].astype(F32) + rv[1, 3, rows, :].astype(F32) + accv[z, rows, :]
+        key = rk[0, rows, :] + rk[1, rows, :] + acc[z, rows, 0:HD]
+        val = rv[0, rows, :].astype(F32) + rv[1, rows, :].astype(F32) + acc[z, rows, HD:]
         key = key * lax.rsqrt(jnp.mean(key * key, axis=-1, keepdims=True) + EPS) * kgain[...]
         kv[here, here_rows(start, n), HD : 2 * HD] = key.astype(BF16)
         kv[here, here_rows(start, n), 2 * HD : 3 * HD] = val.astype(BF16)
@@ -605,11 +609,12 @@
             pltpu.VMEM((16, 512), BF16),
             pltpu.VMEM((512, 1024), BF16),
             pltpu.VMEM((512, 1024), BF16),
-            pltpu.VMEM((8, QUARTER, HD), F32),
-            pltpu.VMEM((8, QUARTER, HD), F32),
-            pltpu.VMEM((2, 4, QUARTER, HD), F32),
-            pltpu.VMEM((2, 4, QUARTER, HD), BF16),
-            pltpu.VMEM((QUARTER, HD), BF16),
+            pltpu.VMEM((8, QUARTER, 2 * HD), F32),
+            pltpu.VMEM((2, 3, QUARTER, 2 * HD), BF16),
+            pltpu.VMEM((2, QUARTER, HD), F32),
+            pltpu.VMEM((2, QUARTER, HD), BF16),
+            pltpu.VMEM((QUARTER, 2 * HD), BF16),
+            pltpu.VMEM((2, QUARTER, HD), F32),
             pltpu.VMEM((IMAGES, HALF, 4 * HD), BF16),
             pltpu.VMEM((4 * TOK, 2 * HD), BF16),
             pltpu.VMEM((4 * TOK, 4 * max(sum(sub[1:]) for sub in SUBS)), BF16),
@@ -629,8 +634,8 @@
             dma((7,)),
             dma((4,)),
             dma((4,)),
-            dma((n, 2, 4, 2)),
-            dma((n, 2, 4, 2)),
+            dma((n, 2, 5)),
+            dma((n, 2, 5)),
             dma((n, 2, 16)),
             dma((n, 2, 16)),
             dma((n, 2, 16)),
@@ -654,7 +659,7 @@
             dma((16,)),
         ],
         compiler_params=pltpu.CompilerParams(
-            collective_id=0, has_side_effects=True, vmem_limit_bytes=54 * 2**20
+            collective_id=0, has_side_effects=True, vmem_limit_bytes=52 * 2**20
         ),
         cost_estimate=pl.CostEstimate(flops=2 * 10**10, bytes_accessed=3 * 10**7, transcendentals=13 * 10**6),
     )(*args)

time: 125 us -> 123 us (0.984)
  Pallas kernels: 120 us -> 115 us
  local copies, waits for them, and re-layouts: 2.95 us -> 6.25 us
    pallas_call x1, Pallas kernels: 120 us -> 115 us  [fused(): pl.pallas_call(kernel, out_shape=jax.ShapeDtypeStruct((TOK, 512), BF16),...]
    unnamed x1 -> x13, local copies, waits for them, and re-layouts: 1.67 us -> 5.55 us
where the time goes in v7:
time: 123 us
  Pallas kernels  115 us (93%)
  local copies, waits for them, and re-layouts  6.25 us (5%)
  between operations  1.96 us (2%)
    pallas_call x1, Pallas kernels, fused(): pl.pallas_call(kernel, out_shape=jax.ShapeDtypeStruct((TOK, 512), BF16),...  115 us
    unnamed x13, local copies, waits for them, and re-layouts  5.55 us

profile of v7, /device:TPU:1, one launch (start us, length us, event | category | flops | bytes accessed | tf_op | source)
XLA Modules:
  0.0 122.8 jit_solution(6048611422627424664)
XLA Ops:
  1.9 0.7 slice_bitcast_fusion.tail
  2.6 0.0 copy-start
  2.6 1.2 copy-done
  3.9 0.0 copy-start.1
  3.9 0.9 copy-done.1
  4.8 0.0 copy-start.2
  4.8 0.7 copy-done.2
  5.5 0.0 copy-start.3
  5.5 0.7 copy-done.3
  6.2 0.0 copy-start.4
  6.2 0.7 copy-done.4
  6.8 0.0 copy-start.5
  6.8 0.7 copy-done.5
  7.5 114.6 %shard_map.118 = bf16[256,512]{1,0:T(8,128)(2,1)S(1)} custom-call(bf16[256,512]{1,0:T(8,128)(2,1)S(1)} %copy-done.1, bf16[512]{0:T(512)(128)(2,1)S(1)} %copy-done.2, bf16[1,512]{1,0:T(2,128)(2,1)S(1)} %slice_bitcast_fusion.tail, bf16[8192,256]{1,0:T(8,128)(2,1)} %wq.1, bf16[512,1024]{1,0:T(8,128)(2,1)S(1)} %copy-done, bf16[256,8192]{1,0:T(8,128)(2,1)} %wout.1, ...), custom_call_target="tpu_custom_call" | custom-call | flops 20000000000 | bytes 30000000 | tf_op jit(solution)/shard_map/pallas_call | solution.py:598
  122.1 0.7 copy.17
Async XLA Ops:
  2.6 1.2 copy-start
  3.9 0.9 copy-start.1
  4.8 0.7 copy-start.2
  5.5 0.7 copy-start.3
  6.2 0.7 copy-start.4
  6.8 0.7 copy-start.5

commit v8 on v6

--- a/solution.py
+++ b/solution.py
@@ -17,93 +17,131 @@
 EPS = 1e-05
 HIDDEN = -30000.0
 
-SUBS = ((256, 48, 32, 48, 32), (0, 64, 64, 64, 64))
+SUBS = ((288, 32, 32, 32, 32), (0, 48, 32, 48, 32), (160, 32, 32, 32, 32))
 
 EARLY = (('start', 0), ('start', 1))
 ORDER = (
     ('text', 1),
     ('ring', 0, 0),
     ('ring', 1, 0),
+    ('text', 2),
     ('ring', 0, 1),
-    ('text', 2),
+    ('start', 2),
     ('ring', 1, 1),
     ('ring', 0, 2),
+    ('ring', 2, 0),
     ('text', 3),
     ('textp',),
+    ('ring', 0, 3),
     ('ring', 1, 2),
-    ('ring', 0, 3),
-    ('text', 4),
+    ('ring', 2, 1),
     ('PF', 0, 0, 3),
     ('PF', 0, 0, 1),
-    ('textc',),
-    ('PF', 0, 1, 3),
-    ('PF', 0, 1, 1),
     ('PS', 0, 0, 0, 3),
     ('PS', 0, 0, 0, 1),
     ('PS', 0, 1, 0, 3),
+    ('PF', 0, 1, 3),
+    ('PF', 0, 1, 1),
     ('PS', 0, 1, 0, 1),
-    ('PG', 0, 0),
+    ('text', 4),
+    ('textc',),
     ('PS', 0, 0, 3, 3),
     ('PS', 0, 0, 3, 1),
     ('ring', 1, 3),
+    ('PT', 0, 1, 0),
     ('PS', 0, 0, 1, 3),
     ('PS', 0, 0, 1, 1),
+    ('PS', 0, 1, 3, 1),
+    ('PG', 0, 0),
     ('PS', 0, 1, 3, 3),
-    ('PS', 0, 1, 3, 1),
+    ('PT', 0, 0, 0),
+    ('PS', 0, 1, 1, 1),
     ('PG', 0, 1),
-    ('PT', 0, 0, 0),
     ('PS', 0, 1, 1, 3),
-    ('PS', 0, 1, 1, 1),
-    ('PS', 0, 0, 2, 1),
-    ('PS', 0, 0, 2, 3),
+    ('ring', 2, 2),
+    ('PT', 0, 0, 3),
+    ('PF', 1, 0, 3),
+    ('PF', 1, 0, 1),
+    ('PS', 1, 0, 0, 3),
+    ('PS', 1, 0, 0, 1),
+    ('PS', 1, 1, 0, 3),
+    ('PF', 1, 1, 3),
+    ('PS', 1, 1, 0, 1),
     ('q2',),
     ('att', 0, (0, 0), (1, 0), (3, 0), (0, 1)),
-    ('PF', 1, 0, 3),
-    ('PF', 1, 0, 1),
-    ('PT', 0, 0, 3),
-    ('PT', 0, 1, 0),
-    ('PF', 1, 1, 3),
-    ('PS', 1, 0, 0, 3),
-    ('PS', 1, 0, 0, 1),
+    ('PT', 0, 0, 1),
     ('PT', 0, 1, 3),
+    ('PT', 0, 1, 1),
     ('PF', 1, 1, 1),
-    ('PT', 0, 0, 1),
+    ('PS', 0, 0, 2, 3),
+    ('PS', 0, 0, 2, 1),
+    ('ring', 2, 3),
     ('PS', 0, 1, 2, 3),
-    ('PS', 1, 1, 0, 3),
     ('PS', 0, 1, 2, 1),
-    ('PT', 0, 0, 2),
-    ('PS', 1, 1, 0, 1),
-    ('att', 0, (0, 3), (1, 1), (1, 3), (3, 1)),
-    ('PT', 0, 1, 1),
     ('PS', 1, 0, 3, 3),
     ('PS', 1, 0, 3, 1),
-    ('PS', 1, 1, 3, 3),
-    ('PS', 1, 0, 1, 3),
-    ('PS', 1, 1, 3, 1),
-    ('PS', 1, 0, 1, 1),
     ('PG', 1, 0),
-    ('att', 0, (3, 3), (2, 0), (0, 2), (2, 1)),
-    ('PT', 0, 1, 2),
+    ('att', 0, (0, 3), (1, 1), (1, 3), (3, 1)),
     ('PT', 1, 0, 0),
     ('PT', 1, 1, 0),
+    ('PS', 1, 0, 1, 3),
+    ('PS', 1, 0, 1, 1),
+    ('PS', 1, 1, 3, 3),
+    ('PS', 1, 1, 3, 1),
+    ('PG', 1, 1),
+    ('att', 0, (3, 3), (2, 0), (0, 2), (2, 1)),
+    ('PT', 0, 0, 2),
+    ('PF', 2, 0, 3),
+    ('PF', 2, 0, 1),
+    ('PF', 2, 1, 3),
+    ('PF', 2, 1, 1),
+    ('PS', 1, 0, 2, 3),
     ('PS', 1, 1, 1, 3),
     ('PS', 1, 1, 1, 1),
-    ('PG', 1, 1),
+    ('PS', 2, 0, 0, 3),
+    ('PS', 2, 0, 0, 1),
+    ('PT', 0, 1, 2),
+    ('PS', 2, 1, 0, 3),
+    ('PS', 2, 1, 0, 1),
+    ('att', 1, (0, 0), (1, 0), (3, 0), (0, 1)),
     ('PT', 1, 0, 3),
-    ('att', 1, (0, 0), (1, 0), (3, 0), (0, 1)),
     ('PT', 1, 0, 1),
     ('PT', 1, 1, 3),
+    ('PS', 1, 0, 2, 1),
+    ('PS', 1, 1, 2, 3),
+    ('PS', 1, 1, 2, 1),
+    ('PS', 2, 0, 3, 3),
+    ('PS', 2, 0, 3, 1),
+    ('PG', 2, 0),
+    ('att', 0, (2, 3), (1, 2), (3, 2), (2, 2)),
+    ('PT', 2, 0, 0),
+    ('PS', 2, 0, 1, 3),
+    ('PS', 2, 0, 1, 1),
     ('PT', 1, 1, 1),
-    ('PS', 1, 0, 2, 3),
-    ('PS', 1, 0, 2, 1),
-    ('PS', 1, 1, 2, 1),
-    ('att', 0, (2, 3), (1, 2), (3, 2), (2, 2)),
-    ('PS', 1, 1, 2, 3),
+    ('PS', 2, 1, 3, 3),
+    ('PS', 2, 1, 3, 1),
+    ('PS', 2, 1, 1, 3),
+    ('PS', 2, 1, 1, 1),
+    ('PG', 2, 1),
     ('att', 1, (0, 3), (1, 1), (1, 3), (3, 1)),
     ('PT', 1, 0, 2),
     ('PT', 1, 1, 2),
+    ('PT', 2, 0, 3),
+    ('PT', 2, 1, 0),
+    ('PS', 2, 0, 2, 3),
     ('att', 1, (3, 3), (2, 0), (0, 2), (2, 1)),
+    ('PT', 2, 0, 1),
+    ('PT', 2, 1, 3),
+    ('PT', 2, 1, 1),
+    ('PS', 2, 0, 2, 1),
+    ('PS', 2, 1, 2, 3),
+    ('PS', 2, 1, 2, 1),
     ('att', 1, (2, 3), (1, 2), (3, 2), (2, 2)),
+    ('att', 2, (0, 0), (1, 0), (3, 0), (0, 1)),
+    ('PT', 2, 0, 2),
+    ('PT', 2, 1, 2),
+    ('att', 2, (0, 3), (1, 1), (1, 3), (3, 1)),
+    ('fin', 2, (3, 3), (2, 0), (0, 2), (2, 1), (2, 3), (1, 2), (3, 2), (2, 2)),
 )
 
 
@@ -422,29 +460,31 @@
         for h in range(4):
             qrows[h * TOK : (h + 1) * TOK, 0:HD] = unseen.astype(BF16)
 
-    def attend_images(u, pair):
+    def attend_images(u, pair, at=slice(0, 4 * TOK)):
         start, n = SUBS[u][0], sum(SUBS[u][1:])
         both = lambda lanes: jnp.concatenate(
             [kv[m, q * QUARTER + start : q * QUARTER + start + n, lanes] for m in pair for q in range(2)], axis=0
         )
         keys, values = both(slice(0, 2 * HD)), both(slice(2 * HD, 4 * HD))
 
-        rows = qrows[...]
+        rows = qrows[at, :]
         for k0 in range(0, 4 * n, 256):
             width = min(256, 4 * n - k0)
             score = lax.dot_general(
                 rows, keys[k0 : k0 + width, :], (((1,), (1,)), ((), ())), preferred_element_type=F32
             )
-            wexp[:, k0 : k0 + width] = jnp.exp2(score * (HD**-0.5 * 1.4426950408889634)).astype(BF16)
-        total[...] += jnp.dot(wexp[:, 0 : 4 * n], values, preferred_element_type=F32)
-
-    def attend(u, images):
+            wexp[at, k0 : k0 + width] = jnp.exp2(score * (HD**-0.5 * 1.4426950408889634)).astype(BF16)
+        total[at, :] += jnp.dot(wexp[at, 0 : 4 * n], values, preferred_element_type=F32)
+
+    def blocks_arrived(u, images):
         for dx, dy in images:
             for par, i, j in ((0, dx, dy), (1, dy, dx)):
                 start, n = piece(u, par)
                 rows = pl.ds(pl.multiple_of((1 - c) * QUARTER + start, 16), n)
                 ref = kv.at[me.image(dx, dy), rows, pl.ds(HD, 2 * HD)]
                 arrived(ref, cs.at[u, par, 4 * i + j], cr.at[u, par, 4 * i + j])
+
+    def attend(u, images, at=slice(0, 4 * TOK)):
         codes = [4 * dx + dy for dx, dy in images]
 
         def one(n, carry):
@@ -454,10 +494,23 @@
                 for i in range(2, len(codes), 2):
                     code = jnp.where(n == i // 2, codes[i + k], code)
                 chosen.append(me.image(code // 4, code % 4))
-            attend_images(u, chosen)
+            attend_images(u, chosen, at)
             return carry
 
         lax.fori_loop(0, len(codes) // 2, one, 0)
+
+    def attend_both(u, *images):
+        blocks_arrived(u, images)
+        attend(u, images)
+
+    def attend_last(u, *images):
+        blocks_arrived(u, images)
+        attend(u, images, slice(2 * TOK, 4 * TOK))
+        half[...] = total[pair_rows, 0:HD].astype(BF16)
+        send(half, theirs, ts.at[0], tr.at[0], pair)
+        mhalf[...] = total[pair_rows, HD:].T[0:8, :]
+        send(mhalf, mtheirs, ts.at[1], tr.at[1], pair)
+        attend(u, images, slice(0, 2 * TOK))
 
     def ring_step(u, stage):
         ring_receive(u, stage)
@@ -490,7 +543,8 @@
         "textp": text_most,
         "textc": queries_swap,
         "q2": queries_arrived,
-        "att": lambda u, *images: attend(u, images),
+        "att": attend_both,
+        "fin": attend_last,
     }
 
     for load in loads[:3]:
@@ -513,10 +567,6 @@
     for name, *args in ORDER:
         handlers[name](*args)
 
-    half[...] = total[pair_rows, 0:HD].astype(BF16)
-    send(half, theirs, ts.at[0], tr.at[0], pair)
-    mhalf[...] = total[pair_rows, HD:].T[0:8, :]
-    send(mhalf, mtheirs, ts.at[1], tr.at[1], pair)
     arrived(mtheirs, ts.at[1], tr.at[1])
     arrived(theirs, ts.at[0], tr.at[0])
     others = jnp.broadcast_to(mtheirs[0:1, :], (HD, 2 * TOK)).T
@@ -654,7 +704,7 @@
             dma((16,)),
         ],
         compiler_params=pltpu.CompilerParams(
-            collective_id=0, has_side_effects=True, vmem_limit_bytes=54 * 2**20
+            collective_id=0, has_side_effects=True, vmem_limit_bytes=52 * 2**20
         ),
         cost_estimate=pl.CostEstimate(flops=2 * 10**10, bytes_accessed=3 * 10**7, transcendentals=13 * 10**6),
     )(*args)

time: 125 us -> 127 us (1.016)
  local copies, waits for them, and re-layouts: 2.95 us -> 6.25 us
    unnamed x1 -> x13, local copies, waits for them, and re-layouts: 1.67 us -> 5.55 us
    pallas_call x1, Pallas kernels: 120 us -> 119 us  [fused(): pl.pallas_call(kernel, out_shape=jax.ShapeDtypeStruct((TOK, 512), BF16),...]
where the time goes in v8:
time: 127 us
  Pallas kernels  119 us (94%)
  local copies, waits for them, and re-layouts  6.25 us (5%)
  between operations  1.96 us (2%)
    pallas_call x1, Pallas kernels, fused(): pl.pallas_call(kernel, out_shape=jax.ShapeDtypeStruct((TOK, 512), BF16),...  119 us
    unnamed x13, local copies, waits for them, and re-layouts  5.55 us

profile of v8, /device:TPU:1, one launch (start us, length us, event | category | flops | bytes accessed | tf_op | source)
XLA Modules:
  0.0 127.0 jit_solution(6701074743435305275)
XLA Ops:
  1.9 0.7 slice_bitcast_fusion.tail
  2.6 0.0 copy-start
  2.6 1.2 copy-done
  3.9 0.0 copy-start.1
  3.9 0.9 copy-done.1
  4.8 0.0 copy-start.2
  4.8 0.7 copy-done.2
  5.5 0.0 copy-start.3
  5.5 0.7 copy-done.3
  6.2 0.0 copy-start.4
  6.2 0.7 copy-done.4
  6.8 0.0 copy-start.5
  6.8 0.7 copy-done.5
  7.5 118.8 %shard_map.118 = bf16[256,512]{1,0:T(8,128)(2,1)S(1)} custom-call(bf16[256,512]{1,0:T(8,128)(2,1)S(1)} %copy-done.1, bf16[512]{0:T(512)(128)(2,1)S(1)} %copy-done.2, bf16[1,512]{1,0:T(2,128)(2,1)S(1)} %slice_bitcast_fusion.tail, bf16[8192,256]{1,0:T(8,128)(2,1)} %wq.1, bf16[512,1024]{1,0:T(8,128)(2,1)S(1)} %copy-done, bf16[256,8192]{1,0:T(8,128)(2,1)} %wout.1, ...), custom_call_target="tpu_custom_call" | custom-call | flops 20000000000 | bytes 30000000 | tf_op jit(solution)/shard_map/pallas_call | solution.py:644
  126.3 0.7 copy.17
Async XLA Ops:
  2.6 1.2 copy-start
  3.9 0.9 copy-start.1
  4.8 0.7 copy-start.2
  5.5 0.7 copy-start.3
  6.2 0.7 copy-start.4
  6.8 0.7 copy-start.5

commit v9 on v6

--- a/solution.py
+++ b/solution.py
@@ -102,8 +102,7 @@
     ('att', 1, (0, 3), (1, 1), (1, 3), (3, 1)),
     ('PT', 1, 0, 2),
     ('PT', 1, 1, 2),
-    ('att', 1, (3, 3), (2, 0), (0, 2), (2, 1)),
-    ('att', 1, (2, 3), (1, 2), (3, 2), (2, 2)),
+    ('fin', 1, (3, 3), (2, 0), (0, 2), (2, 1), (2, 3), (1, 2), (3, 2), (2, 2)),
 )
 
 
@@ -422,29 +421,31 @@
         for h in range(4):
             qrows[h * TOK : (h + 1) * TOK, 0:HD] = unseen.astype(BF16)
 
-    def attend_images(u, pair):
+    def attend_images(u, pair, at=slice(0, 4 * TOK)):
         start, n = SUBS[u][0], sum(SUBS[u][1:])
         both = lambda lanes: jnp.concatenate(
             [kv[m, q * QUARTER + start : q * QUARTER + start + n, lanes] for m in pair for q in range(2)], axis=0
         )
         keys, values = both(slice(0, 2 * HD)), both(slice(2 * HD, 4 * HD))
 
-        rows = qrows[...]
+        rows = qrows[at, :]
         for k0 in range(0, 4 * n, 256):
             width = min(256, 4 * n - k0)
             score = lax.dot_general(
                 rows, keys[k0 : k0 + width, :], (((1,), (1,)), ((), ())), preferred_element_type=F32
             )
-            wexp[:, k0 : k0 + width] = jnp.exp2(score * (HD**-0.5 * 1.4426950408889634)).astype(BF16)
-        total[...] += jnp.dot(wexp[:, 0 : 4 * n], values, preferred_element_type=F32)
-
-    def attend(u, images):
+            wexp[at, k0 : k0 + width] = jnp.exp2(score * (HD**-0.5 * 1.4426950408889634)).astype(BF16)
+        total[at, :] += jnp.dot(wexp[at, 0 : 4 * n], values, preferred_element_type=F32)
+
+    def blocks_arrived(u, images):
         for dx, dy in images:
             for par, i, j in ((0, dx, dy), (1, dy, dx)):
                 start, n = piece(u, par)
                 rows = pl.ds(pl.multiple_of((1 - c) * QUARTER + start, 16), n)
                 ref = kv.at[me.image(dx, dy), rows, pl.ds(HD, 2 * HD)]
                 arrived(ref, cs.at[u, par, 4 * i + j], cr.at[u, par, 4 * i + j])
+
+    def attend(u, images, at=slice(0, 4 * TOK)):
         codes = [4 * dx + dy for dx, dy in images]
 
         def one(n, carry):
@@ -454,10 +455,23 @@
                 for i in range(2, len(codes), 2):
                     code = jnp.where(n == i // 2, codes[i + k], code)
                 chosen.append(me.image(code // 4, code % 4))
-            attend_images(u, chosen)
+            attend_images(u, chosen, at)
             return carry
 
         lax.fori_loop(0, len(codes) // 2, one, 0)
+
+    def attend_both(u, *images):
+        blocks_arrived(u, images)
+        attend(u, images)
+
+    def attend_last(u, *images):
+        blocks_arrived(u, images)
+        attend(u, images, slice(2 * TOK, 4 * TOK))
+        half[...] = total[pair_rows, 0:HD].astype(BF16)
+        send(half, theirs, ts.at[0], tr.at[0], pair)
+        mhalf[...] = total[pair_rows, HD:].T[0:8, :]
+        send(mhalf, mtheirs, ts.at[1], tr.at[1], pair)
+        attend(u, images, slice(0, 2 * TOK))
 
     def ring_step(u, stage):
         ring_receive(u, stage)
@@ -490,7 +504,8 @@
         "textp": text_most,
         "textc": queries_swap,
         "q2": queries_arrived,
-        "att": lambda u, *images: attend(u, images),
+        "att": attend_both,
+        "fin": attend_last,
     }
 
     for load in loads[:3]:
@@ -513,10 +528,6 @@
     for name, *args in ORDER:
         handlers[name](*args)
 
-    half[...] = total[pair_rows, 0:HD].astype(BF16)
-    send(half, theirs, ts.at[0], tr.at[0], pair)
-    mhalf[...] = total[pair_rows, HD:].T[0:8, :]
-    send(mhalf, mtheirs, ts.at[1], tr.at[1], pair)
     arrived(mtheirs, ts.at[1], tr.at[1])
     arrived(theirs, ts.at[0], tr.at[0])
     others = jnp.broadcast_to(mtheirs[0:1, :], (HD, 2 * TOK)).T
@@ -654,7 +665,7 @@
             dma((16,)),
         ],
         compiler_params=pltpu.CompilerParams(
-            collective_id=0, has_side_effects=True, vmem_limit_bytes=54 * 2**20
+            collective_id=0, has_side_effects=True, vmem_limit_bytes=52 * 2**20
         ),
         cost_estimate=pl.CostEstimate(flops=2 * 10**10, bytes_accessed=3 * 10**7, transcendentals=13 * 10**6),
     )(*args)

time: 125 us -> 126 us (level); the launches traced: 125 us -> 124 us
  Pallas kernels: 120 us -> 116 us
  local copies, waits for them, and re-layouts: 2.95 us -> 6.25 us
    pallas_call x1, Pallas kernels: 120 us -> 116 us  [fused(): pl.pallas_call(kernel, out_shape=jax.ShapeDtypeStruct((TOK, 512), BF16),...]
    unnamed x1 -> x13, local copies, waits for them, and re-layouts: 1.67 us -> 5.55 us
where the time goes in v9:
time: 126 us; the launch traced here: 124 us
  Pallas kernels  116 us (92%)
  local copies, waits for them, and re-layouts  6.25 us (5%)
  between operations  1.96 us (2%)
    pallas_call x1, Pallas kernels, fused(): pl.pallas_call(kernel, out_shape=jax.ShapeDtypeStruct((TOK, 512), BF16),...  116 us
    unnamed x13, local copies, waits for them, and re-layouts  5.55 us

profile of v9, /device:TPU:1, one launch (start us, length us, event | category | flops | bytes accessed | tf_op | source)
XLA Modules:
  0.0 124.1 jit_solution(5528470124383750637)
XLA Ops:
  1.9 0.7 slice_bitcast_fusion.tail
  2.6 0.0 copy-start
  2.6 1.2 copy-done
  3.9 0.0 copy-start.1
  3.9 0.9 copy-done.1
  4.8 0.0 copy-start.2
  4.8 0.7 copy-done.2
  5.5 0.0 copy-start.3
  5.5 0.7 copy-done.3
  6.2 0.0 copy-start.4
  6.2 0.7 copy-done.4
  6.8 0.0 copy-start.5
  6.8 0.7 copy-done.5
  7.5 115.9 %shard_map.118 = bf16[256,512]{1,0:T(8,128)(2,1)S(1)} custom-call(bf16[256,512]{1,0:T(8,128)(2,1)S(1)} %copy-done.1, bf16[512]{0:T(512)(128)(2,1)S(1)} %copy-done.2, bf16[1,512]{1,0:T(2,128)(2,1)S(1)} %slice_bitcast_fusion.tail, bf16[8192,256]{1,0:T(8,128)(2,1)} %wq.1, bf16[512,1024]{1,0:T(8,128)(2,1)S(1)} %copy-done, bf16[256,8192]{1,0:T(8,128)(2,1)} %wout.1, ...), custom_call_target="tpu_custom_call" | custom-call | flops 20000000000 | bytes 30000000 | tf_op jit(solution)/shard_map/pallas_call | solution.py:605
  123.4 0.7 copy.17
Async XLA Ops:
  2.6 1.2 copy-start
  3.9 0.9 copy-start.1
  4.8 0.7 copy-start.2
  5.5 0.7 copy-start.3
  6.2 0.7 copy-start.4
  6.8 0.7 copy-start.5
